TPU v7x, 256 devices: a whole 4x4x8 slice. The times are simulated.
256 devices in a mesh: rep: 8 (over y, core), edge: 32 (over z, x).
Axes of the slice: x: 4, y: 4, z: 8, core: 2. Of those that a mesh axis runs over, the one named last changes fastest.
Arguments:
- node_feats: bfloat16 [8, 8192, 128], P('rep', 'edge'), may hold values from -6 to 6
- edge_attr: bfloat16 [8, 65536, 128], P('rep', 'edge'), may hold values from -6 to 6
- edge_src: int32 [8, 65536], P('rep', 'edge'), may hold values from 0 to 8191, as said below
- edge_dst: int32 [8, 65536], P('rep', 'edge'), may hold values from 0 to 8191, as said below
- species: int32 [8, 8192], P('rep'), may hold values from 0 to 2
- orbital_mask: int32 [3, 27], replicated, may hold values 0 or 1
- tile_owner: int32 [8, 65536, 1], P('rep', 'edge'), may hold values from 0 to 31; in each aligned block of 2048 rows (0 to 2047, 2048 to 4095, ..., all dimensions but the last counted through in order) at most 96 rows name the same one
- target_send: bfloat16 [8, 23328, 3072], P('rep', 'edge'), may hold values from -6 to 6
- w_dst: bfloat16 [128, 128], replicated, may hold values from -0.5 to 0.5
- w_src: bfloat16 [128, 128], replicated, may hold values from -0.5 to 0.5
- w_attr: bfloat16 [128, 128], replicated, may hold values from -0.5 to 0.5
- w_mix: bfloat16 [128, 128], replicated, may hold values from -0.5 to 0.5
- w_left: bfloat16 [729, 128], replicated, may hold values from -0.5 to 0.5
- w_right: bfloat16 [729, 128], replicated, may hold values from -0.5 to 0.5
- cg_basis: bfloat16 [729, 729], replicated, may hold values from -0.21875 to 0.21875
Outputs:
- grad_dst: float32 [128, 128], replicated
- grad_src: float32 [128, 128], replicated
- grad_attr: float32 [128, 128], replicated
- grad_mix: float32 [128, 128], replicated
- grad_left: float32 [729, 128], replicated
- grad_right: float32 [729, 128], replicated
- edge_error: float32 [8, 65536], P('rep', 'edge')
Inputs may be any that keep to these rules, and one draw needn't show every extreme that they name: `edge_src`: device q of edge holds the edges q * 2048 to (q + 1) * 2048 - 1 and the atoms q * 256 to (q + 1) * 256 - 1 of each structure. An edge's source atom lies in the atoms of its device or of the two devices beside it; on every device both ends of that range occur. `edge_dst`: an edge's target atom lies in the atoms of its own device; on every device both ends of that range occur. `tile_owner`: among the 2048 edges of one device, at most 96 name the same holder.
All inputs are finite; a program needn't handle non-finite values.
Results may differ from a plain program's by a relative error of at most 0.0034.
The roundings to bfloat16 on the way count: a program that leaves them out, or rounds other values in their place, can miss the bound.
Values may be sent and summed in bfloat16 or wider, within the bound.
No kernel may reach another device: no remote copies, remote signals or barrier semaphores. Data moves between devices by JAX's collectives and lax.ppermute only.
A program may use at most 128 MiB of HBM per device.

v0:
```python
import jax
import jax.numpy as jnp
from jax import lax
from jax.sharding import PartitionSpec as P


def with_halo(cells, sides, width):
    for axis, dim in sides:
        count = lax.axis_size(axis)
        ends = count - 1
        head = lax.slice_in_dim(cells, 0, width, axis=dim)
        tail = lax.slice_in_dim(cells, cells.shape[dim] - width, cells.shape[dim], axis=dim)
        cells = jnp.concatenate(
            [
                lax.ppermute(tail, axis, [(i, (i + 1) % count) for i in range(ends)]),
                cells,
                lax.ppermute(head, axis, [((i + 1) % count, i) for i in range(ends)]),
            ],
            axis=dim,
        )
    return cells


def silu_slope(value):
    sigma = jax.nn.sigmoid(value)
    return sigma * (1.0 + value * (1.0 - sigma))


def edge_block(
    feat_dst,
    feat_src,
    attr,
    spec_dst,
    spec_src,
    target,
    w_dst,
    w_src,
    w_attr,
    w_mix,
    w_left,
    w_right,
    cg_basis,
    orbital_mask,
):
    pre = jnp.dot(feat_dst, w_dst, preferred_element_type=jnp.float32)
    pre = pre + jnp.dot(feat_src, w_src, preferred_element_type=jnp.float32)
    pre = pre + jnp.dot(attr, w_attr, preferred_element_type=jnp.float32)
    first = jax.nn.silu(pre).astype(jnp.bfloat16)
    mixpre = jnp.dot(first, w_mix, preferred_element_type=jnp.float32)
    second = (first.astype(jnp.float32) + jax.nn.silu(mixpre)).astype(jnp.bfloat16)
    contract_c = (((1,), (1,)), ((), ()))
    left_t = lax.dot_general(w_left, second, contract_c, preferred_element_type=jnp.float32)
    right_t = lax.dot_general(w_right, second, contract_c, preferred_element_type=jnp.float32)
    coupled = (left_t * right_t).astype(jnp.bfloat16)
    predicted = lax.dot_general(
        cg_basis, coupled, (((0,), (0,)), ((), ())), preferred_element_type=jnp.float32
    )
    kinds = orbital_mask.shape[0]
    orbs = orbital_mask.shape[1]
    table = orbital_mask.astype(jnp.float32).T
    onehot_dst = (jnp.arange(kinds, dtype=jnp.int32)[:, None] == spec_dst[None, :]).astype(
        jnp.float32
    )
    onehot_src = (jnp.arange(kinds, dtype=jnp.int32)[:, None] == spec_src[None, :]).astype(
        jnp.float32
    )
    rows_dst = jnp.dot(table, onehot_dst)
    rows_src = jnp.dot(table, onehot_src)
    mask = (rows_dst[:, None, :] * rows_src[None, :, :]).reshape(orbs * orbs, -1)
    resid = mask * (predicted - target.astype(jnp.float32))
    errors = jnp.sum(resid * resid, axis=0) / (orbs * orbs)
    dpred = (resid / (orbs * orbs)).astype(jnp.bfloat16)
    dcoupled = jnp.dot(cg_basis, dpred, preferred_element_type=jnp.float32)
    dleft = (dcoupled * right_t).astype(jnp.bfloat16)
    dright = (dcoupled * left_t).astype(jnp.bfloat16)
    grad_left = jnp.dot(dleft, second, preferred_element_type=jnp.float32)
    grad_right = jnp.dot(dright, second, preferred_element_type=jnp.float32)
    contract_rows = (((0,), (0,)), ((), ()))
    dsecond = lax.dot_general(dleft, w_left, contract_rows, preferred_element_type=jnp.float32)
    dsecond = dsecond + lax.dot_general(
        dright, w_right, contract_rows, preferred_element_type=jnp.float32
    )
    dmix = (dsecond * silu_slope(mixpre)).astype(jnp.bfloat16)
    grad_mix = lax.dot_general(first, dmix, contract_rows, preferred_element_type=jnp.float32)
    dfirst = dsecond + lax.dot_general(dmix, w_mix, contract_c, preferred_element_type=jnp.float32)
    dpre = (dfirst * silu_slope(pre)).astype(jnp.bfloat16)
    grad_dst = lax.dot_general(feat_dst, dpre, contract_rows, preferred_element_type=jnp.float32)
    grad_src = lax.dot_general(feat_src, dpre, contract_rows, preferred_element_type=jnp.float32)
    grad_attr = lax.dot_general(attr, dpre, contract_rows, preferred_element_type=jnp.float32)
    return ((grad_dst, grad_src, grad_attr, grad_mix, grad_left, grad_right), errors)


def local(
    node_feats,
    edge_attr,
    edge_src,
    edge_dst,
    species,
    orbital_mask,
    tile_owner,
    target_send,
    w_dst,
    w_src,
    w_attr,
    w_mix,
    w_left,
    w_right,
    cg_basis,
):
    atom_count = node_feats.shape[1]
    devices = lax.axis_size("edge")
    position = lax.axis_index("edge")
    capacity = target_send.shape[2] // devices
    widened = with_halo(node_feats, (("edge", 1),), atom_count)[0]
    offset = (position - 1) * atom_count
    feat_src = jnp.take(widened, edge_src[0] - offset, axis=0)
    feat_dst = jnp.take(widened, edge_dst[0] - offset, axis=0)
    attr = edge_attr[0]
    spec_src = jnp.take(species[0], edge_src[0])
    spec_dst = jnp.take(species[0], edge_dst[0])
    holder = tile_owner[0, :, 0]
    onehot = (holder[:, None] == jnp.arange(devices, dtype=jnp.int32)[None, :]).astype(jnp.int32)
    before = jnp.cumsum(onehot, axis=0) - onehot
    rank = jnp.sum(before * onehot, axis=1)
    slots = holder * capacity + rank
    weights = (w_dst, w_src, w_attr, w_mix, w_left, w_right, cg_basis, orbital_mask)
    target = jnp.take(
        lax.all_to_all(target_send, "edge", split_axis=2, concat_axis=2, tiled=True), slots, axis=2
    )[0]
    grads, errors = edge_block(feat_dst, feat_src, attr, spec_dst, spec_src, target, *weights)
    grad_dst, grad_src, grad_attr, grad_mix, grad_left, grad_right = grads
    summed = lax.psum(
        (grad_dst, grad_src, grad_attr, grad_mix, grad_left, grad_right), ("rep", "edge")
    )
    return (summed[0], summed[1], summed[2], summed[3], summed[4], summed[5], errors[None, :])


def solution(mesh):
    return jax.shard_map(
        local,
        mesh=mesh,
        in_specs=(
            P("rep", "edge", None),
            P("rep", "edge", None),
            P("rep", "edge"),
            P("rep", "edge"),
            P("rep", None),
            P(),
            P("rep", "edge", None),
            P("rep", "edge", None),
            P(),
            P(),
            P(),
            P(),
            P(),
            P(),
            P(),
        ),
        out_specs=(P(), P(), P(), P(), P(), P(), P("rep", "edge")),
        check_vma=False,
    )
```

profile of v0, /device:TPU:1, one launch (start us, length us, event | category | flops | bytes accessed | tf_op | source)
XLA Modules:
  0.0 583.0 jit_solution(2457980622977366921)
XLA Ops:
  7.2 0.0 copy-start
  7.2 20.5 %copy.37 = bf16[1,729,3072]{1,0,2:T(2,128)(2,1)} copy(bf16[1,729,3072]{2,1,0:T(8,128)(2,1)} %param.26) | data formatting | bytes 8957952 | tf_op args[7]
  27.7 0.5 broadcast.114
  28.2 53.5 %reduce = bf16[3072,729]{1,0:T(8,128)(2,1)} reduce(bf16[3072,1,729]{2,1,0:T(2,128)(2,1)} %bitcast.86, bf16[]{:T(256)} %broadcast.114), dimensions={1}, to_apply=%bitcast.49.reduce_sub_computation | reduce | bytes 8957954
  81.7 11.1 %reshape.160 = bf16[32,2,34992]{2,1,0:T(2,128)(2,1)} reshape(bf16[3072,729]{1,0:T(8,128)(2,1)} %reduce) | data formatting | bytes 8957952
  92.8 12.1 %all-to-all-start = ((bf16[32,2,34992]{2,1,0:T(2,128)(2,1)}), bf16[32,2,34992]{2,1,0:T(2,128)(2,1)}, u32[]{:S(2)}, u32[]{:S(2)}) async-start(bf16[32,2,34992]{2,1,0:T(2,128)(2,1)} %reshape.160), calls=%async_computation | async-start | bytes 8978432 | tf_op jit(solution)/shard_map/all_to_all | solution.py:128
  104.9 0.0 all-reduce.3.cloned.1.call-start
  105.0 1.3 collective-permute-start.1
  106.3 4.2 collective-permute-start
  110.5 11.8 %gather_fusion.2 = s32[2048]{0:T(1024)S(1)} fusion(s32[8192]{0:T(1024)S(1)} %bitcast.81, s32[2048]{0:T(1024)S(1)} %fusion.15), kind=kCustom, calls=%fused_computation.1.clone | custom fusion | bytes 24576 | tf_op jit(solution)/shard_map/jit(_take)/gather | solution.py:120
  122.3 0.0 copy-start.15
  122.3 0.0 copy-start.21
  122.3 11.8 %gather_fusion.3 = s32[2048]{0:T(1024)S(1)} fusion(s32[8192]{0:T(1024)S(1)} %bitcast.82, s32[2048]{0:T(1024)S(1)} %fusion.16), kind=kCustom, calls=%fused_computation.3.clone | custom fusion | bytes 24576 | tf_op jit(solution)/shard_map/jit(_take)/gather | solution.py:119
  134.2 9.1 %reduce-window.6 = s32[32,16,128]{2,1,0:T(8,128)S(1)} reduce-window(s32[32,16,128]{2,1,0:T(8,128)S(1)} %fusion.9, s32[]{:T(128)} %constant.41.clone.1), window={size=1x1x128 pad=0_0x0_0x127_0}, to_apply=%region_0.3 | reduce-window | flops 8323072 | bytes 524292 | tf_op jit(solution)/shard_map/reduce-window
  143.2 0.1 slice.18
  143.4 0.2 copy.42
  143.6 0.2 reduce-window.9
  143.8 0.1 broadcast_add_fusion
  143.9 0.1 fusion.8
  144.1 0.2 convolution_bitcast_fusion
  144.4 0.2 convolution_bitcast_fusion.1
  144.6 3.7 broadcast_multiply_fusion
  148.4 6.5 %mul.92 = f32[729,2048]{1,0:T(8,128)} reshape(f32[27,27,2048]{2,1,0:T(8,128)} %broadcast_multiply_fusion) | data formatting | bytes 11943936 | tf_op jit(solution)/shard_map/mul | solution.py:69
  154.9 6.2 %gather_fusion.1 = bf16[2048,128]{1,0:T(8,128)(2,1)S(1)} fusion(bf16[768,128]{1,0:T(8,128)(2,1)S(1)} %maximum_bitcast_fusion, s32[2048]{0:T(1024)S(1)} %get-tuple-element.47), kind=kCustom, calls=%fused_computation.clone | custom fusion | bytes 1056768 | tf_op jit(solution)/shard_map/jit(_take)/gather | solution.py:117
  161.1 0.0 copy-start.22
  161.1 6.2 %gather_fusion.4 = bf16[2048,128]{1,0:T(8,128)(2,1)S(1)} fusion(bf16[768,128]{1,0:T(8,128)(2,1)S(1)} %maximum_bitcast_fusion, s32[2048]{0:T(1024)S(1)} %get-tuple-element.60), kind=kCustom, calls=%fused_computation.2.clone | custom fusion | bytes 1056768 | tf_op jit(solution)/shard_map/jit(_take)/gather | solution.py:116
  167.3 0.0 copy-start.23
  167.3 0.7 fusion.11
  168.0 0.7 convolution_add_fusion.3
  168.8 0.0 copy-start.7
  168.8 1.4 multiply_convert_fusion.7
  170.2 0.9 copy-done.11
  171.0 1.4 add_convert_fusion
  172.4 3.6 fusion.26
  176.0 3.5 fusion.27
  179.5 24.6 %all-to-all-done = bf16[32,2,34992]{2,1,0:T(2,128)(2,1)} async-done(((bf16[32,2,34992]{2,1,0:T(2,128)(2,1)}), bf16[32,2,34992]{2,1,0:T(2,128)(2,1)}, u32[]{:S(2)}, u32[]{:S(2)}) %all-to-all-start) | async-done | bytes 4479008 | tf_op jit(solution)/shard_map/all_to_all | solution.py:128
  204.1 24.2 %reshape.161 = bf16[3072,1,729]{2,1,0:T(2,128)(2,1)} reshape(bf16[32,2,34992]{2,1,0:T(2,128)(2,1)} %all-to-all-done) | data formatting | bytes 8957952
  228.3 6.7 %copy.47 = bf16[1,729,3072]{1,2,0:T(8,128)(2,1)} copy(bf16[1,729,3072]{1,0,2:T(2,128)(2,1)} %bitcast.87) | data formatting | bytes 8957952 | tf_op jit(solution)/shard_map/all_to_all | solution.py:128
  235.0 13.1 %gather_fusion = bf16[2048,729]{1,0:T(8,128)(2,1)} fusion(bf16[729,3072]{0,1:T(8,128)(2,1)} %bitcast.83, s32[2048]{0:T(1024)S(1)} %broadcast_clamp_fusion), kind=kCustom, calls=%fused_computation.4 | custom fusion | bytes 5980160 | tf_op jit(solution)/shard_map/jit(_take)/gather | solution.py:127
  248.1 4.9 copy.40
  253.0 10.7 %multiply_reduce_fusion = (f32[2048]{0:T(1024)S(1)}, f32[729,2048]{1,0:T(8,128)S(1)}) fusion(f32[729,2048]{1,0:T(8,128)} %mul.92, bf16[2048,729]{0,1:T(8,128)(2,1)} %copy.40, pred[2048]{0:T(1024)(128)(4,1)S(1)} %compare_and_fusion.2, bf16[729,729]{1,0:T(8,128)(2,1)S(1)} %copy-done, f32[2048,729]{0,1:T(8,128)} %fusion.26, f32[2048,729]{0,1:T(8,128)} %fusion.27), kind=kOutput, calls=%fused_computation.6 | convolution fusion | flops 2188724224 | bytes 27946978 | tf_op jit(solution)/shard_map/dot_general | solution.py:55
  263.7 7.2 %multiply_convert_fusion = (bf16[2048,729]{0,1:T(8,128)(2,1)}, bf16[2048,729]{0,1:T(8,128)(2,1)S(1)}) fusion(f32[2048,729]{0,1:T(8,128)S(1)} %bitcast.85, f32[2048,729]{0,1:T(8,128)} %fusion.27, bf16[729,729]{1,0:T(8,128)(2,1)S(1)} %copy-done, f32[729,2048]{1,0:T(8,128)S(1)} %get-tuple-element.56), kind=kOutput, calls=%fused_computation.7 | convolution fusion | flops 2185740288 | bytes 24950754 | tf_op jit(solution)/shard_map/dot_general | solution.py:73
  270.9 1.1 fusion.28
  272.0 0.8 copy-done.2
  272.8 0.3 copy-done.25
  273.1 1.1 multiply_convert_fusion.6
  274.3 0.1 copy-done.24
  274.3 0.5 fusion.3
  274.9 0.4 copy-done.4
  275.3 1.3 fusion.10
  276.7 1.3 fusion.12
  278.0 1.0 convolution_bitcast_fusion.2
  279.0 1.0 fusion.29
  279.9 1.7 fusion.30
  281.6 1.7 fusion.31
  283.3 0.0 all-reduce.3.cloned.1.call-update
  283.3 0.6 broadcast_multiply_fusion.1
  283.9 282.7 %all-reduce.3.cloned.1.call-done = (f32[128,128]{1,0:T(8,128)}, f32[128,128]{1,0:T(8,128)}, f32[128,128]{0,1:T(8,128)}, f32[128,128]{1,0:T(8,128)}, f32[729,128]{1,0:T(8,128)}, /*index=5*/f32[729,128]{1,0:T(8,128)}) async-done(((f32[128,128]{1,0:T(8,128)}, f32[128,128]{1,0:T(8,128)}, f32[128,128]{0,1:T(8,128)}, f32[128,128]{1,0:T(8,128)}, f32[729,128]{1,0:T(8,128)}, /*index=5*/f32[729,128]{1,0:T(8,128)}), ...) | async-done | bytes 1008656 | tf_op jit(solution)/shard_map/psum | solution.py:132
  566.6 1.6 copy.41
  568.2 1.5 copy.54
  569.7 1.5 copy.55
  571.1 1.5 copy.56
  572.6 1.8 copy.57
  574.4 1.8 copy.58
  (57 shorter events, 0.2 us)
Async XLA Ops:
  7.2 245.8 %copy-start = (bf16[729,729]{1,0:T(8,128)(2,1)S(1)}, bf16[729,729]{1,0:T(8,128)(2,1)}, u32[]{:S(2)}) copy-start(bf16[729,729]{1,0:T(8,128)(2,1)} %param.33) | copy-start | bytes 3188650
  92.8 12.2 %copy-start.18 = (bf16[1,256,128]{2,1,0:T(8,128)(2,1)S(1)}, bf16[1,256,128]{2,1,0:T(8,128)(2,1)}, u32[]{:S(2)}) copy-start(bf16[1,256,128]{2,1,0:T(8,128)(2,1)} %param.19) | copy-start | bytes 196612
  92.8 17.7 %copy-start.16 = (s32[1,2048]{1,0:T(1,128)S(1)}, s32[1,2048]{1,0:T(1,128)}, u32[]{:S(2)}) copy-start(s32[1,2048]{1,0:T(1,128)} %param.22) | copy-start | bytes 24580
  92.8 17.7 %copy-start.1 = (s32[1,8192]{1,0:T(1,128)S(1)}, s32[1,8192]{1,0:T(1,128)}, u32[]{:S(2)}) copy-start(s32[1,8192]{1,0:T(1,128)} %param.23) | copy-start | bytes 98308
  92.8 111.3 %all-to-all-start = ((bf16[32,2,34992]{2,1,0:T(2,128)(2,1)}), bf16[32,2,34992]{2,1,0:T(2,128)(2,1)}, u32[]{:S(2)}, u32[]{:S(2)}) async-start(bf16[32,2,34992]{2,1,0:T(2,128)(2,1)} %reshape.160), calls=%async_computation | async-start | bytes 8978432 | tf_op jit(solution)/shard_map/all_to_all | solution.py:128
  104.9 17.4 %copy-start.17 = (s32[1,2048]{1,0:T(1,128)S(1)}, s32[1,2048]{1,0:T(1,128)}, u32[]{:S(2)}) copy-start(s32[1,2048]{1,0:T(1,128)} %param.21) | copy-start | bytes 24580
  104.9 461.7 %all-reduce.3.cloned.1.call-start = ((), (), s32[]{:S(2)}) async-start(), calls=%async_computation.1 | async-start | bytes 2031616 | tf_op jit(solution)/shard_map/psum | solution.py:132
  105.0 49.9 %collective-permute-start.1 = (bf16[1,256,128]{2,1,0:T(8,128)(2,1)S(1)}, bf16[1,256,128]{2,1,0:T(8,128)(2,1)S(1)}, u32[]{:S(2)}, u32[]{:S(2)}) collective-permute-start(bf16[1,256,128]{2,1,0:T(8,128)(2,1)S(1)} %copy-done.18), channel_id=1, source_target_pairs={{1,0},{2,1},{3,2},{4,3},{5,4},{6,5},{7,6},{8,7},{9,8},{10,9},{11,1... | collective-permute-start | bytes 196616 | tf_op jit(solution)/shard_map/ppermute | solution.py:17
  106.3 48.6 %collective-permute-start = (bf16[1,256,128]{2,1,0:T(8,128)(2,1)S(1)}, bf16[1,256,128]{2,1,0:T(8,128)(2,1)S(1)}, u32[]{:S(2)}, u32[]{:S(2)}) collective-permute-start(bf16[1,256,128]{2,1,0:T(8,128)(2,1)S(1)} %copy-done.18), channel_id=1, source_target_pairs={{0,1},{1,2},{2,3},{3,4},{4,5},{5,6},{6,7},{7,8},{8,9},{9,10},{10,1... | collective-permute-start | bytes 196616 | tf_op jit(solution)/shard_map/ppermute | solution.py:15
  122.3 11.8 %copy-start.15 = (s32[1,2048,1]{1,2,0:T(1,128)S(1)}, s32[1,2048,1]{1,2,0:T(1,128)}, u32[]{:S(2)}) copy-start(s32[1,2048,1]{1,2,0:T(1,128)} %param.25) | copy-start | bytes 24580
  122.3 21.8 %copy-start.21 = (s32[3,27]{1,0:T(4,128)S(1)}, s32[3,27]{1,0:T(4,128)}, u32[]{:S(2)}) copy-start(s32[3,27]{1,0:T(4,128)} %param.24) | copy-start | bytes 976
  154.9 12.5 %copy-start.20 = (bf16[128,128]{1,0:T(8,128)(2,1)S(1)}, bf16[128,128]{1,0:T(8,128)(2,1)}, u32[]{:S(2)}) copy-start(bf16[128,128]{1,0:T(8,128)(2,1)} %param.27) | copy-start | bytes 98308
  154.9 13.2 %copy-start.19 = (bf16[128,128]{1,0:T(8,128)(2,1)S(1)}, bf16[128,128]{1,0:T(8,128)(2,1)}, u32[]{:S(2)}) copy-start(bf16[128,128]{1,0:T(8,128)(2,1)} %param.28) | copy-start | bytes 98308
  161.1 7.7 %copy-start.3 = (bf16[2048,128]{1,0:T(8,128)(2,1)}, bf16[2048,128]{1,0:T(8,128)(2,1)S(1)}, u32[]{:S(2)}) copy-start(bf16[2048,128]{1,0:T(8,128)(2,1)S(1)} %gather_fusion.1) | copy-start | bytes 1572868
  161.1 7.7 %copy-start.9 = (bf16[1,2048,128]{2,1,0:T(8,128)(2,1)S(1)}, bf16[1,2048,128]{2,1,0:T(8,128)(2,1)}, u32[]{:S(2)}) copy-start(bf16[1,2048,128]{2,1,0:T(8,128)(2,1)} %param.20) | copy-start | bytes 1572868
  161.1 7.7 %copy-start.22 = (bf16[128,128]{1,0:T(8,128)(2,1)S(1)}, bf16[128,128]{1,0:T(8,128)(2,1)}, u32[]{:S(2)}) copy-start(bf16[128,128]{1,0:T(8,128)(2,1)} %param.29) | copy-start | bytes 98308
  167.3 2.9 copy-start.5
  167.3 3.7 copy-start.23
  168.8 3.6 copy-start.7
  170.2 0.9 copy-start.11
  172.4 3.6 copy-start.13
  248.1 15.6 %slice-start = ((s8[6029312]{0:T(1024)(128)(4,1)}), s8[1835008]{0:T(1024)(128)(4,1)S(1)}, s32[]{:S(2)}) async-start(s8[6029312]{0:T(1024)(128)(4,1)} %bitcast.84), calls=%async_computation.2 | async-start | bytes 3670016
  253.0 10.7 %slice-start.1 = ((s8[6029312]{0:T(1024)(128)(4,1)}), s8[4194304]{0:T(1024)(128)(4,1)S(1)}, s32[]{:S(2)}) async-start(s8[6029312]{0:T(1024)(128)(4,1)} %bitcast.84), calls=%async_computation.3 | async-start | bytes 8388608
  263.7 7.2 %copy-start.8 = (bf16[729,128]{1,0:T(8,128)(2,1)S(1)}, bf16[729,128]{1,0:T(8,128)(2,1)}, u32[]{:S(2)}) copy-start(bf16[729,128]{1,0:T(8,128)(2,1)} %param.31) | copy-start | bytes 559876
  270.9 1.9 copy-start.2
  270.9 1.9 copy-start.14
  270.9 2.2 copy-start.25
  273.1 1.2 copy-start.24
  274.3 1.1 copy-start.4
  274.3 2.4 copy-start.6
  274.3 3.6 copy-start.10
  274.3 4.6 copy-start.12
Sparse Core Ops, SparseCore 0:
  283.5 283.1 all-reduce.2
where the time goes:
time: 585 us; the launch traced here: 583 us
  waiting for transfers between devices  307 us (52%)
  local copies, waits for them, and re-layouts  136 us (23%)
  other arithmetic  67.4 us (12%)
  matrix products  40.2 us (7%)
  starting transfers between devices  17.6 us (3%)
  between operations  14.5 us (2%)
    psum x1, waiting for transfers between devices, local(): lax.psum((grad_dst, grad_src, grad_attr, grad_mix, grad_left, grad_right)...  283 us
    unnamed x66, local copies, waits for them, and re-layouts  68.4 us
    unnamed x2, other arithmetic  53.5 us
    all_to_all x1, waiting for transfers between devices, local(): lax.all_to_all(target_send, 'edge', split_axis=2, concat_axis=2, tiled=True)  24.6 us
    gather x2, local copies, waits for them, and re-layouts, local(): jnp.take(lax.all_to_all(target_send, 'edge', split_axis=2, concat_axis=2,...  18 us
    all_to_all x1, starting transfers between devices, local(): lax.all_to_all(target_send, 'edge', split_axis=2, concat_axis=2, tiled=True)  12.1 us
    gather x1, local copies, waits for them, and re-layouts, local(): spec_dst = jnp.take(species[0], edge_dst[0])  11.8 us
    gather x1, local copies, waits for them, and re-layouts, local(): spec_src = jnp.take(species[0], edge_src[0])  11.8 us
  transfers between devices with their start and end apart: 4, of which 2 were waited for; matrix products, arithmetic and copies ran while one was open for 12% of the time, Pallas kernels for 0%

commit v1 on v0

v1 whole, which is shorter than its diff:
```python
import jax
import jax.numpy as jnp
import numpy as np
from jax import lax
from jax.experimental import pallas as pl
from jax.experimental.pallas import tpu as pltpu
from jax.sharding import PartitionSpec as P

F32 = jnp.float32
BF16 = jnp.bfloat16
GROUP = 8
TAIL = 16
LANES = 128
CHUNK = 256
MIB = 1 << 20


def ring(count, shift):
    return [(i, (i + shift) % count) for i in range(count)]


def matmul(a, b):
    return jnp.dot(a, b, preferred_element_type=F32)


def matmul_nt(a, b):
    return lax.dot_general(a, b, (((1,), (1,)), ((), ())), preferred_element_type=F32)


def matmul_tn(a, b):
    return lax.dot_general(a, b, (((0,), (0,)), ((), ())), preferred_element_type=F32)


def indicator(condition):
    return jnp.where(condition, 1.0, 0.0).astype(BF16)


def slope(value, sigma):
    return sigma * (1.0 + value * (1.0 - sigma))


def slot_onehot(out, holder, rank, base, capacity):
    edges = holder.shape[1]
    place = lax.broadcasted_iota(jnp.int32, (capacity, edges), 0)
    for p in range(GROUP):
        mine = jnp.where(holder == base + p, rank, -1)
        out[p * capacity : (p + 1) * capacity, :] = indicator(place == mine)


def edge_kernel(
    pos_ref,
    dst_ref,
    src_ref,
    holder_ref,
    spec_lo,
    spec_mid,
    spec_hi,
    node_lo,
    node_mid,
    node_hi,
    attr_ref,
    wdst_t,
    wsrc_t,
    wattr_t,
    wmix_t,
    out_ref,
    rank_ref,
    xdst_ref,
    xsrc_ref,
    first_ref,
    pre_ref,
    mixpre_ref,
    second,
    onehot,
    tags,
):
    step = pl.program_id(0)
    edges = dst_ref.shape[1]
    devices = tags.shape[0] // 2
    capacity = out_ref.shape[1] - TAIL
    atoms = node_mid.shape[0]
    holder = holder_ref[...]

    @pl.when(step == 0)
    def _():
        offset = pos_ref[0] * atoms
        same = lax.broadcasted_iota(jnp.int32, (devices, edges), 0) == holder
        named = jnp.where(same, 1.0, 0.0)
        named_bf = named.astype(BF16)
        rows = lax.broadcasted_iota(jnp.int32, (CHUNK, CHUNK), 0)
        cols = lax.broadcasted_iota(jnp.int32, (CHUNK, CHUNK), 1)
        earlier = indicator(rows < cols)
        carry = jnp.zeros((devices, 1), F32)
        for c in range(edges // CHUNK):
            part = slice(c * CHUNK, (c + 1) * CHUNK)
            before = matmul(named_bf[:, part], earlier) + carry
            carry = carry + jnp.sum(named[:, part], axis=1, keepdims=True)
            rank_ref[:, part] = jnp.sum(
                before * named[:, part], axis=0, keepdims=True
            ).astype(jnp.int32)
        rank = rank_ref[...]

        def table_of(nodes, spec):
            kinds = jnp.broadcast_to((spec[...] + 1).astype(F32), (TAIL, atoms)).astype(BF16)
            return jnp.concatenate([nodes[...].T, kinds], axis=0)

        table_mid = table_of(node_mid, spec_mid)
        table = jnp.concatenate(
            [table_of(node_lo, spec_lo), table_mid, table_of(node_hi, spec_hi)], axis=1
        )
        channels = node_mid.shape[1]
        ids = lax.broadcasted_iota(jnp.int32, (atoms, edges), 0)
        from_dst = matmul(table_mid, indicator(ids == dst_ref[...] - offset))
        ids = lax.broadcasted_iota(jnp.int32, (3 * atoms, edges), 0)
        from_src = matmul(table, indicator(ids == src_ref[...] - (offset - atoms)))
        xdst = from_dst[:channels].astype(BF16)
        xsrc = from_src[:channels].astype(BF16)
        xdst_ref[...] = xdst
        xsrc_ref[...] = xsrc
        pre = matmul(wdst_t[...], xdst) + matmul(wsrc_t[...], xsrc)
        pre = pre + matmul_nt(wattr_t[...], attr_ref[...])
        pre_ref[...] = pre
        first = (pre * jax.nn.sigmoid(pre)).astype(BF16)
        first_ref[...] = first
        mixpre = matmul(wmix_t[...], first)
        mixpre_ref[...] = mixpre
        second[...] = (first.astype(F32) + mixpre * jax.nn.sigmoid(mixpre)).astype(BF16)
        tagged = jnp.concatenate(
            [named * from_dst[channels : channels + 1], named * from_src[channels : channels + 1]],
            axis=0,
        ).astype(BF16)
        at_rank = indicator(lax.broadcasted_iota(jnp.int32, (LANES, edges), 0) == rank)
        tags[...] = matmul_nt(tagged, at_rank)

    slot_onehot(onehot, holder, rank_ref[...], step * GROUP, capacity)
    moved = matmul_nt(onehot[...], second[...]).astype(BF16)
    line = lax.broadcasted_iota(jnp.int32, (TAIL, LANES), 0)
    for p in range(GROUP):
        out_ref[p, :capacity, :] = moved[p * capacity : (p + 1) * capacity]
        tag_dst = tags[pl.ds(step * GROUP + p, 1), :]
        tag_src = tags[pl.ds(devices + step * GROUP + p, 1), :]
        tail = jnp.where(line == 0, tag_dst, jnp.where(line == 1, tag_src, 0.0))
        out_ref[p, capacity:, :] = tail.astype(BF16)


def holder_kernel(
    recv_ref,
    target_ref,
    wlr_ref,
    wlr_t,
    cg_ref,
    cg_t,
    pairs_ref,
    place_ref,
    back_ref,
    grad_ref,
    dlr,
):
    step = pl.program_id(0)
    capacity = recv_ref.shape[1] - TAIL
    width = GROUP * capacity
    channels = recv_ref.shape[2]
    rows = cg_ref.shape[0]
    orb2 = target_ref.shape[1]
    kinds = 3
    second = recv_ref[:, :capacity, :].reshape(width, channels)
    line = lax.broadcasted_iota(jnp.int32, (GROUP * TAIL, width), 0)
    start = place_ref[0:1, :]
    spread = indicator(lax.broadcasted_iota(jnp.int32, (LANES, width), 0) == place_ref[1:2, :])
    tails = recv_ref[:, capacity:, :].reshape(GROUP * TAIL, LANES)
    tags = matmul(tails, spread)
    tag_dst = jnp.sum(jnp.where(line == start, tags, 0.0), axis=0, keepdims=True)
    tag_src = jnp.sum(jnp.where(line == start + 1, tags, 0.0), axis=0, keepdims=True)
    code = jnp.where(tag_dst > 0.5, (tag_dst - 1.0) * kinds + (tag_src - 1.0), -1.0)
    code = code.astype(jnp.int32)
    pair_line = lax.broadcasted_iota(jnp.int32, (pairs_ref.shape[1], width), 0)
    pair = indicator(pair_line == code)
    errors = []
    for n in range(width // CHUNK):
        part = slice(n * CHUNK, (n + 1) * CHUNK)
        both = matmul_nt(wlr_ref[...], second[part])
        left = both[:rows]
        right = both[rows:]
        predicted = matmul(cg_t[...], (left * right).astype(BF16))
        mask = matmul(pairs_ref[...], pair[:, part])
        goal = target_ref[0, :, part].astype(F32)
        goal = jnp.concatenate([goal, jnp.zeros((rows - orb2, CHUNK), F32)], axis=0)
        resid = mask * (predicted - goal)
        errors.append(jnp.sum(resid * resid, axis=0, keepdims=True) / orb2)
        dpred = (resid / orb2).astype(BF16)
        dcoupled = matmul(cg_ref[...], dpred)
        dlr[:rows, part] = (dcoupled * right).astype(BF16)
        dlr[rows:, part] = (dcoupled * left).astype(BF16)
    dsecond = matmul(wlr_t[...], dlr[...])
    moved = dsecond.T.astype(BF16)
    for q in range(GROUP):
        back_ref[q, :capacity, :] = moved[q * capacity : (q + 1) * capacity]
    error = jnp.concatenate(errors, axis=1)
    high = error.astype(BF16).astype(F32)
    middle = (error - high).astype(BF16).astype(F32)
    low = error - high - middle
    packed = jnp.where(
        line == start,
        high,
        jnp.where(line == start + 1, middle, jnp.where(line == start + 2, low, 0.0)),
    ).astype(BF16)
    spelled = matmul_nt(packed, spread).astype(BF16)
    for q in range(GROUP):
        back_ref[q, capacity:, :] = spelled[q * TAIL : (q + 1) * TAIL]
    grad = matmul(dlr[...], second)

    @pl.when(step == 0)
    def _():
        grad_ref[...] = grad

    @pl.when(step > 0)
    def _():
        grad_ref[...] += grad


def finish_kernel(
    back_ref,
    holder_ref,
    rank_ref,
    xdst_ref,
    xsrc_ref,
    attr_ref,
    first_ref,
    pre_ref,
    mixpre_ref,
    wmix,
    grad_ref,
    error_ref,
    onehot,
    dsecond,
    found,
):
    step = pl.program_id(0)
    capacity = back_ref.shape[1] - TAIL
    edges = holder_ref.shape[1]
    channels = back_ref.shape[2]
    holder = holder_ref[...]
    rank = rank_ref[...]

    @pl.when(step == 0)
    def _():
        dsecond[...] = jnp.zeros_like(dsecond)
        found[...] = jnp.zeros_like(found)

    slot_onehot(onehot, holder, rank, step * GROUP, capacity)
    rows = back_ref[:, :capacity, :].reshape(GROUP * capacity, channels)
    dsecond[...] += matmul_tn(rows, onehot[...])
    line = lax.broadcasted_iota(jnp.int32, (GROUP * TAIL, edges), 0)
    low = (holder - step * GROUP) * TAIL
    at_holder = indicator(jnp.logical_and(line >= low, line < low + TAIL))
    tails = back_ref[:, capacity:, :].reshape(GROUP * TAIL, LANES)
    found[...] += matmul_tn(tails, at_holder)

    @pl.when(step == pl.num_programs(0) - 1)
    def _():
        place = lax.broadcasted_iota(jnp.int32, found.shape, 0)
        error_ref[...] = jnp.sum(
            jnp.where(place == rank, found[...], 0.0), axis=0, keepdims=True
        )
        dsec = dsecond[...]
        mixpre = mixpre_ref[...]
        dmix = (dsec * slope(mixpre, jax.nn.sigmoid(mixpre))).astype(BF16)
        dfirst = dsec + matmul(wmix[...], dmix)
        pre = pre_ref[...]
        dpre = (dfirst * slope(pre, jax.nn.sigmoid(pre))).astype(BF16)
        grad_ref[0:channels] = matmul_nt(xdst_ref[...], dpre)
        grad_ref[channels : 2 * channels] = matmul_nt(xsrc_ref[...], dpre)
        grad_ref[2 * channels : 3 * channels] = matmul(dpre, attr_ref[...]).T
        grad_ref[3 * channels : 4 * channels] = matmul_nt(first_ref[...], dmix)


def exchange(array, axis, groups):
    return lax.all_to_all(
        array, axis, split_axis=0, concat_axis=0, tiled=True, axis_index_groups=groups
    )


def sum_everywhere(part, wide, narrow, deep):
    half = part.shape[0] // 2
    core = lax.rem(lax.axis_index("rep"), 2)
    swap = [(i, i ^ 1) for i in range(wide * 2)]
    keep = lax.dynamic_slice_in_dim(part, core * half, half, 0)
    give = lax.dynamic_slice_in_dim(part, (1 - core) * half, half, 0)
    part = keep + lax.ppermute(give, "rep", swap)
    edge = narrow * deep
    plane = [
        [(y * 2 + c) * edge + z * narrow + x for y in range(wide) for x in range(narrow)]
        for c in range(2)
        for z in range(deep)
    ]
    column = [[z * narrow + x for z in range(deep)] for x in range(narrow)]
    peers = wide * narrow
    got = exchange(part, ("rep", "edge"), plane)
    part = jnp.sum(got.reshape(peers, half // peers, -1), axis=0)
    got = exchange(jnp.tile(part, (deep, 1)), "edge", column)
    part = jnp.sum(got.reshape(deep, half // peers, -1), axis=0)
    part = exchange(jnp.tile(part, (peers, 1)), ("rep", "edge"), plane)
    other = lax.ppermute(part, "rep", swap)
    low = jnp.where(core == 0, part, other)
    high = jnp.where(core == 0, other, part)
    return jnp.concatenate([low, high], axis=0)


def local(
    node_feats,
    edge_attr,
    edge_src,
    edge_dst,
    species,
    orbital_mask,
    tile_owner,
    target_send,
    w_dst,
    w_src,
    w_attr,
    w_mix,
    w_left,
    w_right,
    cg_basis,
):
    atoms, channels = node_feats.shape[1:]
    edges = edge_attr.shape[1]
    orb2, columns = target_send.shape[1:]
    devices = lax.axis_size("edge")
    capacity = columns // devices
    steps = devices // GROUP
    block = capacity + TAIL
    position = lax.axis_index("edge")
    rows = -(-orb2 // 32) * 32
    nodes = node_feats[0]
    node_lo = lax.ppermute(nodes, "edge", ring(devices, 1))
    node_hi = lax.ppermute(nodes, "edge", ring(devices, -1))
    holder = tile_owner.reshape(1, edges)
    attr = edge_attr[0]

    def whole(shape):
        return pl.BlockSpec(shape, lambda *_: (0,) * len(shape))

    def kinds_of(shift):
        return pl.BlockSpec(
            (1, atoms), lambda i, pos: (0, jnp.clip(pos[0] + shift, 0, devices - 1))
        )

    square = whole((channels, channels))
    line = whole((1, edges))
    wide = whole((channels, edges))
    sent, rank, xdst, xsrc, first, pre, mixpre = pl.pallas_call(
        edge_kernel,
        out_shape=(
            jax.ShapeDtypeStruct((devices, block, channels), BF16),
            jax.ShapeDtypeStruct((1, edges), jnp.int32),
            jax.ShapeDtypeStruct((channels, edges), BF16),
            jax.ShapeDtypeStruct((channels, edges), BF16),
            jax.ShapeDtypeStruct((channels, edges), BF16),
            jax.ShapeDtypeStruct((channels, edges), F32),
            jax.ShapeDtypeStruct((channels, edges), F32),
        ),
        grid_spec=pltpu.PrefetchScalarGridSpec(
            num_scalar_prefetch=1,
            grid=(steps,),
            in_specs=[
                line,
                line,
                line,
                kinds_of(-1),
                kinds_of(0),
                kinds_of(1),
                whole((atoms, channels)),
                whole((atoms, channels)),
                whole((atoms, channels)),
                whole((edges, channels)),
                square,
                square,
                square,
                square,
            ],
            out_specs=[
                pl.BlockSpec((GROUP, block, channels), lambda i, pos: (i, 0, 0)),
                line,
                wide,
                wide,
                wide,
                wide,
                wide,
            ],
            scratch_shapes=[
                pltpu.VMEM((channels, edges), BF16),
                pltpu.VMEM((GROUP * capacity, edges), BF16),
                pltpu.VMEM((2 * devices, LANES), F32),
            ],
        ),
        compiler_params=pltpu.CompilerParams(vmem_limit_bytes=48 * MIB),
    )(
        position.astype(jnp.int32)[None],
        edge_dst,
        edge_src,
        holder,
        species,
        species,
        species,
        node_lo,
        nodes,
        node_hi,
        attr,
        w_dst.T,
        w_src.T,
        w_attr.T,
        w_mix.T,
    )

    received = lax.all_to_all(sent, "edge", split_axis=0, concat_axis=0, tiled=True)

    pad = ((0, rows - orb2), (0, 0))
    wlr = jnp.concatenate([jnp.pad(w_left, pad), jnp.pad(w_right, pad)], axis=0)
    cg = jnp.pad(cg_basis, ((0, rows - orb2), (0, rows - orb2)))
    carried = orbital_mask.astype(F32)
    pairs = (carried[:, None, :, None] * carried[None, :, None, :]).reshape(-1, orb2).T
    pairs = jnp.pad(pairs, ((0, rows - orb2), (0, TAIL - pairs.shape[1]))).astype(BF16)
    slots = np.arange(GROUP * capacity)
    places = jnp.asarray(
        np.stack([slots // capacity * TAIL, slots % capacity]).astype(np.int32)
    )
    back, grad_wide = pl.pallas_call(
        holder_kernel,
        out_shape=(
            jax.ShapeDtypeStruct((devices, block, channels), BF16),
            jax.ShapeDtypeStruct((2 * rows, channels), F32),
        ),
        grid=(steps,),
        in_specs=[
            pl.BlockSpec((GROUP, block, channels), lambda i: (i, 0, 0)),
            pl.BlockSpec((1, orb2, GROUP * capacity), lambda i: (0, 0, i)),
            whole(wlr.shape),
            whole(wlr.shape[::-1]),
            whole(cg.shape),
            whole(cg.shape),
            whole(pairs.shape),
            whole(places.shape),
        ],
        out_specs=[
            pl.BlockSpec((GROUP, block, channels), lambda i: (i, 0, 0)),
            whole((2 * rows, channels)),
        ],
        scratch_shapes=[pltpu.VMEM((2 * rows, GROUP * capacity), BF16)],
        compiler_params=pltpu.CompilerParams(vmem_limit_bytes=56 * MIB),
    )(received, target_send, wlr, wlr.T, cg, cg.T, pairs, places)

    returned = lax.all_to_all(back, "edge", split_axis=0, concat_axis=0, tiled=True)

    grad_small, errors = pl.pallas_call(
        finish_kernel,
        out_shape=(
            jax.ShapeDtypeStruct((4 * channels, channels), F32),
            jax.ShapeDtypeStruct((1, edges), F32),
        ),
        grid=(steps,),
        in_specs=[
            pl.BlockSpec((GROUP, block, channels), lambda i: (i, 0, 0)),
            line,
            line,
            wide,
            wide,
            whole((edges, channels)),
            wide,
            wide,
            wide,
            square,
        ],
        out_specs=[whole((4 * channels, channels)), line],
        scratch_shapes=[
            pltpu.VMEM((GROUP * capacity, edges), BF16),
            pltpu.VMEM((channels, edges), F32),
            pltpu.VMEM((LANES, edges), F32),
        ],
        compiler_params=pltpu.CompilerParams(vmem_limit_bytes=48 * MIB),
    )(returned, holder, rank, xdst, xsrc, attr, first, pre, mixpre, w_mix)

    used = 4 * channels + 2 * rows
    unit = 256 * 8
    total = -(-used // unit) * unit
    grads = jnp.concatenate(
        [grad_small, grad_wide, jnp.zeros((total - used, channels), F32)], axis=0
    )
    grads = sum_everywhere(grads, 4, 4, 8)
    outs = [grads[i * channels : (i + 1) * channels] for i in range(4)]
    outs += [grads[4 * channels + i * rows :][:orb2] for i in range(2)]
    return (*outs, errors)


def solution(mesh):
    return jax.shard_map(
        local,
        mesh=mesh,
        in_specs=(
            P("rep", "edge", None),
            P("rep", "edge", None),
            P("rep", "edge"),
            P("rep", "edge"),
            P("rep", None),
            P(),
            P("rep", "edge", None),
            P("rep", "edge", None),
            P(),
            P(),
            P(),
            P(),
            P(),
            P(),
            P(),
        ),
        out_specs=(P(), P(), P(), P(), P(), P(), P("rep", "edge")),
        check_vma=False,
    )
```

time: 585 us -> 179 us (0.31)
  waiting for transfers between devices: 307 us -> 31.9 us
  local copies, waits for them, and re-layouts: 136 us -> 28.4 us
  other arithmetic: 67.4 us -> 3.46 us
  blocking collectives: 0 us -> 41.6 us
  Pallas kernels: 0 us -> 40.6 us
  matrix products: 40.2 us -> 0 us
  starting transfers between devices: 17.6 us -> 31.3 us
  between operations: 14.5 us -> 0.82 us
    psum x1 -> x0, waiting for transfers between devices: 283 us -> none  [local(): lax.psum((grad_dst, grad_src, grad_attr, grad_mix, grad_left, grad_right)...]
    gather x6 -> x0, local copies, waits for them, and re-layouts: 53.9 us -> none  [the longest x2 18 us: local(): jnp.take(lax.all_to_all(target_send, 'edge', split_axis=2, concat_axis=2,...]
    unnamed x2 -> x0, other arithmetic: 53.5 us -> none
    unnamed x66 -> x44, local copies, waits for them, and re-layouts: 68.4 us -> 20.5 us
    all_to_all x0 -> x3, blocking collectives: none -> 41.6 us  [exchange(): lax.all_to_all(array, axis, split_axis=0, concat_axis=0, tiled=True, axis...]
    pallas_call x0 -> x3, Pallas kernels: none -> 40.6 us  [the longest x1 26.9 us: local(): pl.pallas_call(holder_kernel, out_shape=(jax.ShapeDtypeStruct((devices, b...]
    dot_general x19 -> x0, matrix products: 40.2 us -> none  [the longest x1 10.7 us: edge_block(): lax.dot_general(cg_basis, coupled, (((0,), (0,)), ((), ())), preferred_el...]
    ppermute x2 -> x4, starting transfers between devices: 5.46 us -> 17.9 us  [the longest x1 6.65 us: local(): node_hi = lax.ppermute(nodes, 'edge', ring(devices, -1))]
  transfers between devices with their start and end apart: 4 -> 6, of which waited for: 2 -> 4; matrix products, arithmetic and copies ran while one was open for 12% -> 10% of each run, Pallas kernels for 0% -> 0%
where the time goes in v1:
time: 179 us; the launch traced here: 178 us
  blocking collectives  41.6 us (23%)
  Pallas kernels  40.6 us (23%)
  waiting for transfers between devices  31.9 us (18%)
  starting transfers between devices  31.3 us (17%)
  local copies, waits for them, and re-layouts  28.4 us (16%)
  other arithmetic  3.46 us (2%)
    all_to_all x3, blocking collectives, exchange(): lax.all_to_all(array, axis, split_axis=0, concat_axis=0, tiled=True, axis...  41.6 us
    pallas_call x1, Pallas kernels, local(): pl.pallas_call(holder_kernel, out_shape=(jax.ShapeDtypeStruct((devices, b...  26.9 us
    all_to_all x1, waiting for transfers between devices, local(): lax.all_to_all(back, 'edge', split_axis=0, concat_axis=0, tiled=True)  21.1 us
    unnamed x44, local copies, waits for them, and re-layouts  20.5 us
    all_to_all x1, waiting for transfers between devices, local(): lax.all_to_all(sent, 'edge', split_axis=0, concat_axis=0, tiled=True)  7.7 us
    pallas_call x1, Pallas kernels, local(): pl.pallas_call(finish_kernel, out_shape=(jax.ShapeDtypeStruct((4 * channe...  7.08 us
    all_to_all x1, starting transfers between devices, local(): lax.all_to_all(back, 'edge', split_axis=0, concat_axis=0, tiled=True)  7.05 us
    ppermute x1, starting transfers between devices, local(): node_hi = lax.ppermute(nodes, 'edge', ring(devices, -1))  6.65 us
  transfers between devices with their start and end apart: 6, of which 4 were waited for; matrix products, arithmetic and copies ran while one was open for 10% of the time, Pallas kernels for 0%

profile of v1, /device:TPU:1, one launch (start us, length us, event | category | flops | bytes accessed | tf_op | source)
XLA Modules:
  0.0 178.1 jit_solution(15541126931001428346)
XLA Ops:
  0.6 2.1 %collective-permute-start = (bf16[256,128]{1,0:T(8,128)(2,1)}, bf16[256,128]{1,0:T(8,128)(2,1)S(1)}, u32[]{:S(2)}, u32[]{:S(2)}) collective-permute-start(bf16[256,128]{1,0:T(8,128)(2,1)} %bitcast.23), channel_id=1, source_target_pairs={{0,1},{1,2},{2,3},{3,4},{4,5},{5,6},{6,7},{7,8},{8,9},{9,10},{10,1... | collective-permute-start | bytes 196616 | tf_op jit(solution)/shard_map/ppermute | solution.py:336
  2.8 6.7 %collective-permute-start.1 = (bf16[256,128]{1,0:T(8,128)(2,1)}, bf16[256,128]{1,0:T(8,128)(2,1)S(1)}, u32[]{:S(2)}, u32[]{:S(2)}) collective-permute-start(bf16[256,128]{1,0:T(8,128)(2,1)} %bitcast.24), channel_id=1, source_target_pairs={{0,31},{1,0},{2,1},{3,2},{4,3},{5,4},{6,5},{7,6},{8,7},{9,8},{10,9... | collective-permute-start | bytes 196616 | tf_op jit(solution)/shard_map/ppermute | solution.py:337
  9.4 0.9 copy.44
  10.3 0.9 copy.45
  11.1 0.9 copy.46
  12.0 0.9 copy.47
  12.9 0.0 collective-permute-done.node_lo
  12.9 0.0 collective-permute-done.1.node_hi
  12.9 0.0 copy-start
  12.9 1.0 copy-done
  14.0 0.0 copy-start.8
  14.0 0.8 copy-done.8
  14.7 0.0 copy-start.10
  14.7 0.8 copy-done.10
  15.6 0.0 copy-start.11
  15.6 0.7 copy-done.11
  16.3 0.7 copy-done.13
  17.0 0.7 copy-done.14
  17.7 6.6 %shard_map.207 = (bf16[32,112,128]{2,1,0:T(8,128)(2,1)}, s32[1,2048]{1,0:T(1,128)S(1)}, bf16[128,2048]{1,0:T(8,128)(2,1)S(1)}, bf16[128,2048]{1,0:T(8,128)(2,1)S...) custom-call(s32[1]{0:T(128)} %bitcast.pos_ref, s32[1,2048]{1,0:T(1,128)S(1)} %copy-done.13, ...), custom_call_target="tpu_custom_call" | custom-call | tf_op jit(solution)/shard_map/pallas_call | solution.py:352
  24.3 0.8 copy-done.2
  25.1 0.8 copy-done.4
  25.9 0.8 copy-done.6
  26.7 6.3 %all-to-all-start = ((bf16[32,112,128]{2,1,0:T(8,128)(2,1)}), bf16[32,112,128]{2,1,0:T(8,128)(2,1)}, u32[]{:S(2)}, u32[]{:S(2)}) async-start(bf16[32,112,128]{2,1,0:T(8,128)(2,1)} %get-tuple-element.18), calls=%async_computation | async-start | bytes 1835008 | tf_op jit(solution)/shard_map/all_to_all | solution.py:416
  33.1 1.7 copy.50
  34.7 1.5 copy.54
  36.2 1.1 copy.48
  37.3 0.0 copy-start.17
  37.3 1.7 copy.49
  39.0 2.0 %fusion.3 = (bf16[128,1472]{1,0:T(8,128)(2,1)}, bf16[1472,128]{0,1:T(8,128)(2,1)}) fusion(bf16[729,128]{0,1:T(8,128)(2,1)} %copy.49, bf16[729,128]{0,1:T(8,128)(2,1)S(1)} %copy.48), kind=kLoop, calls=%fused_computation.13 | loop fusion | flops 1507328 | bytes 1126912 | tf_op jit(solution)/shard_map/transpose | solution.py:451
  41.0 1.9 %copy.52.wlr_ref = bf16[1472,128]{1,0:T(8,128)(2,1)} copy(bf16[1472,128]{0,1:T(8,128)(2,1)} %get-tuple-element.38) | data formatting | bytes 753664 | tf_op jit(solution)/shard_map/concatenate | solution.py:419
  42.9 0.0 copy-done.17
  42.9 0.1 multiply_convert_fusion
  43.0 0.1 mul.26
  43.2 0.2 copy.51
  43.3 2.4 %pad.18.clone.cg_ref = bf16[736,736]{1,0:T(8,128)(2,1)} pad(bf16[729,729]{1,0:T(8,128)(2,1)} %copy.54, bf16[]{:T(256)} %constant.25.clone.1), padding=0_7x0_7 | pad | bytes 2146276 | tf_op jit(solution)/shard_map/jit(_pad)/pad | solution.py:420
  45.7 0.7 pad.19.pairs_ref
  46.4 1.1 pad_bitcast_fusion.cg_t
  47.5 7.7 %all-to-all-done.recv_ref = bf16[32,112,128]{2,1,0:T(8,128)(2,1)} async-done(((bf16[32,112,128]{2,1,0:T(8,128)(2,1)}), bf16[32,112,128]{2,1,0:T(8,128)(2,1)}, u32[]{:S(2)}, u32[]{:S(2)}) %all-to-all-start) | async-done | bytes 917536 | tf_op jit(solution)/shard_map/all_to_all | solution.py:416
  55.2 26.9 %shard_map.208 = (bf16[32,112,128]{2,1,0:T(8,128)(2,1)}, f32[1472,128]{1,0:T(8,128)}) custom-call(bf16[32,112,128]{2,1,0:T(8,128)(2,1)} %all-to-all-done.recv_ref, bf16[1,729,3072]{2,1,0:T(8,128)(2,1)} %target_ref.1, bf16[1472,128]{1,0:T(8,128)(2,1)} %copy.52.wlr_ref, bf16[128,1472]{1,0:T(8,128)(2,1)} %get-tuple-element.37.wlr_t, ...), custom_call_target="tpu_custom_call" | custom-call | tf_op jit(solution)/shard_map/pallas_call | solution.py:428
  82.1 0.0 copy-start.12
  82.1 7.1 %all-to-all-start.1 = ((bf16[32,112,128]{2,1,0:T(8,128)(2,1)}), bf16[32,112,128]{2,1,0:T(8,128)(2,1)S(1)}, u32[]{:S(2)}, u32[]{:S(2)}) async-start(bf16[32,112,128]{2,1,0:T(8,128)(2,1)} %get-tuple-element.19), calls=%async_computation.1 | async-start | bytes 1835008 | tf_op jit(solution)/shard_map/all_to_all | solution.py:453
  89.2 0.7 pad.24.clone
  89.9 21.1 %all-to-all-done.1.back_ref = bf16[32,112,128]{2,1,0:T(8,128)(2,1)S(1)} async-done(((bf16[32,112,128]{2,1,0:T(8,128)(2,1)}), bf16[32,112,128]{2,1,0:T(8,128)(2,1)S(1)}, u32[]{:S(2)}, u32[]{:S(2)}) %all-to-all-start.1) | async-done | bytes 917536 | tf_op jit(solution)/shard_map/all_to_all | solution.py:453
  111.0 0.0 copy-done.1
  111.0 0.0 copy-done.12
  111.0 1.0 copy-done.3
  112.1 1.0 copy-done.5
  113.1 1.0 copy-done.7
  114.1 0.8 copy-done.9
  114.9 7.1 %shard_map.209 = (f32[512,128]{1,0:T(8,128)S(1)}, f32[1,2048]{1,0:T(1,128)}) custom-call(bf16[32,112,128]{2,1,0:T(8,128)(2,1)S(1)} %all-to-all-done.1.back_ref, s32[1,2048]{1,0:T(1,128)S(1)} %bitcast.27, s32[1,2048]{1,0:T(1,128)S(1)} %get-tuple-element.20.rank_ref, bf16[128,2048]{1,0:T(8,128)(2,1)S(1)} %copy-done.3, bf16[128,2048]{1,0:T(8,128)(2,1)S(1)} %copy-done.5, ...), custom_call_target="tpu_custom_call" | custom-call | tf_op jit(solution)/shard_map/pallas_call | solution.py:455
  122.0 0.0 copy-done.15
  122.0 0.0 copy-done.16
  122.0 0.3 maximum_maximum_fusion
  122.4 5.1 %collective-permute-start.2 = (f32[1024,128]{1,0:T(8,128)S(1)}, f32[1024,128]{1,0:T(8,128)S(1)}, u32[]{:S(2)}, u32[]{:S(2)}) collective-permute-start(f32[1024,128]{1,0:T(8,128)S(1)} %constant_dynamic-slice_fusion), channel_id=1, source_target_pairs={{0,32},{32,0},{64,96},{96,64},{128,160},{160,128},{192,224},{224,1... | collective-permute-start | bytes 1572872 | tf_op jit(solution)/shard_map/ppermute | solution.py:289
  127.4 1.5 collective-permute-done.2
  129.0 0.1 dynamic-slice_add_fusion
  129.0 16.8 %all_to_all.34 = f32[16,64,128]{2,1,0:T(8,128)S(1)} all-to-all(f32[16,64,128]{2,1,0:T(8,128)S(1)} %bitcast.29), channel_id=1, replica_groups={{0,1,2,3,64,65,66,67,128,129,130,131,192,193,194,195},{4,5,6,7,68,69,70..., dimensions={0} | all-to-all | bytes 1048576 | tf_op jit(solution)/shard_map/all_to_all | solution.py:278
  145.8 11.9 %all_to_all.35 = f32[8,64,128]{2,1,0:T(8,128)S(1)} all-to-all(f32[8,64,128]{2,1,0:T(8,128)S(1)} %tile.4), channel_id=1, replica_groups={{0,4,8,12,16,20,24,28},{1,5,9,13,17,21,25,29},{2,6,10,14,18,22,26,30},{..., dimensions={0} | all-to-all | bytes 524288 | tf_op jit(solution)/shard_map/all_to_all | solution.py:278
  157.9 12.9 %all_to_all.36 = f32[16,64,128]{2,1,0:T(8,128)S(1)} all-to-all(f32[16,64,128]{2,1,0:T(8,128)S(1)} %tile.5), channel_id=1, replica_groups={{0,1,2,3,64,65,66,67,128,129,130,131,192,193,194,195},{4,5,6,7,68,69,70..., dimensions={0} | all-to-all | bytes 1048576 | tf_op jit(solution)/shard_map/all_to_all | solution.py:278
  170.7 4.1 %collective-permute-start.3 = (f32[1024,128]{1,0:T(8,128)S(1)}, f32[1024,128]{1,0:T(8,128)S(1)}, u32[]{:S(2)}, u32[]{:S(2)}) collective-permute-start(f32[1024,128]{1,0:T(8,128)S(1)} %bitcast.28), channel_id=1, source_target_pairs={{0,32},{32,0},{64,96},{96,64},{128,160},{160,128},{192,224},{224,1... | collective-permute-start | bytes 1572872 | tf_op jit(solution)/shard_map/ppermute | solution.py:303
  174.8 1.5 collective-permute-done.3
  176.4 0.1 broadcast_select_fusion
  176.5 0.7 fusion.5
  177.2 0.9 fusion.4
  (19 shorter events, 0.2 us)
Async XLA Ops:
  0.6 12.3 %collective-permute-start = (bf16[256,128]{1,0:T(8,128)(2,1)}, bf16[256,128]{1,0:T(8,128)(2,1)S(1)}, u32[]{:S(2)}, u32[]{:S(2)}) collective-permute-start(bf16[256,128]{1,0:T(8,128)(2,1)} %bitcast.23), channel_id=1, source_target_pairs={{0,1},{1,2},{2,3},{3,4},{4,5},{5,6},{6,7},{7,8},{8,9},{9,10},{10,1... | collective-permute-start | bytes 196616 | tf_op jit(solution)/shard_map/ppermute | solution.py:336
  2.8 10.2 %collective-permute-start.1 = (bf16[256,128]{1,0:T(8,128)(2,1)}, bf16[256,128]{1,0:T(8,128)(2,1)S(1)}, u32[]{:S(2)}, u32[]{:S(2)}) collective-permute-start(bf16[256,128]{1,0:T(8,128)(2,1)} %bitcast.24), channel_id=1, source_target_pairs={{0,31},{1,0},{2,1},{3,2},{4,3},{5,4},{6,5},{7,6},{8,7},{9,8},{10,9... | collective-permute-start | bytes 196616 | tf_op jit(solution)/shard_map/ppermute | solution.py:337
  12.9 1.0 copy-start
  14.0 0.8 copy-start.8
  14.7 0.8 copy-start.10
  15.6 0.7 copy-start.11
  16.3 0.7 copy-start.13
  17.0 0.7 copy-start.14
  24.3 0.8 copy-start.2
  25.1 0.8 copy-start.4
  25.9 0.8 copy-start.6
  26.7 28.5 %all-to-all-start = ((bf16[32,112,128]{2,1,0:T(8,128)(2,1)}), bf16[32,112,128]{2,1,0:T(8,128)(2,1)}, u32[]{:S(2)}, u32[]{:S(2)}) async-start(bf16[32,112,128]{2,1,0:T(8,128)(2,1)} %get-tuple-element.18), calls=%async_computation | async-start | bytes 1835008 | tf_op jit(solution)/shard_map/all_to_all | solution.py:416
  37.3 5.6 %copy-start.17 = (s32[3,27]{1,0:T(4,128)S(1)}, s32[3,27]{1,0:T(4,128)}, u32[]{:S(2)}) copy-start(s32[3,27]{1,0:T(4,128)} %param.21) | copy-start | bytes 976
  82.1 28.9 %copy-start.1 = (bf16[1,2048,128]{2,1,0:T(8,128)(2,1)S(1)}, bf16[1,2048,128]{2,1,0:T(8,128)(2,1)}, u32[]{:S(2)}) copy-start(bf16[1,2048,128]{2,1,0:T(8,128)(2,1)} %param.17) | copy-start | bytes 1572868
  82.1 28.9 %copy-start.12 = (s32[1,2048,1]{1,2,0:T(1,128)S(1)}, s32[1,2048,1]{1,2,0:T(1,128)}, u32[]{:S(2)}) copy-start(s32[1,2048,1]{1,2,0:T(1,128)} %param.22) | copy-start | bytes 24580
  82.1 28.9 %all-to-all-start.1 = ((bf16[32,112,128]{2,1,0:T(8,128)(2,1)}), bf16[32,112,128]{2,1,0:T(8,128)(2,1)S(1)}, u32[]{:S(2)}, u32[]{:S(2)}) async-start(bf16[32,112,128]{2,1,0:T(8,128)(2,1)} %get-tuple-element.19), calls=%async_computation.1 | async-start | bytes 1835008 | tf_op jit(solution)/shard_map/all_to_all | solution.py:453
  111.0 1.0 copy-start.3
  112.0 1.0 copy-start.5
  113.1 1.0 copy-start.7
  114.1 0.8 copy-start.9
  114.9 7.1 %copy-start.15 = (f32[1472,128]{1,0:T(8,128)S(1)}, f32[1472,128]{1,0:T(8,128)}, u32[]{:S(2)}) copy-start(f32[1472,128]{1,0:T(8,128)} %get-tuple-element.27) | copy-start | bytes 2260996
  114.9 7.1 %copy-start.16 = (f32[2048]{0:T(1024)S(1)}, f32[2048]{0:T(1024)}, u32[]{:S(2)}) copy-start(f32[2048]{0:T(1024)} %pad.24.clone) | copy-start | bytes 24580
  122.4 6.6 %collective-permute-start.2 = (f32[1024,128]{1,0:T(8,128)S(1)}, f32[1024,128]{1,0:T(8,128)S(1)}, u32[]{:S(2)}, u32[]{:S(2)}) collective-permute-start(f32[1024,128]{1,0:T(8,128)S(1)} %constant_dynamic-slice_fusion), channel_id=1, source_target_pairs={{0,32},{32,0},{64,96},{96,64},{128,160},{160,128},{192,224},{224,1... | collective-permute-start | bytes 1572872 | tf_op jit(solution)/shard_map/ppermute | solution.py:289
  170.7 5.6 %collective-permute-start.3 = (f32[1024,128]{1,0:T(8,128)S(1)}, f32[1024,128]{1,0:T(8,128)S(1)}, u32[]{:S(2)}, u32[]{:S(2)}) collective-permute-start(f32[1024,128]{1,0:T(8,128)S(1)} %bitcast.28), channel_id=1, source_target_pairs={{0,32},{32,0},{64,96},{96,64},{128,160},{160,128},{192,224},{224,1... | collective-permute-start | bytes 1572872 | tf_op jit(solution)/shard_map/ppermute | solution.py:303

commit v2 on v1

v2 whole, which is shorter than its diff:
```python
import functools

import jax
import jax.numpy as jnp
import numpy as np
from jax import lax
from jax.experimental import pallas as pl
from jax.experimental.pallas import tpu as pltpu
from jax.sharding import PartitionSpec as P

F32 = jnp.float32
BF16 = jnp.bfloat16
GROUP = 16
TAIL = 16
LANES = 128
CHUNK = 256
VMEM = 60 << 20


def ring(count, shift):
    return [(i, (i + shift) % count) for i in range(count)]


def matmul(a, b):
    return jnp.dot(a, b, preferred_element_type=F32)


def matmul_nt(a, b):
    return lax.dot_general(a, b, (((1,), (1,)), ((), ())), preferred_element_type=F32)


def matmul_tn(a, b):
    return lax.dot_general(a, b, (((0,), (0,)), ((), ())), preferred_element_type=F32)


def indicator(condition):
    return jnp.where(condition, 1.0, 0.0).astype(BF16)


def slope(value, sigma):
    return sigma * (1.0 + value * (1.0 - sigma))


def slot_onehot(out, holder, rank, base, capacity):
    edges = holder.shape[1]
    place = lax.broadcasted_iota(jnp.int32, (capacity, edges), 0)
    for p in range(GROUP):
        mine = jnp.where(holder == base + p, rank, -1)
        out[p * capacity : (p + 1) * capacity, :] = indicator(place == mine)


def edge_kernel(
    pos_ref,
    dst_ref,
    src_ref,
    holder_ref,
    spec_lo,
    spec_mid,
    spec_hi,
    node_lo,
    node_mid,
    node_hi,
    attr_ref,
    w_dst,
    w_src,
    w_attr,
    w_mix,
    out_ref,
    rank_ref,
    xdst_ref,
    xsrc_ref,
    first_ref,
    pre_ref,
    mixpre_ref,
    second_ref,
    onehot,
    tags,
):
    step = pl.program_id(0)
    edges = dst_ref.shape[1]
    devices = tags.shape[0] // 2
    capacity = out_ref.shape[1] - TAIL
    atoms = node_mid.shape[0]
    holder = holder_ref[...]

    @pl.when(step == 0)
    def _():
        offset = pos_ref[0] * atoms
        same = lax.broadcasted_iota(jnp.int32, (devices, edges), 0) == holder
        named = jnp.where(same, 1.0, 0.0)
        named_bf = named.astype(BF16)
        rows = lax.broadcasted_iota(jnp.int32, (CHUNK, CHUNK), 0)
        cols = lax.broadcasted_iota(jnp.int32, (CHUNK, CHUNK), 1)
        earlier = indicator(rows < cols)
        carry = jnp.zeros((devices, 1), F32)
        for c in range(edges // CHUNK):
            part = slice(c * CHUNK, (c + 1) * CHUNK)
            before = matmul(named_bf[:, part], earlier) + carry
            carry = carry + jnp.sum(named[:, part], axis=1, keepdims=True)
            rank_ref[:, part] = jnp.sum(
                before * named[:, part], axis=0, keepdims=True
            ).astype(jnp.int32)
        rank = rank_ref[...]

        def table_of(nodes, spec):
            kinds = jnp.broadcast_to((spec[...] + 1).astype(F32), (TAIL, atoms)).astype(BF16)
            return jnp.concatenate([nodes[...].T, kinds], axis=0)

        table_mid = table_of(node_mid, spec_mid)
        table = jnp.concatenate(
            [table_of(node_lo, spec_lo), table_mid, table_of(node_hi, spec_hi)], axis=1
        )
        channels = node_mid.shape[1]
        ids = lax.broadcasted_iota(jnp.int32, (atoms, edges), 0)
        from_dst = matmul(table_mid, indicator(ids == dst_ref[...] - offset))
        ids = lax.broadcasted_iota(jnp.int32, (3 * atoms, edges), 0)
        from_src = matmul(table, indicator(ids == src_ref[...] - (offset - atoms)))
        xdst = from_dst[:channels].astype(BF16)
        xsrc = from_src[:channels].astype(BF16)
        xdst_ref[...] = xdst
        xsrc_ref[...] = xsrc
        pre = matmul(w_dst[...].T, xdst) + matmul(w_src[...].T, xsrc)
        pre = pre + matmul_nt(w_attr[...].T, attr_ref[...])
        pre_ref[...] = pre
        first = (pre * jax.nn.sigmoid(pre)).astype(BF16)
        first_ref[...] = first
        mixpre = matmul(w_mix[...].T, first)
        mixpre_ref[...] = mixpre
        second_ref[...] = (first.astype(F32) + mixpre * jax.nn.sigmoid(mixpre)).astype(BF16)
        tagged = jnp.concatenate(
            [named * from_dst[channels : channels + 1], named * from_src[channels : channels + 1]],
            axis=0,
        ).astype(BF16)
        at_rank = indicator(lax.broadcasted_iota(jnp.int32, (LANES, edges), 0) == rank)
        tags[...] = matmul_nt(tagged, at_rank)

    slot_onehot(onehot, holder, rank_ref[...], step * GROUP, capacity)
    moved = matmul_nt(onehot[...], second_ref[...]).astype(BF16)
    line = lax.broadcasted_iota(jnp.int32, (TAIL, LANES), 0)
    for p in range(GROUP):
        out_ref[p, :capacity, :] = moved[p * capacity : (p + 1) * capacity]
        tag_dst = tags[pl.ds(step * GROUP + p, 1), :]
        tag_src = tags[pl.ds(devices + step * GROUP + p, 1), :]
        tail = jnp.where(line == 0, tag_dst, jnp.where(line == 1, tag_src, 0.0))
        out_ref[p, capacity:, :] = tail.astype(BF16)


def later_kernel(holder_ref, rank_ref, second_ref, out_ref, onehot):
    capacity = out_ref.shape[1]
    base = pl.program_id(0) * GROUP
    slot_onehot(onehot, holder_ref[...], rank_ref[...] - capacity, base, capacity)
    moved = matmul_nt(onehot[...], second_ref[...]).astype(BF16)
    for p in range(GROUP):
        out_ref[p] = moved[p * capacity : (p + 1) * capacity]


def prepare_kernel(
    target_ref,
    moves_ref,
    cg_ref,
    wleft_ref,
    wright_ref,
    mask_ref,
    pick_a,
    pick_b,
    pick_dst,
    pick_src,
    early_ref,
    later_ref,
    cg_out,
    cg_t,
    wlr_out,
    pairs_ref,
):
    rows = early_ref.shape[0]
    half = early_ref.shape[1]
    orb2 = target_ref.shape[1]
    width = 2 * half

    def pad_rows(array):
        empty = jnp.zeros((rows - orb2, array.shape[1]), array.dtype)
        return jnp.concatenate([array, empty], axis=0)

    moves = indicator(lax.broadcasted_iota(jnp.int32, (width, width), 0) == moves_ref[...])
    moved = pad_rows(matmul(target_ref[0], moves)).astype(BF16)
    early_ref[...] = moved[:, :half]
    later_ref[...] = moved[:, half:]

    @pl.when(pl.program_id(0) == 0)
    def _():
        tall = pad_rows(cg_ref[...].astype(F32))
        across = jnp.concatenate([tall, jnp.zeros((rows, rows - orb2), F32)], axis=1)
        cg_out[...] = across.astype(BF16)
        cg_t[...] = across.T.astype(BF16)
        left = pad_rows(wleft_ref[...].astype(F32))
        right = pad_rows(wright_ref[...].astype(F32))
        both = jnp.concatenate([left, right], axis=0)
        wlr_out[...] = both.astype(BF16)
        carried = mask_ref[...].astype(F32).astype(BF16)
        dst = matmul_tn(carried, pick_dst[...]).astype(BF16)
        src = matmul_tn(carried, pick_src[...]).astype(BF16)
        pairs_ref[...] = (matmul(pick_a[...], dst) * matmul(pick_b[...], src)).astype(BF16)


def holder_kernel(
    last,
    orb2,
    rows_ref,
    tails_ref,
    target_ref,
    wlr_ref,
    cg_ref,
    cg_t,
    pairs_ref,
    place_ref,
    *refs,
):
    if last:
        err_ref, before_ref, back_ref, grad_ref, dlr = refs
    else:
        back_ref, grad_ref, err_ref, dlr = refs
    step = pl.program_id(0)
    capacity = tails_ref.shape[1] - TAIL
    width = GROUP * capacity
    channels = rows_ref.shape[2]
    rows = cg_ref.shape[0]
    kinds = 3
    second = rows_ref[:, :capacity, :].reshape(width, channels)
    line = lax.broadcasted_iota(jnp.int32, (GROUP * TAIL, width), 0)
    start = place_ref[0:1, :]
    lane = lax.broadcasted_iota(jnp.int32, (LANES, width), 0)
    spread = indicator(lane == place_ref[1:2, :] + (capacity if last else 0))
    tails = tails_ref[:, capacity:, :].reshape(GROUP * TAIL, LANES)
    tags = matmul(tails, spread)
    tag_dst = jnp.sum(jnp.where(line == start, tags, 0.0), axis=0, keepdims=True)
    tag_src = jnp.sum(jnp.where(line == start + 1, tags, 0.0), axis=0, keepdims=True)
    code = jnp.where(tag_dst > 0.5, (tag_dst - 1.0) * kinds + (tag_src - 1.0), -1.0)
    code = code.astype(jnp.int32)
    pair_line = lax.broadcasted_iota(jnp.int32, (pairs_ref.shape[1], width), 0)
    pair = indicator(pair_line == code)
    both = matmul_nt(wlr_ref[...], second)
    left = both[:rows]
    right = both[rows:]
    predicted = matmul(cg_t[...], (left * right).astype(BF16))
    mask = matmul(pairs_ref[...], pair)
    resid = mask * (predicted - target_ref[...].astype(F32))
    error = jnp.sum(resid * resid, axis=0, keepdims=True) / orb2
    dpred = (resid * (1.0 / orb2)).astype(BF16)
    dcoupled = matmul(cg_ref[...], dpred)
    dlr[:rows] = (dcoupled * right).astype(BF16)
    dlr[rows:] = (dcoupled * left).astype(BF16)
    moved = matmul_tn(dlr[...], wlr_ref[...]).astype(BF16)
    for q in range(GROUP):
        back_ref[q, :capacity, :] = moved[q * capacity : (q + 1) * capacity]
    if last:

        def spell(values, spread):
            high = values.astype(BF16).astype(F32)
            middle = (values - high).astype(BF16).astype(F32)
            low = values - high - middle
            packed = jnp.where(line == start + 2, low, 0.0)
            packed = jnp.where(line == start + 1, middle, packed)
            packed = jnp.where(line == start, high, packed)
            return matmul_nt(packed.astype(BF16), spread)

        spelled = spell(err_ref[...], indicator(lane == place_ref[1:2, :]))
        spelled = (spelled + spell(error, spread)).astype(BF16)
        for q in range(GROUP):
            back_ref[q, capacity:, :] = spelled[q * TAIL : (q + 1) * TAIL]
    else:
        err_ref[...] = error
    grad = matmul(dlr[...], second)

    @pl.when(step == 0)
    def _():
        grad_ref[...] = before_ref[...] + grad if last else grad

    @pl.when(step > 0)
    def _():
        grad_ref[...] += grad


def collect_kernel(back_ref, holder_ref, rank_ref, dsecond, onehot):
    step = pl.program_id(0)
    capacity = back_ref.shape[1]
    slot_onehot(onehot, holder_ref[...], rank_ref[...], step * GROUP, capacity)
    rows = back_ref[...].reshape(GROUP * capacity, back_ref.shape[2])
    found = matmul_tn(rows, onehot[...])

    @pl.when(step == 0)
    def _():
        dsecond[...] = found

    @pl.when(step > 0)
    def _():
        dsecond[...] += found


def finish_kernel(
    back_ref,
    before_ref,
    holder_ref,
    rank_ref,
    xdst_ref,
    xsrc_ref,
    attr_ref,
    first_ref,
    pre_ref,
    mixpre_ref,
    wmix,
    grad_ref,
    error_ref,
    onehot,
    dsecond,
    found,
):
    step = pl.program_id(0)
    capacity = back_ref.shape[1] - TAIL
    edges = holder_ref.shape[1]
    channels = back_ref.shape[2]
    holder = holder_ref[...]
    rank = rank_ref[...]

    @pl.when(step == 0)
    def _():
        dsecond[...] = before_ref[...]
        found[...] = jnp.zeros_like(found)

    slot_onehot(onehot, holder, rank - capacity, step * GROUP, capacity)
    rows = back_ref[:, :capacity, :].reshape(GROUP * capacity, channels)
    dsecond[...] += matmul_tn(rows, onehot[...])
    line = lax.broadcasted_iota(jnp.int32, (GROUP * TAIL, edges), 0)
    low = (holder - step * GROUP) * TAIL
    at_holder = indicator(jnp.logical_and(line >= low, line < low + TAIL))
    tails = back_ref[:, capacity:, :].reshape(GROUP * TAIL, LANES)
    found[...] += matmul_tn(tails, at_holder)

    @pl.when(step == pl.num_programs(0) - 1)
    def _():
        place = lax.broadcasted_iota(jnp.int32, found.shape, 0)
        error_ref[...] = jnp.sum(
            jnp.where(place == rank, found[...], 0.0), axis=0, keepdims=True
        )
        dsec = dsecond[...]
        mixpre = mixpre_ref[...]
        dmix = (dsec * slope(mixpre, jax.nn.sigmoid(mixpre))).astype(BF16)
        dfirst = dsec + matmul(wmix[...], dmix)
        pre = pre_ref[...]
        dpre = (dfirst * slope(pre, jax.nn.sigmoid(pre))).astype(BF16)
        grad_ref[0:channels] = matmul_nt(xdst_ref[...], dpre)
        grad_ref[channels : 2 * channels] = matmul_nt(xsrc_ref[...], dpre)
        grad_ref[2 * channels : 3 * channels] = matmul(dpre, attr_ref[...]).T
        grad_ref[3 * channels : 4 * channels] = matmul_nt(first_ref[...], dmix)


def exchange(array, axis, groups=None):
    return lax.all_to_all(
        array, axis, split_axis=0, concat_axis=0, tiled=True, axis_index_groups=groups
    )


WIDE, NARROW, DEEP = 4, 4, 8
PEERS = WIDE * NARROW
SWAP = [(i, i ^ 1) for i in range(WIDE * 2)]
PLANE = [
    [(y * 2 + c) * NARROW * DEEP + z * NARROW + x for y in range(WIDE) for x in range(NARROW)]
    for c in range(2)
    for z in range(DEEP)
]
COLUMN = [[z * NARROW + x for z in range(DEEP)] for x in range(NARROW)]


def sum_planes(part, core):
    half = part.shape[0] // 2
    keep = lax.dynamic_slice_in_dim(part, core * half, half, 0)
    give = lax.dynamic_slice_in_dim(part, (1 - core) * half, half, 0)
    part = keep + lax.ppermute(give, "rep", SWAP)
    got = exchange(part, ("rep", "edge"), PLANE)
    return jnp.sum(got.reshape(PEERS, half // PEERS, -1), axis=0)


def sum_columns(part, core):
    got = exchange(jnp.tile(part, (DEEP, 1)), "edge", COLUMN)
    part = jnp.sum(got.reshape(DEEP, *part.shape), axis=0)
    part = exchange(jnp.tile(part, (PEERS, 1)), ("rep", "edge"), PLANE)
    other = lax.ppermute(part, "rep", SWAP)
    low = jnp.where(core == 0, part, other)
    high = jnp.where(core == 0, other, part)
    return low, high


def local(
    node_feats,
    edge_attr,
    edge_src,
    edge_dst,
    species,
    orbital_mask,
    tile_owner,
    target_send,
    w_dst,
    w_src,
    w_attr,
    w_mix,
    w_left,
    w_right,
    cg_basis,
):
    atoms, channels = node_feats.shape[1:]
    edges = edge_attr.shape[1]
    orb2, columns = target_send.shape[1:]
    devices = lax.axis_size("edge")
    capacity = columns // devices // 2
    steps = devices // GROUP
    width = GROUP * capacity
    position = lax.axis_index("edge")
    core = lax.rem(lax.axis_index("rep"), 2)
    rows = -(-orb2 // 32) * 32
    nodes = node_feats[0]
    node_lo = lax.ppermute(nodes, "edge", ring(devices, 1))
    node_hi = lax.ppermute(nodes, "edge", ring(devices, -1))
    holder = tile_owner.reshape(1, edges)
    attr = edge_attr[0]
    params = pltpu.CompilerParams(vmem_limit_bytes=VMEM)

    def whole(shape):
        return pl.BlockSpec(shape, lambda *_: (0,) * len(shape))

    def kinds_of(shift):
        return pl.BlockSpec(
            (1, atoms), lambda i, pos: (0, jnp.clip(pos[0] + shift, 0, devices - 1))
        )

    def blocks(length):
        return pl.BlockSpec((GROUP, length, channels), lambda i, *_: (i, 0, 0))

    def packets(length):
        return jax.ShapeDtypeStruct((devices, length, channels), BF16)

    def array(shape, dtype=BF16):
        return jax.ShapeDtypeStruct(shape, dtype)

    square = whole((channels, channels))
    line = whole((1, edges))
    wide = whole((channels, edges))
    onehot = pltpu.VMEM((width, edges), BF16)
    early, rank, xdst, xsrc, first, pre, mixpre, second = pl.pallas_call(
        edge_kernel,
        out_shape=(
            packets(capacity + TAIL),
            array((1, edges), jnp.int32),
            array((channels, edges)),
            array((channels, edges)),
            array((channels, edges)),
            array((channels, edges), F32),
            array((channels, edges), F32),
            array((channels, edges)),
        ),
        grid_spec=pltpu.PrefetchScalarGridSpec(
            num_scalar_prefetch=1,
            grid=(steps,),
            in_specs=[line, line, line, kinds_of(-1), kinds_of(0), kinds_of(1)]
            + [whole((atoms, channels))] * 3
            + [whole((edges, channels))]
            + [square] * 4,
            out_specs=[blocks(capacity + TAIL), line] + [wide] * 6,
            scratch_shapes=[onehot, pltpu.VMEM((2 * devices, LANES), F32)],
        ),
        compiler_params=params,
    )(
        position.astype(jnp.int32)[None],
        edge_dst,
        edge_src,
        holder,
        species,
        species,
        species,
        node_lo,
        nodes,
        node_hi,
        attr,
        w_dst,
        w_src,
        w_attr,
        w_mix,
    )
    got_early = exchange(early, "edge")
    later = pl.pallas_call(
        later_kernel,
        out_shape=packets(capacity),
        grid=(steps,),
        in_specs=[line, line, wide],
        out_specs=blocks(capacity),
        scratch_shapes=[onehot],
        compiler_params=params,
    )(holder, rank, second)

    slots = np.arange(width)
    places = np.stack([slots // capacity * TAIL, slots % capacity]).astype(np.int32)
    q, k = slots % (width // 2) // capacity, slots % capacity
    moves = (q * 2 * capacity + k + slots // (width // 2) * capacity)[None].astype(np.int32)
    species_count, orbs = orbital_mask.shape
    entry = np.arange(rows)[:, None]
    orbit = np.arange(orbs)[None, :]
    valid = entry < orb2
    pick_a = (valid & (entry // orbs == orbit)).astype(BF16)
    pick_b = (valid & (entry % orbs == orbit)).astype(BF16)
    code = np.arange(TAIL)[None, :]
    kind = np.arange(species_count)[:, None]
    known = code < species_count**2
    pick_dst = (known & (code // species_count == kind)).astype(BF16)
    pick_src = (known & (code % species_count == kind)).astype(BF16)
    halves = pl.BlockSpec((rows, width // 2), lambda i: (0, i))
    prepared = [
        array((rows, columns // 2)),
        array((rows, columns // 2)),
        array((rows, rows)),
        array((rows, rows)),
        array((2 * rows, channels)),
        array((rows, TAIL)),
    ]
    goal_early, goal_later, cg, cg_t, wlr, pairs = pl.pallas_call(
        prepare_kernel,
        out_shape=prepared,
        grid=(columns // width,),
        in_specs=[pl.BlockSpec((1, orb2, width), lambda i: (0, 0, i)), whole((1, width))]
        + [whole(a.shape) for a in (cg_basis, w_left, w_right, orbital_mask)]
        + [whole(a.shape) for a in (pick_a, pick_b, pick_dst, pick_src)],
        out_specs=[halves, halves] + [whole(a.shape) for a in prepared[2:]],
        compiler_params=params,
    )(
        target_send,
        moves,
        cg_basis,
        w_left,
        w_right,
        orbital_mask,
        pick_a,
        pick_b,
        pick_dst,
        pick_src,
    )

    later, goal_early = lax.optimization_barrier((later, goal_early))
    got_later = exchange(later, "edge")
    shared = (wlr, cg, cg_t, pairs, places)
    grad_shape = array((2 * rows, channels), F32)
    error_line = pl.BlockSpec((1, width), lambda i: (0, i))
    holder_specs = [
        pl.BlockSpec((rows, width), lambda i: (0, i)),
        *[whole(a.shape) for a in shared],
    ]
    dlr = pltpu.VMEM((2 * rows, width), BF16)
    back_early, grad_early, error_early = pl.pallas_call(
        functools.partial(holder_kernel, False, orb2),
        out_shape=(packets(capacity), grad_shape, array((1, devices * capacity), F32)),
        grid=(steps,),
        in_specs=[blocks(capacity + TAIL), blocks(capacity + TAIL), *holder_specs],
        out_specs=[blocks(capacity), whole(grad_shape.shape), error_line],
        scratch_shapes=[dlr],
        compiler_params=params,
    )(got_early, got_early, goal_early, *shared)
    returned_early = exchange(back_early, "edge")
    back_later, grad_wide = pl.pallas_call(
        functools.partial(holder_kernel, True, orb2),
        out_shape=(packets(capacity + TAIL), grad_shape),
        grid=(steps,),
        in_specs=[
            blocks(capacity),
            blocks(capacity + TAIL),
            *holder_specs,
            error_line,
            whole(grad_shape.shape),
        ],
        out_specs=[blocks(capacity + TAIL), whole(grad_shape.shape)],
        scratch_shapes=[dlr],
        compiler_params=params,
    )(got_later, got_early, goal_later, *shared, error_early, grad_early)
    returned_later = exchange(back_later, "edge")

    dsecond = pl.pallas_call(
        collect_kernel,
        out_shape=array((channels, edges), F32),
        grid=(steps,),
        in_specs=[blocks(capacity), line, line],
        out_specs=wide,
        scratch_shapes=[onehot],
        compiler_params=params,
    )(returned_early, holder, rank)
    grad_small, errors = pl.pallas_call(
        finish_kernel,
        out_shape=(array((4 * channels, channels), F32), array((1, edges), F32)),
        grid=(steps,),
        in_specs=[blocks(capacity + TAIL), wide, line, line, wide, wide]
        + [whole((edges, channels)), wide, wide, wide, square],
        out_specs=[whole((4 * channels, channels)), line],
        scratch_shapes=[
            onehot,
            pltpu.VMEM((channels, edges), F32),
            pltpu.VMEM((LANES, edges), F32),
        ],
        compiler_params=params,
    )(returned_later, dsecond, holder, rank, xdst, xsrc, attr, first, pre, mixpre, w_mix)

    unit = 2 * PEERS * 8
    full = -(-2 * rows // unit) * unit
    grad_wide = jnp.pad(grad_wide, ((0, full - 2 * rows), (0, 0)))
    part_wide = sum_planes(grad_wide, core)
    part_small = sum_planes(grad_small, core)
    split = part_wide.shape[0]
    parts = sum_columns(jnp.concatenate([part_wide, part_small], axis=0), core)
    parts = [p.reshape(PEERS, -1, channels) for p in parts]
    wide_sum = jnp.concatenate([p[:, :split].reshape(-1, channels) for p in parts], axis=0)
    small_sum = jnp.concatenate([p[:, split:].reshape(-1, channels) for p in parts], axis=0)
    outs = [small_sum[i * channels : (i + 1) * channels] for i in range(4)]
    outs += [wide_sum[i * rows :][:orb2] for i in range(2)]
    return (*outs, errors)


def solution(mesh):
    return jax.shard_map(
        local,
        mesh=mesh,
        in_specs=(
            P("rep", "edge", None),
            P("rep", "edge", None),
            P("rep", "edge"),
            P("rep", "edge"),
            P("rep", None),
            P(),
            P("rep", "edge", None),
            P("rep", "edge", None),
            P(),
            P(),
            P(),
            P(),
            P(),
            P(),
            P(),
        ),
        out_specs=(P(), P(), P(), P(), P(), P(), P("rep", "edge")),
        check_vma=False,
    )
```

time: 179 us -> 177 us (0.989)
  starting transfers between devices: 31.3 us -> 70.7 us
  local copies, waits for them, and re-layouts: 28.4 us -> 4.04 us
  blocking collectives: 41.6 us -> 24.7 us
  Pallas kernels: 40.6 us -> 57.1 us
  waiting for transfers between devices: 31.9 us -> 15.5 us
    all_to_all x2 -> x6, starting transfers between devices: 13.4 us -> 47.9 us  [exchange(): lax.all_to_all(array, axis, split_axis=0, concat_axis=0, tiled=True, axis...]
    unnamed x44 -> x14, local copies, waits for them, and re-layouts: 20.5 us -> 0.67 us
    all_to_all x2 -> x6, waiting for transfers between devices: 28.8 us -> 9.85 us  [exchange(): lax.all_to_all(array, axis, split_axis=0, concat_axis=0, tiled=True, axis...]
    all_to_all x3 -> x2, blocking collectives: 41.6 us -> 24.7 us  [exchange(): lax.all_to_all(array, axis, split_axis=0, concat_axis=0, tiled=True, axis...]
    pallas_call x3 -> x7, Pallas kernels: 40.6 us -> 57.1 us  [the longest x1 14 us: local(): pl.pallas_call(functools.partial(holder_kernel, True, orb2), out_shape=(p...]
    ppermute x2 -> x3, starting transfers between devices: 9.17 us -> 14.1 us  [the longest x2 9.98 us: sum_planes(): part = keep + lax.ppermute(give, 'rep', SWAP)]
    pad x2 -> x0, local copies, waits for them, and re-layouts: 3.09 us -> none  [the longest x1 2.38 us: local(): cg = jnp.pad(cg_basis, ((0, rows - orb2), (0, rows - orb2)))]
    concatenate x2 -> x0, local copies, waits for them, and re-layouts: 2.6 us -> none  [the longest x1 1.92 us: local(): wlr = jnp.concatenate([jnp.pad(w_left, pad), jnp.pad(w_right, pad)], axis=0)]
  transfers between devices with their start and end apart: 6 -> 11, of which waited for: 4 -> 7; matrix products, arithmetic and copies ran while one was open for 10% -> 2% of each run, Pallas kernels for 0% -> 29%
where the time goes in v2:
time: 177 us; the launch traced here: 176 us
  starting transfers between devices  70.7 us (40%)
  Pallas kernels  57.1 us (32%)
  blocking collectives  24.7 us (14%)
  waiting for transfers between devices  15.5 us (9%)
  local copies, waits for them, and re-layouts  4.04 us (2%)
  other arithmetic  3.44 us (2%)
    all_to_all x6, starting transfers between devices, exchange(): lax.all_to_all(array, axis, split_axis=0, concat_axis=0, tiled=True, axis...  47.9 us
    all_to_all x2, blocking collectives, exchange(): lax.all_to_all(array, axis, split_axis=0, concat_axis=0, tiled=True, axis...  24.7 us
    pallas_call x1, Pallas kernels, local(): pl.pallas_call(functools.partial(holder_kernel, True, orb2), out_shape=(p...  14 us
    pallas_call x1, Pallas kernels, local(): pl.pallas_call(functools.partial(holder_kernel, False, orb2), out_shape=(...  12 us
    ppermute x2, starting transfers between devices, sum_planes(): part = keep + lax.ppermute(give, 'rep', SWAP)  9.98 us
    all_to_all x6, waiting for transfers between devices, exchange(): lax.all_to_all(array, axis, split_axis=0, concat_axis=0, tiled=True, axis...  9.85 us
    pallas_call x1, Pallas kernels, local(): pl.pallas_call(prepare_kernel, out_shape=prepared, grid=(columns // width...  9.41 us
    pallas_call x1, Pallas kernels, local(): pl.pallas_call(finish_kernel, out_shape=(array((4 * channels, channels),...  7.91 us
  transfers between devices with their start and end apart: 11, of which 7 were waited for; matrix products, arithmetic and copies ran while one was open for 2% of the time, Pallas kernels for 29%

profile of v2, /device:TPU:1, one launch (start us, length us, event | category | flops | bytes accessed | tf_op | source)
XLA Modules:
  0.0 176.3 jit_solution(18017429825923243489)
XLA Ops:
  0.6 2.1 %collective-permute-start = (bf16[256,128]{1,0:T(8,128)(2,1)}, bf16[256,128]{1,0:T(8,128)(2,1)S(1)}, u32[]{:S(2)}, u32[]{:S(2)}) collective-permute-start(bf16[256,128]{1,0:T(8,128)(2,1)} %bitcast.30), channel_id=1, source_target_pairs={{0,1},{1,2},{2,3},{3,4},{4,5},{5,6},{6,7},{7,8},{8,9},{9,10},{10,1... | collective-permute-start | bytes 196616 | tf_op jit(solution)/shard_map/ppermute | solution.py:420
  2.8 6.6 %collective-permute-start.1 = (bf16[256,128]{1,0:T(8,128)(2,1)}, bf16[256,128]{1,0:T(8,128)(2,1)S(1)}, u32[]{:S(2)}, u32[]{:S(2)}) collective-permute-start(bf16[256,128]{1,0:T(8,128)(2,1)} %bitcast.31), channel_id=1, source_target_pairs={{0,31},{1,0},{2,1},{3,2},{4,3},{5,4},{6,5},{7,6},{8,7},{9,8},{10,9... | collective-permute-start | bytes 196616 | tf_op jit(solution)/shard_map/ppermute | solution.py:421
  9.4 1.8 %collective-permute-done.node_lo = bf16[256,128]{1,0:T(8,128)(2,1)S(1)} collective-permute-done((bf16[256,128]{1,0:T(8,128)(2,1)}, bf16[256,128]{1,0:T(8,128)(2,1)S(1)}, u32[]{:S(2)}, u32[]{:S(2)}) %collective-permute-start) | collective-permute-done | bytes 65568 | tf_op jit(solution)/shard_map/ppermute | solution.py:420
  11.2 0.0 copy-start.5
  11.2 0.0 collective-permute-done.1.node_hi
  11.2 0.0 copy-start.6
  11.2 0.6 copy-done.5
  11.8 0.0 copy-done.6
  11.8 6.4 %shard_map.252 = (bf16[32,64,128]{2,1,0:T(8,128)(2,1)}, s32[1,2048]{1,0:T(1,128)}, bf16[128,2048]{1,0:T(8,128)(2,1)}, bf16[128,2048]{1,0:T(8,128)(2,1)}, bf16[12...) custom-call(s32[1]{0:T(128)} %bitcast.1.pos_ref, ...), custom_call_target="tpu_custom_call" | custom-call | tf_op jit(solution)/shard_map/pallas_call | solution.py:447
  18.2 7.9 %all-to-all-start.1 = ((bf16[32,64,128]{2,1,0:T(8,128)(2,1)}), bf16[32,64,128]{2,1,0:T(8,128)(2,1)S(1)}, u32[]{:S(2)}, u32[]{:S(2)}) async-start(bf16[32,64,128]{2,1,0:T(8,128)(2,1)} %get-tuple-element.34), calls=%async_computation.1 | async-start | bytes 1048576 | tf_op jit(solution)/shard_map/all_to_all | solution.py:357
  26.1 9.4 %shard_map.254 = (bf16[736,1536]{1,0:T(8,128)(2,1)}, bf16[736,1536]{1,0:T(8,128)(2,1)}, bf16[736,736]{1,0:T(8,128)(2,1)}, bf16[736,736]{1,0:T(8,128)(2,1)}, bf16...) custom-call(bf16[1,729,3072]{2,1,0:T(8,128)(2,1)} %target_ref.1, s32[1,768]{1,0:T(1,128)} %constant.39.clone.moves_ref, ...), custom_call_target="tpu_custom_call" | custom-call | tf_op jit(solution)/shard_map/pallas_call | solution.py:522
  35.5 3.8 %shard_map.253 = bf16[32,48,128]{2,1,0:T(8,128)(2,1)} custom-call(s32[1,2048]{1,0:T(1,128)} %bitcast.27, s32[1,2048]{1,0:T(1,128)} %get-tuple-element.30.rank_ref, bf16[128,2048]{1,0:T(8,128)(2,1)} %get-tuple-element.31.second_ref), custom_call_target="tpu_custom_call" | custom-call | tf_op jit(solution)/shard_map/pallas_call | solution.py:488
  39.3 1.4 all-to-all-done.1.rows_ref.tails_ref
  40.6 0.0 copy-start
  40.6 7.9 %all-to-all-start = ((bf16[32,48,128]{2,1,0:T(8,128)(2,1)}), bf16[32,48,128]{2,1,0:T(8,128)(2,1)S(1)}, u32[]{:S(2)}, u32[]{:S(2)}) async-start(bf16[32,48,128]{2,1,0:T(8,128)(2,1)} %shard_map.253), calls=%async_computation | async-start | bytes 786432 | tf_op jit(solution)/shard_map/all_to_all | solution.py:357
  48.5 0.0 copy-done
  48.5 12.0 %shard_map.255 = (bf16[32,48,128]{2,1,0:T(8,128)(2,1)}, f32[1472,128]{1,0:T(8,128)}, f32[1,1536]{1,0:T(1,128)}) custom-call(bf16[32,64,128]{2,1,0:T(8,128)(2,1)} %copy-done, bf16[32,64,128]{2,1,0:T(8,128)(2,1)} %copy-done, bf16[736,1536]{1,0:T(8,128)(2,1)} %get-tuple-element.40.target_ref, bf16[1472,128]{1,0:T(8,128)(2,1)} %get-tuple-element.36.wlr_ref, ...), custom_call_target="tpu_custom_call" | custom-call | tf_op jit(solution)/shard_map/pallas_call | solution.py:554
  60.5 0.0 all-to-all-done.rows_ref
  60.5 0.0 copy-start.3
  60.5 9.2 %all-to-all-start.4 = ((bf16[32,48,128]{2,1,0:T(8,128)(2,1)}), bf16[32,48,128]{2,1,0:T(8,128)(2,1)S(1)}, u32[]{:S(2)}, u32[]{:S(2)}) async-start(bf16[32,48,128]{2,1,0:T(8,128)(2,1)} %get-tuple-element.45), calls=%async_computation.4 | async-start | bytes 786432 | tf_op jit(solution)/shard_map/all_to_all | solution.py:357
  69.8 0.0 copy-done.3
  69.8 14.0 %shard_map.256 = (bf16[32,64,128]{2,1,0:T(8,128)(2,1)}, f32[1472,128]{1,0:T(8,128)}) custom-call(bf16[32,48,128]{2,1,0:T(8,128)(2,1)} %copy-done.3, bf16[32,64,128]{2,1,0:T(8,128)(2,1)} %copy-done, bf16[736,1536]{1,0:T(8,128)(2,1)} %get-tuple-element.35.target_ref, bf16[1472,128]{1,0:T(8,128)(2,1)} %get-tuple-element.36.wlr_ref, ...), custom_call_target="tpu_custom_call" | custom-call | tf_op jit(solution)/shard_map/pallas_call | solution.py:564
  83.7 0.0 copy-start.1
  83.7 0.0 all-to-all-done.4.back_ref
  83.8 0.0 copy-start.4
  83.8 9.4 %all-to-all-start.3 = ((bf16[32,64,128]{2,1,0:T(8,128)(2,1)}), bf16[32,64,128]{2,1,0:T(8,128)(2,1)S(1)}, u32[]{:S(2)}, u32[]{:S(2)}) async-start(bf16[32,64,128]{2,1,0:T(8,128)(2,1)} %get-tuple-element.44), calls=%async_computation.3 | async-start | bytes 1048576 | tf_op jit(solution)/shard_map/all_to_all | solution.py:357
  93.1 1.0 pad_dynamic-slice_fusion
  94.2 4.1 %collective-permute-start.2 = (f32[768,128]{1,0:T(8,128)S(1)}, f32[768,128]{1,0:T(8,128)S(1)}, u32[]{:S(2)}, u32[]{:S(2)}) collective-permute-start(f32[768,128]{1,0:T(8,128)S(1)} %pad_dynamic-slice_fusion), channel_id=1, source_target_pairs={{0,32},{32,0},{64,96},{96,64},{128,160},{160,128},{192,224},{224,1... | collective-permute-start | bytes 1179656 | tf_op jit(solution)/shard_map/ppermute | solution.py:377
  98.3 1.3 collective-permute-done.2
  99.7 0.0 copy-done.1
  99.7 0.8 fusion
  100.5 0.0 copy-done.4
  100.5 3.7 %shard_map.257.before_ref = f32[128,2048]{1,0:T(8,128)} custom-call(bf16[32,48,128]{2,1,0:T(8,128)(2,1)} %copy-done.4, s32[1,2048]{1,0:T(1,128)} %bitcast.28, s32[1,2048]{1,0:T(1,128)} %get-tuple-element.30.rank_ref), custom_call_target="tpu_custom_call" | custom-call | tf_op jit(solution)/shard_map/pallas_call | solution.py:581
  104.2 1.7 all-to-all-done.3.back_ref
  105.9 0.0 copy-start.2
  105.9 6.6 %all-to-all-start.2 = ((f32[16,48,128]{2,1,0:T(8,128)}), f32[16,48,128]{2,1,0:T(8,128)S(1)}, u32[]{:S(2)}, u32[]{:S(2)}) async-start(f32[16,48,128]{2,1,0:T(8,128)} %bitcast.4), calls=%async_computation.2 | async-start | bytes 786432 | tf_op jit(solution)/shard_map/all_to_all | solution.py:357
  112.5 0.0 copy-done.2
  112.5 7.9 %shard_map.258 = (f32[512,128]{1,0:T(8,128)}, f32[1,2048]{1,0:T(1,128)}) custom-call(bf16[32,64,128]{2,1,0:T(8,128)(2,1)} %copy-done.2, f32[128,2048]{1,0:T(8,128)} %shard_map.257.before_ref, s32[1,2048]{1,0:T(1,128)} %bitcast.29, s32[1,2048]{1,0:T(1,128)} %get-tuple-element.30.rank_ref, bf16[128,2048]{1,0:T(8,128)(2,1)} %get-tuple-element.46.xdst_ref, ...), custom_call_target="tpu_custom_call" | custom-call | tf_op jit(solution)/shard_map/pallas_call | solution.py:590
  120.4 0.9 constant_dynamic-slice_fusion
  121.3 5.9 %collective-permute-start.3 = (f32[256,128]{1,0:T(8,128)S(1)}, f32[256,128]{1,0:T(8,128)S(1)}, u32[]{:S(2)}, u32[]{:S(2)}) collective-permute-start(f32[256,128]{1,0:T(8,128)S(1)} %constant_dynamic-slice_fusion), channel_id=1, source_target_pairs={{0,32},{32,0},{64,96},{96,64},{128,160},{160,128},{192,224},{224,1... | collective-permute-start | bytes 393224 | tf_op jit(solution)/shard_map/ppermute | solution.py:377
  127.2 1.0 collective-permute-done.3
  128.1 1.6 dynamic-slice_add_fusion
  129.7 0.0 all-to-all-done.2
  129.7 6.9 %all-to-all-start.5 = ((f32[16,16,128]{2,1,0:T(8,128)}), f32[16,16,128]{2,1,0:T(8,128)S(1)}, u32[]{:S(2)}, u32[]{:S(2)}) async-start(f32[16,16,128]{2,1,0:T(8,128)} %bitcast.5), calls=%async_computation.5 | async-start | bytes 262144 | tf_op jit(solution)/shard_map/all_to_all | solution.py:357
  136.7 6.8 %all-to-all-done.5 = f32[16,16,128]{2,1,0:T(8,128)S(1)} async-done(((f32[16,16,128]{2,1,0:T(8,128)}), f32[16,16,128]{2,1,0:T(8,128)S(1)}, u32[]{:S(2)}, u32[]{:S(2)}) %all-to-all-start.5) | async-done | bytes 131104 | tf_op jit(solution)/shard_map/all_to_all | solution.py:357
  143.6 11.9 %all_to_all.53 = f32[8,64,128]{2,1,0:T(8,128)S(1)} all-to-all(f32[8,64,128]{2,1,0:T(8,128)S(1)} %tile.4), channel_id=1, replica_groups={{0,4,8,12,16,20,24,28},{1,5,9,13,17,21,25,29},{2,6,10,14,18,22,26,30},{..., dimensions={0} | all-to-all | bytes 524288 | tf_op jit(solution)/shard_map/all_to_all | solution.py:357
  155.6 12.7 %all_to_all.54 = f32[16,64,128]{2,1,0:T(8,128)S(1)} all-to-all(f32[16,64,128]{2,1,0:T(8,128)S(1)} %tile.5), channel_id=1, replica_groups={{0,1,2,3,64,65,66,67,128,129,130,131,192,193,194,195},{4,5,6,7,68,69,70..., dimensions={0} | all-to-all | bytes 1048576 | tf_op jit(solution)/shard_map/all_to_all | solution.py:357
  168.3 4.1 %collective-permute-start.4 = (f32[1024,128]{1,0:T(8,128)S(1)}, f32[1024,128]{1,0:T(8,128)S(1)}, u32[]{:S(2)}, u32[]{:S(2)}) collective-permute-start(f32[1024,128]{1,0:T(8,128)S(1)} %bitcast.18), channel_id=1, source_target_pairs={{0,32},{32,0},{64,96},{96,64},{128,160},{160,128},{192,224},{224,1... | collective-permute-start | bytes 1572872 | tf_op jit(solution)/shard_map/ppermute | solution.py:386
  172.4 1.5 collective-permute-done.4
  173.9 0.1 broadcast_select_fusion
  174.0 0.7 fusion.1
  174.7 0.7 fusion.2
  175.4 0.9 pad_maximum_fusion
  (8 shorter events, 0.2 us)
Async XLA Ops:
  0.6 10.5 %collective-permute-start = (bf16[256,128]{1,0:T(8,128)(2,1)}, bf16[256,128]{1,0:T(8,128)(2,1)S(1)}, u32[]{:S(2)}, u32[]{:S(2)}) collective-permute-start(bf16[256,128]{1,0:T(8,128)(2,1)} %bitcast.30), channel_id=1, source_target_pairs={{0,1},{1,2},{2,3},{3,4},{4,5},{5,6},{6,7},{7,8},{8,9},{9,10},{10,1... | collective-permute-start | bytes 196616 | tf_op jit(solution)/shard_map/ppermute | solution.py:420
  2.8 8.4 %collective-permute-start.1 = (bf16[256,128]{1,0:T(8,128)(2,1)}, bf16[256,128]{1,0:T(8,128)(2,1)S(1)}, u32[]{:S(2)}, u32[]{:S(2)}) collective-permute-start(bf16[256,128]{1,0:T(8,128)(2,1)} %bitcast.31), channel_id=1, source_target_pairs={{0,31},{1,0},{2,1},{3,2},{4,3},{5,4},{6,5},{7,6},{8,7},{9,8},{10,9... | collective-permute-start | bytes 196616 | tf_op jit(solution)/shard_map/ppermute | solution.py:421
  11.2 0.6 copy-start.5
  11.2 0.6 copy-start.6
  18.2 22.5 %all-to-all-start.1 = ((bf16[32,64,128]{2,1,0:T(8,128)(2,1)}), bf16[32,64,128]{2,1,0:T(8,128)(2,1)S(1)}, u32[]{:S(2)}, u32[]{:S(2)}) async-start(bf16[32,64,128]{2,1,0:T(8,128)(2,1)} %get-tuple-element.34), calls=%async_computation.1 | async-start | bytes 1048576 | tf_op jit(solution)/shard_map/all_to_all | solution.py:357
  40.6 7.9 %copy-start = (bf16[32,64,128]{2,1,0:T(8,128)(2,1)}, bf16[32,64,128]{2,1,0:T(8,128)(2,1)S(1)}, u32[]{:S(2)}) copy-start(bf16[32,64,128]{2,1,0:T(8,128)(2,1)S(1)} %all-to-all-done.1.rows_ref.tails_ref) | copy-start | bytes 1572868
  40.6 19.9 %all-to-all-start = ((bf16[32,48,128]{2,1,0:T(8,128)(2,1)}), bf16[32,48,128]{2,1,0:T(8,128)(2,1)S(1)}, u32[]{:S(2)}, u32[]{:S(2)}) async-start(bf16[32,48,128]{2,1,0:T(8,128)(2,1)} %shard_map.253), calls=%async_computation | async-start | bytes 786432 | tf_op jit(solution)/shard_map/all_to_all | solution.py:357
  60.5 9.2 %copy-start.3 = (bf16[32,48,128]{2,1,0:T(8,128)(2,1)}, bf16[32,48,128]{2,1,0:T(8,128)(2,1)S(1)}, u32[]{:S(2)}) copy-start(bf16[32,48,128]{2,1,0:T(8,128)(2,1)S(1)} %all-to-all-done.rows_ref) | copy-start | bytes 1179652
  60.5 23.2 %all-to-all-start.4 = ((bf16[32,48,128]{2,1,0:T(8,128)(2,1)}), bf16[32,48,128]{2,1,0:T(8,128)(2,1)S(1)}, u32[]{:S(2)}, u32[]{:S(2)}) async-start(bf16[32,48,128]{2,1,0:T(8,128)(2,1)} %get-tuple-element.45), calls=%async_computation.4 | async-start | bytes 786432 | tf_op jit(solution)/shard_map/all_to_all | solution.py:357
  83.7 15.9 %copy-start.1 = (f32[1472,128]{1,0:T(8,128)S(1)}, f32[1472,128]{1,0:T(8,128)}, u32[]{:S(2)}) copy-start(f32[1472,128]{1,0:T(8,128)} %get-tuple-element.43) | copy-start | bytes 2260996
  83.8 16.7 %copy-start.4 = (bf16[32,48,128]{2,1,0:T(8,128)(2,1)}, bf16[32,48,128]{2,1,0:T(8,128)(2,1)S(1)}, u32[]{:S(2)}) copy-start(bf16[32,48,128]{2,1,0:T(8,128)(2,1)S(1)} %all-to-all-done.4.back_ref) | copy-start | bytes 1179652
  83.8 22.1 %all-to-all-start.3 = ((bf16[32,64,128]{2,1,0:T(8,128)(2,1)}), bf16[32,64,128]{2,1,0:T(8,128)(2,1)S(1)}, u32[]{:S(2)}, u32[]{:S(2)}) async-start(bf16[32,64,128]{2,1,0:T(8,128)(2,1)} %get-tuple-element.44), calls=%async_computation.3 | async-start | bytes 1048576 | tf_op jit(solution)/shard_map/all_to_all | solution.py:357
  94.2 5.5 %collective-permute-start.2 = (f32[768,128]{1,0:T(8,128)S(1)}, f32[768,128]{1,0:T(8,128)S(1)}, u32[]{:S(2)}, u32[]{:S(2)}) collective-permute-start(f32[768,128]{1,0:T(8,128)S(1)} %pad_dynamic-slice_fusion), channel_id=1, source_target_pairs={{0,32},{32,0},{64,96},{96,64},{128,160},{160,128},{192,224},{224,1... | collective-permute-start | bytes 1179656 | tf_op jit(solution)/shard_map/ppermute | solution.py:377
  105.9 6.6 %copy-start.2 = (bf16[32,64,128]{2,1,0:T(8,128)(2,1)}, bf16[32,64,128]{2,1,0:T(8,128)(2,1)S(1)}, u32[]{:S(2)}) copy-start(bf16[32,64,128]{2,1,0:T(8,128)(2,1)S(1)} %all-to-all-done.3.back_ref) | copy-start | bytes 1572868
  105.9 23.8 %all-to-all-start.2 = ((f32[16,48,128]{2,1,0:T(8,128)}), f32[16,48,128]{2,1,0:T(8,128)S(1)}, u32[]{:S(2)}, u32[]{:S(2)}) async-start(f32[16,48,128]{2,1,0:T(8,128)} %bitcast.4), calls=%async_computation.2 | async-start | bytes 786432 | tf_op jit(solution)/shard_map/all_to_all | solution.py:357
  121.3 6.8 %collective-permute-start.3 = (f32[256,128]{1,0:T(8,128)S(1)}, f32[256,128]{1,0:T(8,128)S(1)}, u32[]{:S(2)}, u32[]{:S(2)}) collective-permute-start(f32[256,128]{1,0:T(8,128)S(1)} %constant_dynamic-slice_fusion), channel_id=1, source_target_pairs={{0,32},{32,0},{64,96},{96,64},{128,160},{160,128},{192,224},{224,1... | collective-permute-start | bytes 393224 | tf_op jit(solution)/shard_map/ppermute | solution.py:377
  129.7 13.8 %all-to-all-start.5 = ((f32[16,16,128]{2,1,0:T(8,128)}), f32[16,16,128]{2,1,0:T(8,128)S(1)}, u32[]{:S(2)}, u32[]{:S(2)}) async-start(f32[16,16,128]{2,1,0:T(8,128)} %bitcast.5), calls=%async_computation.5 | async-start | bytes 262144 | tf_op jit(solution)/shard_map/all_to_all | solution.py:357
  168.3 5.6 %collective-permute-start.4 = (f32[1024,128]{1,0:T(8,128)S(1)}, f32[1024,128]{1,0:T(8,128)S(1)}, u32[]{:S(2)}, u32[]{:S(2)}) collective-permute-start(f32[1024,128]{1,0:T(8,128)S(1)} %bitcast.18), channel_id=1, source_target_pairs={{0,32},{32,0},{64,96},{96,64},{128,160},{160,128},{192,224},{224,1... | collective-permute-start | bytes 1572872 | tf_op jit(solution)/shard_map/ppermute | solution.py:386

commit v3 on v0

v3 whole, which is shorter than its diff:
```python
import functools

import jax
import jax.numpy as jnp
import numpy as np
from jax import lax
from jax.experimental import pallas as pl
from jax.experimental.pallas import tpu as pltpu
from jax.sharding import PartitionSpec as P

F32 = jnp.float32
BF16 = jnp.bfloat16
GROUP = 8
TAIL = 16
LANES = 128
CHUNK = 256
KINDS = 3
VMEM = 60 << 20


def matmul(a, b):
    return jnp.dot(a, b, preferred_element_type=F32)


def matmul_nt(a, b):
    return lax.dot_general(a, b, (((1,), (1,)), ((), ())), preferred_element_type=F32)


def matmul_tn(a, b):
    return lax.dot_general(a, b, (((0,), (0,)), ((), ())), preferred_element_type=F32)


def indicator(condition):
    return jnp.where(condition, 1.0, 0.0).astype(BF16)


def slope(value, sigma):
    return sigma * (1.0 + value * (1.0 - sigma))


def slot_onehot(out, holder, rank, base, capacity):
    edges = holder.shape[1]
    place = lax.broadcasted_iota(jnp.int32, (capacity, edges), 0)
    for p in range(GROUP):
        mine = jnp.where(holder == base + p, rank, -1)
        out[p * capacity : (p + 1) * capacity, :] = indicator(place == mine)


def table_kernel(nodes_ref, species_ref, out_ref):
    atoms, channels = nodes_ref.shape
    out_ref[:channels] = nodes_ref[...].T
    kinds = jnp.broadcast_to((species_ref[...] + 1).astype(F32), (TAIL, atoms))
    out_ref[channels:] = kinds.astype(BF16)


def edge_kernel(
    pos_ref, dst_ref, src_ref, holder_ref, attr_ref, out_ref, rank_ref, onehot, tags, *, atoms
):
    step = pl.program_id(0)
    edges = dst_ref.shape[1]
    devices = tags.shape[0] // 4
    capacity = out_ref.shape[1] - TAIL
    holder = holder_ref[...]

    @pl.when(step == 0)
    def _():
        same = lax.broadcasted_iota(jnp.int32, (devices, edges), 0) == holder
        named = jnp.where(same, 1.0, 0.0)
        named_bf = named.astype(BF16)
        rows = lax.broadcasted_iota(jnp.int32, (CHUNK, CHUNK), 0)
        cols = lax.broadcasted_iota(jnp.int32, (CHUNK, CHUNK), 1)
        earlier = indicator(rows < cols)
        carry = jnp.zeros((devices, 1), F32)
        for c in range(edges // CHUNK):
            part = slice(c * CHUNK, (c + 1) * CHUNK)
            before = matmul(named_bf[:, part], earlier) + carry
            carry = carry + jnp.sum(named[:, part], axis=1, keepdims=True)
            rank_ref[:, part] = jnp.sum(
                before * named[:, part], axis=0, keepdims=True
            ).astype(jnp.int32)
        offset = pos_ref[0] * atoms
        dst = dst_ref[...] - offset
        src = src_ref[...] - (offset - atoms)
        first = jnp.where(src >= 2 * atoms, 2, jnp.where(src >= atoms, 1, 0))
        within = src - first * atoms
        tagged = jnp.concatenate(
            [named * dst.astype(F32), named * first.astype(F32), named * within.astype(F32), named],
            axis=0,
        ).astype(BF16)
        at_rank = indicator(lax.broadcasted_iota(jnp.int32, (LANES, edges), 0) == rank_ref[...])
        tags[...] = matmul_nt(tagged, at_rank)

    slot_onehot(onehot, holder, rank_ref[...], step * GROUP, capacity)
    moved = matmul(onehot[...], attr_ref[...]).astype(BF16)
    line = lax.broadcasted_iota(jnp.int32, (TAIL, LANES), 0)
    for p in range(GROUP):
        out_ref[p, :capacity, :] = moved[p * capacity : (p + 1) * capacity]
        tail = jnp.zeros((TAIL, LANES), F32)
        for i in range(4):
            tail = jnp.where(line == i, tags[pl.ds(i * devices + step * GROUP + p, 1), :], tail)
        out_ref[p, capacity:, :] = tail.astype(BF16)


def prepare_kernel(
    cg_ref,
    wleft_ref,
    wright_ref,
    mask_ref,
    pick_a,
    pick_b,
    pick_dst,
    pick_src,
    cg_out,
    cg_t,
    wlr_out,
    wlr_t,
    pairs_ref,
):
    rows = cg_out.shape[0]
    orb2 = cg_ref.shape[0]

    def pad_rows(array):
        empty = jnp.zeros((rows - orb2, array.shape[1]), F32)
        return jnp.concatenate([array.astype(F32), empty], axis=0)

    tall = pad_rows(cg_ref[...])
    across = jnp.concatenate([tall, jnp.zeros((rows, rows - orb2), F32)], axis=1)
    cg_out[...] = across.astype(BF16)
    cg_t[...] = across.T.astype(BF16)
    both = jnp.concatenate([pad_rows(wleft_ref[...]), pad_rows(wright_ref[...])], axis=0)
    wlr_out[...] = both.astype(BF16)
    wlr_t[...] = both.T.astype(BF16)
    carried = mask_ref[...].astype(F32).astype(BF16)
    dst = matmul_tn(carried, pick_dst[...]).astype(BF16)
    src = matmul_tn(carried, pick_src[...]).astype(BF16)
    pairs_ref[...] = (matmul(pick_a[...], dst) * matmul(pick_b[...], src)).astype(BF16)


def holder_kernel(
    recv_ref,
    target_ref,
    table_ref,
    w_dst,
    w_src,
    w_attr,
    w_mix,
    wlr_ref,
    wlr_t,
    cg_ref,
    cg_t,
    pairs_ref,
    place_ref,
    grad_ref,
    err_ref,
    dlr,
):
    step = pl.program_id(0)
    steps = pl.num_programs(0)
    capacity = recv_ref.shape[1] - TAIL
    width = GROUP * capacity
    channels = recv_ref.shape[2]
    rows = cg_ref.shape[0]
    orb2 = target_ref.shape[1]
    tall = channels + TAIL
    atoms = table_ref.shape[1]

    @pl.when(step == 0)
    def _():
        grad_ref[...] = jnp.zeros_like(grad_ref)

    ids = lax.broadcasted_iota(jnp.int32, (3 * atoms, 2 * capacity), 0)
    from_dst = []
    from_src = []
    for i in range(GROUP):
        tail = recv_ref[i, capacity:, :].astype(F32)[:, :capacity]
        absent = (tail[3:4] - 1.0) * (4.0 * atoms)
        dst = tail[0:1] + (atoms + absent)
        src = tail[1:2] * atoms + tail[2:3] + absent
        place = jnp.concatenate([src, dst], axis=1).astype(jnp.int32)
        q = step * GROUP + i
        window = []
        for near in (jnp.maximum(q - 1, 0), q, jnp.minimum(q + 1, steps * GROUP - 1)):
            start = pl.multiple_of(near * tall, TAIL)
            window.append(table_ref[pl.ds(start, tall), :])
        found = matmul(jnp.concatenate(window, axis=1), indicator(ids == place))
        from_src.append(found[:, :capacity])
        from_dst.append(found[:, capacity:])
    from_dst = jnp.concatenate(from_dst, axis=1)
    from_src = jnp.concatenate(from_src, axis=1)
    xdst = from_dst[:channels].astype(BF16)
    xsrc = from_src[:channels].astype(BF16)
    kind_dst = from_dst[channels : channels + 1]
    kind_src = from_src[channels : channels + 1]
    code = jnp.where(kind_dst > 0.5, (kind_dst - 1.0) * KINDS + (kind_src - 1.0), -1.0)
    pair_line = lax.broadcasted_iota(jnp.int32, (pairs_ref.shape[1], width), 0)
    pair = indicator(pair_line == code.astype(jnp.int32))
    attr = recv_ref[:, :capacity, :].reshape(width, channels)

    pre = matmul(w_dst[...].T, xdst) + matmul(w_src[...].T, xsrc)
    pre = pre + matmul_nt(w_attr[...].T, attr)
    sig_pre = jax.nn.sigmoid(pre)
    first = (pre * sig_pre).astype(BF16)
    mixpre = matmul(w_mix[...].T, first)
    sig_mix = jax.nn.sigmoid(mixpre)
    second = (first.astype(F32) + mixpre * sig_mix).astype(BF16)

    both = matmul(wlr_ref[...], second)
    left = both[:rows]
    right = both[rows:]
    predicted = matmul(cg_t[...], (left * right).astype(BF16))
    mask = matmul(pairs_ref[...], pair)
    goal = target_ref[0].astype(F32)
    goal = jnp.concatenate([goal, jnp.zeros((rows - orb2, width), F32)], axis=0)
    resid = mask * (predicted - goal)
    error = jnp.sum(resid * resid, axis=0, keepdims=True) / orb2
    dpred = (resid * (1.0 / orb2)).astype(BF16)
    dcoupled = matmul(cg_ref[...], dpred)
    dlr[:rows] = (dcoupled * right).astype(BF16)
    dlr[rows:] = (dcoupled * left).astype(BF16)

    dsecond = matmul(wlr_t[...], dlr[...])
    dmix = (dsecond * slope(mixpre, sig_mix)).astype(BF16)
    dfirst = dsecond + matmul(w_mix[...], dmix)
    dpre = (dfirst * slope(pre, sig_pre)).astype(BF16)
    grad_ref[0:channels] += matmul_nt(xdst, dpre)
    grad_ref[channels : 2 * channels] += matmul_nt(xsrc, dpre)
    grad_ref[2 * channels : 3 * channels] += matmul(dpre, attr)
    grad_ref[3 * channels : 4 * channels] += matmul_nt(first, dmix)
    grad_ref[4 * channels : 4 * channels + 2 * rows] += matmul_nt(dlr[...], second)

    line = lax.broadcasted_iota(jnp.int32, (GROUP, width), 0)
    spread = indicator(
        lax.broadcasted_iota(jnp.int32, (LANES, width), 0) == place_ref[1:2, :]
    )
    total = jnp.zeros((GROUP, LANES), F32)
    rest = jnp.where(line == place_ref[0:1, :], error, 0.0)
    for _ in range(3):
        top = rest.astype(BF16)
        rest = rest - top.astype(F32)
        total = total + matmul_nt(top, spread)
    err_ref[...] = total

    @pl.when(step == steps - 1)
    def _():
        flipped = grad_ref[2 * channels : 3 * channels]
        grad_ref[2 * channels : 3 * channels] = flipped.T


def pick_kernel(table_ref, holder_ref, rank_ref, error_ref):
    devices, lanes = table_ref.shape
    edges = holder_ref.shape[1]
    named = indicator(
        lax.broadcasted_iota(jnp.int32, (devices, edges), 0) == holder_ref[...]
    )
    found = jnp.zeros((lanes, edges), F32)
    rest = table_ref[...]
    for _ in range(3):
        top = rest.astype(BF16)
        rest = rest - top.astype(F32)
        found = found + matmul_tn(top, named)
    place = lax.broadcasted_iota(jnp.int32, (lanes, edges), 0)
    error_ref[...] = jnp.sum(
        jnp.where(place == rank_ref[...], found, 0.0), axis=0, keepdims=True
    )


def exchange(array, axis, groups=None):
    return lax.all_to_all(
        array, axis, split_axis=0, concat_axis=0, tiled=True, axis_index_groups=groups
    )


WIDE, NARROW, DEEP = 4, 4, 8
PEERS = WIDE * NARROW
SWAP = [(i, i ^ 1) for i in range(WIDE * 2)]
PLANE = [
    [(y * 2 + c) * NARROW * DEEP + z * NARROW + x for y in range(WIDE) for x in range(NARROW)]
    for c in range(2)
    for z in range(DEEP)
]
COLUMN = [[z * NARROW + x for z in range(DEEP)] for x in range(NARROW)]
ROW = [[z * NARROW + x for x in range(NARROW)] for z in range(DEEP)]


def sum_and_return(part, errors):
    half = part.shape[0] // 2
    core = lax.rem(lax.axis_index("rep"), 2)
    row = lax.div(lax.axis_index("rep"), 2)
    length = half // PEERS
    keep = lax.dynamic_slice_in_dim(part, core * half, half, 0)
    give = lax.dynamic_slice_in_dim(part, (1 - core) * half, half, 0)
    part = keep + lax.ppermute(give, "rep", SWAP)

    lanes = errors.shape[1]
    errors = errors.reshape(DEEP, NARROW, lanes).transpose(1, 0, 2)
    errors = jnp.broadcast_to(errors[None], (WIDE, NARROW, DEEP, lanes))
    sent = jnp.concatenate(
        [part.reshape(PEERS, length, lanes), errors.reshape(PEERS, DEEP, lanes)], axis=1
    )
    got = exchange(sent, ("rep", "edge"), PLANE)
    part = jnp.sum(got[:, :length], axis=0)
    errors = lax.dynamic_slice_in_dim(got[:, length:], row * NARROW, NARROW, 0)
    errors = jnp.pad(errors.transpose(1, 0, 2), ((0, 0), (0, 8 - NARROW), (0, 0)))
    sent = jnp.concatenate(
        [jnp.broadcast_to(part[None], (DEEP, length, lanes)), errors], axis=1
    )
    got = exchange(sent, "edge", COLUMN)
    part = jnp.sum(got[:, :length], axis=0)
    errors = got[:, length : length + NARROW].reshape(DEEP * NARROW, lanes)

    part = exchange(jnp.tile(part, (PEERS, 1)), ("rep", "edge"), PLANE)
    other = lax.ppermute(part, "rep", SWAP)
    low = jnp.where(core == 0, part, other)
    high = jnp.where(core == 0, other, part)
    return jnp.concatenate([low, high], axis=0), errors


def local(
    node_feats,
    edge_attr,
    edge_src,
    edge_dst,
    species,
    orbital_mask,
    tile_owner,
    target_send,
    w_dst,
    w_src,
    w_attr,
    w_mix,
    w_left,
    w_right,
    cg_basis,
):
    atoms, channels = node_feats.shape[1:]
    edges = edge_attr.shape[1]
    orb2, columns = target_send.shape[1:]
    devices = lax.axis_size("edge")
    capacity = columns // devices
    steps = devices // GROUP
    width = GROUP * capacity
    block = capacity + TAIL
    tall = channels + TAIL
    position = lax.axis_index("edge").astype(jnp.int32)[None]
    rows = -(-orb2 // 32) * 32
    holder = tile_owner.reshape(1, edges)
    params = pltpu.CompilerParams(vmem_limit_bytes=VMEM)

    def whole(shape):
        return pl.BlockSpec(shape, lambda *_: (0,) * len(shape))

    def array(shape, dtype=BF16):
        return jax.ShapeDtypeStruct(shape, dtype)

    square = whole((channels, channels))
    line = whole((1, edges))
    packets = pl.BlockSpec((GROUP, block, channels), lambda i, *_: (i, 0, 0))

    table = pl.pallas_call(
        lambda pos_ref, *refs: table_kernel(*refs),
        out_shape=array((tall, atoms)),
        grid_spec=pltpu.PrefetchScalarGridSpec(
            num_scalar_prefetch=1,
            grid=(1,),
            in_specs=[
                whole((atoms, channels)),
                pl.BlockSpec((1, atoms), lambda i, pos: (0, pos[0])),
            ],
            out_specs=whole((tall, atoms)),
        ),
        compiler_params=params,
    )(position, node_feats[0], species)
    table = exchange(jnp.tile(table, (NARROW, 1)), "edge", ROW)
    table = lax.all_gather(table, "edge", axis=0, tiled=True, axis_index_groups=COLUMN)

    sent, rank = pl.pallas_call(
        functools.partial(edge_kernel, atoms=atoms),
        out_shape=(array((devices, block, channels)), array((1, edges), jnp.int32)),
        grid_spec=pltpu.PrefetchScalarGridSpec(
            num_scalar_prefetch=1,
            grid=(steps,),
            in_specs=[line, line, line, whole((edges, channels))],
            out_specs=[packets, line],
            scratch_shapes=[
                pltpu.VMEM((width, edges), BF16),
                pltpu.VMEM((4 * devices, LANES), F32),
            ],
        ),
        compiler_params=params,
    )(position, edge_dst, edge_src, holder, edge_attr[0])
    received = exchange(sent, "edge")

    species_count, orbs = orbital_mask.shape
    entry = np.arange(rows)[:, None]
    orbit = np.arange(orbs)[None, :]
    valid = entry < orb2
    pick_a = (valid & (entry // orbs == orbit)).astype(BF16)
    pick_b = (valid & (entry % orbs == orbit)).astype(BF16)
    code = np.arange(TAIL)[None, :]
    kind = np.arange(species_count)[:, None]
    known = code < species_count**2
    pick_dst = (known & (code // species_count == kind)).astype(BF16)
    pick_src = (known & (code % species_count == kind)).astype(BF16)
    prepared = [
        array((rows, rows)),
        array((rows, rows)),
        array((2 * rows, channels)),
        array((channels, 2 * rows)),
        array((rows, TAIL)),
    ]
    ready = pl.pallas_call(prepare_kernel, out_shape=prepared, compiler_params=params)(
        cg_basis, w_left, w_right, orbital_mask, pick_a, pick_b, pick_dst, pick_src
    )
    cg, cg_t, wlr, wlr_t, pairs = ready

    slots = np.arange(width)
    places = np.stack([slots // capacity, slots % capacity]).astype(np.int32)
    unit = 2 * PEERS * 8
    total = -(-(4 * channels + 2 * rows) // unit) * unit
    shared = (wlr, wlr_t, cg, cg_t, pairs, places)
    grads, errors = pl.pallas_call(
        holder_kernel,
        out_shape=(array((total, channels), F32), array((devices, LANES), F32)),
        grid=(steps,),
        in_specs=[
            packets,
            pl.BlockSpec((1, orb2, width), lambda i: (0, 0, i)),
            whole(table.shape),
            square,
            square,
            square,
            square,
            *[whole(a.shape) for a in shared],
        ],
        out_specs=[whole((total, channels)), pl.BlockSpec((GROUP, LANES), lambda i: (i, 0))],
        scratch_shapes=[pltpu.VMEM((2 * rows, width), BF16)],
        compiler_params=params,
    )(received, target_send, table, w_dst, w_src, w_attr, w_mix, *shared)

    grads, errors = sum_and_return(grads, errors)
    edge_error = pl.pallas_call(
        pick_kernel,
        out_shape=array((1, edges), F32),
        compiler_params=params,
    )(errors, holder, rank)
    outs = [grads[i * channels : (i + 1) * channels] for i in range(4)]
    outs += [grads[4 * channels + i * rows :][:orb2] for i in range(2)]
    return (*outs, edge_error)


def solution(mesh):
    return jax.shard_map(
        local,
        mesh=mesh,
        in_specs=(
            P("rep", "edge", None),
            P("rep", "edge", None),
            P("rep", "edge"),
            P("rep", "edge"),
            P("rep", None),
            P(),
            P("rep", "edge", None),
            P("rep", "edge", None),
            P(),
            P(),
            P(),
            P(),
            P(),
            P(),
            P(),
        ),
        out_specs=(P(), P(), P(), P(), P(), P(), P("rep", "edge")),
        check_vma=False,
    )
```

time: 585 us -> 176 us (0.30)
  waiting for transfers between devices: 307 us -> 53.3 us
  local copies, waits for them, and re-layouts: 136 us -> 4.19 us
  other arithmetic: 67.4 us -> 1.96 us
  Pallas kernels: 0 us -> 42.3 us
  matrix products: 40.2 us -> 0 us
  blocking collectives: 0 us -> 36.7 us
    psum x1 -> x0, waiting for transfers between devices: 283 us -> none  [local(): lax.psum((grad_dst, grad_src, grad_attr, grad_mix, grad_left, grad_right)...]
    unnamed x66 -> x5, local copies, waits for them, and re-layouts: 68.4 us -> 0.01 us
    gather x6 -> x0, local copies, waits for them, and re-layouts: 53.9 us -> none  [the longest x2 18 us: local(): jnp.take(lax.all_to_all(target_send, 'edge', split_axis=2, concat_axis=2,...]
    unnamed x2 -> x0, other arithmetic: 53.5 us -> none
    pallas_call x0 -> x5, Pallas kernels: none -> 42.3 us  [the longest x1 28.8 us: local(): pl.pallas_call(holder_kernel, out_shape=(array((total, channels), F32), a...]
    dot_general x19 -> x0, matrix products: 40.2 us -> none  [the longest x1 10.7 us: edge_block(): lax.dot_general(cg_basis, coupled, (((0,), (0,)), ((), ())), preferred_el...]
    all_to_all x0 -> x3, blocking collectives: none -> 36.7 us  [exchange(): lax.all_to_all(array, axis, split_axis=0, concat_axis=0, tiled=True, axis...]
    all_to_all x1 -> x2, waiting for transfers between devices: 24.6 us -> 42.3 us  [exchange(): lax.all_to_all(array, axis, split_axis=0, concat_axis=0, tiled=True, axis...]
  transfers between devices with their start and end apart: 4 -> 5, of which waited for: 2 -> 4; matrix products, arithmetic and copies ran while one was open for 12% -> 1% of each run, Pallas kernels for 0% -> 7%
where the time goes in v3:
time: 176 us; the launch traced here: 175 us
  waiting for transfers between devices  53.3 us (30%)
  Pallas kernels  42.3 us (24%)
  blocking collectives  36.7 us (21%)
  starting transfers between devices  22.6 us (13%)
  between operations  14.2 us (8%)
  local copies, waits for them, and re-layouts  4.19 us (2%)
  other arithmetic  1.96 us (1%)
    all_to_all x2, waiting for transfers between devices, exchange(): lax.all_to_all(array, axis, split_axis=0, concat_axis=0, tiled=True, axis...  42.3 us
    all_to_all x3, blocking collectives, exchange(): lax.all_to_all(array, axis, split_axis=0, concat_axis=0, tiled=True, axis...  36.7 us
    pallas_call x1, Pallas kernels, local(): pl.pallas_call(holder_kernel, out_shape=(array((total, channels), F32), a...  28.8 us
    all_to_all x2, starting transfers between devices, exchange(): lax.all_to_all(array, axis, split_axis=0, concat_axis=0, tiled=True, axis...  15.7 us
    all_gather x1, waiting for transfers between devices, local(): lax.all_gather(table, 'edge', axis=0, tiled=True, axis_index_groups=COLUMN)  10.2 us
    pallas_call x1, Pallas kernels, local(): pl.pallas_call(functools.partial(edge_kernel, atoms=atoms), out_shape=(ar...  6.51 us
    ppermute x1, starting transfers between devices, sum_and_return(): other = lax.ppermute(part, 'rep', SWAP)  4.51 us
    pallas_call x1, Pallas kernels, local(): pl.pallas_call(prepare_kernel, out_shape=prepared, compiler_params=params)  3.54 us
  transfers between devices with their start and end apart: 5, of which 4 were waited for; matrix products, arithmetic and copies ran while one was open for 1% of the time, Pallas kernels for 7%

profile of v3, /device:TPU:1, one launch (start us, length us, event | category | flops | bytes accessed | tf_op | source)
XLA Modules:
  0.0 175.3 jit_solution(17736787019200621830)
XLA Ops:
  7.2 0.0 all-gather.2.cloned.1.call-start
  7.2 1.5 shard_map.244
  8.8 0.9 tile.4
  9.7 10.5 %all_to_all.33 = bf16[4,144,256]{2,1,0:T(8,128)(2,1)} all-to-all(bf16[4,144,256]{2,1,0:T(8,128)(2,1)S(1)} %tile.4), channel_id=1, replica_groups={{0,1,2,3},{4,5,6,7},{8,9,10,11},{12,13,14,15},{16,17,18,19},{20,21,22,2..., dimensions={0} | all-to-all | bytes 589824 | tf_op jit(solution)/shard_map/all_to_all | solution.py:268
  20.1 0.0 all-gather.2.cloned.1.call-update
  20.1 6.5 %shard_map.243 = (bf16[32,112,128]{2,1,0:T(8,128)(2,1)}, s32[1,2048]{1,0:T(1,128)}) custom-call(s32[1]{0:T(128)} %bitcast.pos_ref, s32[1,2048]{1,0:T(1,128)} %dst_ref.1, s32[1,2048]{1,0:T(1,128)} %src_ref.1, s32[1,2048]{1,0:T(1,128)} %bitcast.23, bf16[2048,128]{1,0:T(8,128)(2,1)} %bitcast.19), custom_call_target="tpu_custom_call" | custom-call | tf_op jit(solution)/shard_map/pallas_call | solution.py:376
  26.7 9.4 %all-to-all-start = ((bf16[32,112,128]{2,1,0:T(8,128)(2,1)}), bf16[32,112,128]{2,1,0:T(8,128)(2,1)S(1)}, u32[]{:S(2)}, u32[]{:S(2)}) async-start(bf16[32,112,128]{2,1,0:T(8,128)(2,1)} %get-tuple-element.16), calls=%async_computation | async-start | bytes 1835008 | tf_op jit(solution)/shard_map/all_to_all | solution.py:268
  36.1 3.5 %shard_map.245 = (bf16[736,736]{1,0:T(8,128)(2,1)}, bf16[736,736]{1,0:T(8,128)(2,1)}, bf16[1472,128]{1,0:T(8,128)(2,1)}, bf16[128,1472]{1,0:T(8,128)(2,1)}, bf16[736,16]{1,0:T(8,128)(2,1)}) custom-call(bf16[729,729]{1,0:T(8,128)(2,1)} %cg_ref.1, bf16[729,128]{1,0:T(8,128)(2,1)} %wleft_ref.1, bf16[729,128]{1,0:T(8,128)(2,1)} %wright_ref.1, s32[3,27]{1,0:T(4,128)} %mask_ref.1, ...), custom_call_target="tpu_custom_call" | custom-call | tf_op jit(solution)/shard_map/pallas_call | solution.py:411
  39.6 30.9 %all-to-all-done.recv_ref = bf16[32,112,128]{2,1,0:T(8,128)(2,1)S(1)} async-done(((bf16[32,112,128]{2,1,0:T(8,128)(2,1)}), bf16[32,112,128]{2,1,0:T(8,128)(2,1)S(1)}, u32[]{:S(2)}, u32[]{:S(2)}) %all-to-all-start) | async-done | bytes 917536 | tf_op jit(solution)/shard_map/all_to_all | solution.py:268
  70.6 0.0 copy-start
  70.6 10.2 %all-gather.2.cloned.1.call-done.table_ref = bf16[4608,256]{1,0:T(8,128)(2,1)} async-done(((bf16[576,256]{1,0:T(8,128)(2,1)}), bf16[4608,256]{1,0:T(8,128)(2,1)}) %all-gather.2.cloned.1.call-update) | async-done | bytes 2359312 | tf_op jit(solution)/shard_map/all_gather | solution.py:374
  80.7 0.0 copy-done
  80.7 28.8 %shard_map.246 = (f32[2048,128]{1,0:T(8,128)}, f32[32,128]{1,0:T(8,128)}) custom-call(bf16[32,112,128]{2,1,0:T(8,128)(2,1)} %copy-done, bf16[1,729,3072]{2,1,0:T(8,128)(2,1)} %target_ref.1, bf16[4608,256]{1,0:T(8,128)(2,1)} %all-gather.2.cloned.1.call-done.table_ref, bf16[128,128]{1,0:T(8,128)(2,1)} %w_dst.1, bf16[128,128]{1,0:T(8,128)(2,1)} %w_src.1, ...), custom_call_target="tpu_custom_call" | custom-call | tf_op jit(solution)/shard_map/pallas_call | solution.py:421
  109.5 0.0 copy-start.1
  109.5 1.2 constant_dynamic-slice_fusion
  110.7 2.4 %collective-permute-start = (f32[1024,128]{1,0:T(8,128)S(1)}, f32[1024,128]{1,0:T(8,128)S(1)}, u32[]{:S(2)}, u32[]{:S(2)}) collective-permute-start(f32[1024,128]{1,0:T(8,128)S(1)} %constant_dynamic-slice_fusion), channel_id=1, source_target_pairs={{0,32},{32,0},{64,96},{96,64},{128,160},{160,128},{192,224},{224,1... | collective-permute-start | bytes 1572872 | tf_op jit(solution)/shard_map/ppermute | solution.py:292
  113.1 0.7 copy.28
  113.8 0.8 collective-permute-done
  114.6 0.0 copy-done.1
  114.6 0.1 dynamic-slice_add_fusion
  114.7 0.8 pad_maximum_fusion
  115.5 6.3 %all-to-all-start.2 = ((f32[16,72,128]{2,1,0:T(8,128)}), f32[16,72,128]{2,1,0:T(8,128)S(1)}, u32[]{:S(2)}, u32[]{:S(2)}) async-start(f32[16,72,128]{2,1,0:T(8,128)} %pad_maximum_fusion), calls=%async_computation.2 | async-start | bytes 1179648 | tf_op jit(solution)/shard_map/all_to_all | solution.py:268
  121.8 11.4 %all-to-all-done.2 = f32[16,72,128]{2,1,0:T(8,128)S(1)} async-done(((f32[16,72,128]{2,1,0:T(8,128)}), f32[16,72,128]{2,1,0:T(8,128)S(1)}, u32[]{:S(2)}, u32[]{:S(2)}) %all-to-all-start.2) | async-done | bytes 589856 | tf_op jit(solution)/shard_map/all_to_all | solution.py:268
  133.3 13.0 %all_to_all.34 = f32[8,72,128]{2,1,0:T(8,128)S(1)} all-to-all(f32[8,72,128]{2,1,0:T(8,128)S(1)} %select_maximum_fusion), channel_id=1, replica_groups={{0,4,8,12,16,20,24,28},{1,5,9,13,17,21,25,29},{2,6,10,14,18,22,26,30},{..., dimensions={0} | all-to-all | bytes 589824 | tf_op jit(solution)/shard_map/all_to_all | solution.py:268
  146.4 13.3 %all_to_all.35 = f32[16,64,128]{2,1,0:T(8,128)S(1)} all-to-all(f32[16,64,128]{2,1,0:T(8,128)S(1)} %tile.5), channel_id=1, replica_groups={{0,1,2,3,64,65,66,67,128,129,130,131,192,193,194,195},{4,5,6,7,68,69,70..., dimensions={0} | all-to-all | bytes 1048576 | tf_op jit(solution)/shard_map/all_to_all | solution.py:268
  159.7 4.5 %collective-permute-start.1 = (f32[1024,128]{1,0:T(8,128)S(1)}, f32[1024,128]{1,0:T(8,128)S(1)}, u32[]{:S(2)}, u32[]{:S(2)}) collective-permute-start(f32[1024,128]{1,0:T(8,128)S(1)} %bitcast.16), channel_id=1, source_target_pairs={{0,32},{32,0},{64,96},{96,64},{128,160},{160,128},{192,224},{224,1... | collective-permute-start | bytes 1572872 | tf_op jit(solution)/shard_map/ppermute | solution.py:312
  164.2 0.6 slice.52
  164.8 1.9 %shard_map.247 = f32[1,2048]{1,0:T(1,128)} custom-call(f32[32,128]{1,0:T(8,128)} %bitcast.22, s32[1,2048]{1,0:T(1,128)} %bitcast.24, s32[1,2048]{1,0:T(1,128)} %get-tuple-element.24.rank_ref), custom_call_target="tpu_custom_call" | custom-call | tf_op jit(solution)/shard_map/pallas_call | solution.py:441
  166.7 0.0 collective-permute-done.1
  166.7 0.1 broadcast_select_fusion
  166.8 0.7 fusion.1
  167.5 0.9 fusion
  (9 shorter events, 0.2 us)
Async XLA Ops:
  7.2 73.6 %all-gather.2.cloned.1.call-start = ((), (), s32[]{:S(2)}) async-start(), calls=%async_computation.5 | async-start | bytes 2654208 | tf_op jit(solution)/shard_map/all_gather | solution.py:374
  26.7 43.9 %all-to-all-start = ((bf16[32,112,128]{2,1,0:T(8,128)(2,1)}), bf16[32,112,128]{2,1,0:T(8,128)(2,1)S(1)}, u32[]{:S(2)}, u32[]{:S(2)}) async-start(bf16[32,112,128]{2,1,0:T(8,128)(2,1)} %get-tuple-element.16), calls=%async_computation | async-start | bytes 1835008 | tf_op jit(solution)/shard_map/all_to_all | solution.py:268
  70.6 10.2 %copy-start = (bf16[32,112,128]{2,1,0:T(8,128)(2,1)}, bf16[32,112,128]{2,1,0:T(8,128)(2,1)S(1)}, u32[]{:S(2)}) copy-start(bf16[32,112,128]{2,1,0:T(8,128)(2,1)S(1)} %all-to-all-done.recv_ref) | copy-start | bytes 2752516
  109.5 5.1 %copy-start.1 = (f32[2048,128]{1,0:T(8,128)S(1)}, f32[2048,128]{1,0:T(8,128)}, u32[]{:S(2)}) copy-start(f32[2048,128]{1,0:T(8,128)} %get-tuple-element.22) | copy-start | bytes 3145732
  110.7 3.9 %collective-permute-start = (f32[1024,128]{1,0:T(8,128)S(1)}, f32[1024,128]{1,0:T(8,128)S(1)}, u32[]{:S(2)}, u32[]{:S(2)}) collective-permute-start(f32[1024,128]{1,0:T(8,128)S(1)} %constant_dynamic-slice_fusion), channel_id=1, source_target_pairs={{0,32},{32,0},{64,96},{96,64},{128,160},{160,128},{192,224},{224,1... | collective-permute-start | bytes 1572872 | tf_op jit(solution)/shard_map/ppermute | solution.py:292
  115.5 17.7 %all-to-all-start.2 = ((f32[16,72,128]{2,1,0:T(8,128)}), f32[16,72,128]{2,1,0:T(8,128)S(1)}, u32[]{:S(2)}, u32[]{:S(2)}) async-start(f32[16,72,128]{2,1,0:T(8,128)} %pad_maximum_fusion), calls=%async_computation.2 | async-start | bytes 1179648 | tf_op jit(solution)/shard_map/all_to_all | solution.py:268
  159.7 7.1 %collective-permute-start.1 = (f32[1024,128]{1,0:T(8,128)S(1)}, f32[1024,128]{1,0:T(8,128)S(1)}, u32[]{:S(2)}, u32[]{:S(2)}) collective-permute-start(f32[1024,128]{1,0:T(8,128)S(1)} %bitcast.16), channel_id=1, source_target_pairs={{0,32},{32,0},{64,96},{96,64},{128,160},{160,128},{192,224},{224,1... | collective-permute-start | bytes 1572872 | tf_op jit(solution)/shard_map/ppermute | solution.py:312
Sparse Core Ops, SparseCore 0:
  20.3 60.4 all-gather.1

commit v4 on v2

v4 whole, which is shorter than its diff:
```python
import functools

import jax
import jax.numpy as jnp
import numpy as np
from jax import lax
from jax.experimental import pallas as pl
from jax.experimental.pallas import tpu as pltpu
from jax.sharding import PartitionSpec as P

F32 = jnp.float32
BF16 = jnp.bfloat16
GROUP = 8
TAIL = 16
LANES = 128
CHUNK = 256
KINDS = 3
VMEM = 60 << 20


def ring(count, shift):
    return [(i, (i + shift) % count) for i in range(count)]


def matmul(a, b):
    return jnp.dot(a, b, preferred_element_type=F32)


def matmul_nt(a, b):
    return lax.dot_general(a, b, (((1,), (1,)), ((), ())), preferred_element_type=F32)


def matmul_tn(a, b):
    return lax.dot_general(a, b, (((0,), (0,)), ((), ())), preferred_element_type=F32)


def indicator(condition):
    return jnp.where(condition, 1.0, 0.0).astype(BF16)


def slope(value, sigma):
    return sigma * (1.0 + value * (1.0 - sigma))


def slot_onehot(out, holder, rank, base, capacity):
    edges = holder.shape[1]
    place = lax.broadcasted_iota(jnp.int32, (capacity, edges), 0).astype(BF16)
    one = jnp.ones((capacity, edges), BF16)
    for p in range(GROUP):
        mine = jnp.where(holder == base + p, rank, -1).astype(BF16)
        out[p * capacity : (p + 1) * capacity, :] = jnp.where(place == mine, one, 0.0)


def edge_kernel(
    pos_ref,
    dst_ref,
    src_ref,
    holder_ref,
    spec_lo,
    spec_mid,
    spec_hi,
    node_lo,
    node_mid,
    node_hi,
    attr_ref,
    w_dst,
    w_src,
    w_attr,
    w_mix,
    out_ref,
    rank_ref,
    xdst_ref,
    xsrc_ref,
    first_ref,
    pre_ref,
    mixpre_ref,
    second_ref,
    onehot,
    tags,
):
    step = pl.program_id(0)
    edges = dst_ref.shape[1]
    devices = tags.shape[0] // 2
    capacity = out_ref.shape[1] - TAIL
    atoms = node_mid.shape[0]
    holder = holder_ref[...]

    @pl.when(step == 0)
    def _():
        offset = pos_ref[0] * atoms
        same = lax.broadcasted_iota(jnp.int32, (devices, edges), 0) == holder
        named = jnp.where(same, 1.0, 0.0)
        named_bf = named.astype(BF16)
        rows = lax.broadcasted_iota(jnp.int32, (CHUNK, CHUNK), 0)
        cols = lax.broadcasted_iota(jnp.int32, (CHUNK, CHUNK), 1)
        earlier = indicator(rows < cols)
        carry = jnp.zeros((devices, 1), F32)
        for c in range(edges // CHUNK):
            part = slice(c * CHUNK, (c + 1) * CHUNK)
            before = matmul(named_bf[:, part], earlier) + carry
            carry = carry + jnp.sum(named[:, part], axis=1, keepdims=True)
            rank_ref[:, part] = jnp.sum(
                before * named[:, part], axis=0, keepdims=True
            ).astype(jnp.int32)
        rank = rank_ref[...]

        def table_of(nodes, spec):
            kinds = jnp.broadcast_to((spec[...] + 1).astype(F32), (TAIL, atoms)).astype(BF16)
            return jnp.concatenate([nodes[...].T, kinds], axis=0)

        table_mid = table_of(node_mid, spec_mid)
        table = jnp.concatenate(
            [table_of(node_lo, spec_lo), table_mid, table_of(node_hi, spec_hi)], axis=1
        )
        channels = node_mid.shape[1]
        ids = lax.broadcasted_iota(jnp.int32, (atoms, edges), 0)
        from_dst = matmul(table_mid, indicator(ids == dst_ref[...] - offset))
        ids = lax.broadcasted_iota(jnp.int32, (3 * atoms, edges), 0)
        from_src = matmul(table, indicator(ids == src_ref[...] - (offset - atoms)))
        xdst = from_dst[:channels].astype(BF16)
        xsrc = from_src[:channels].astype(BF16)
        xdst_ref[...] = xdst
        xsrc_ref[...] = xsrc
        pre = matmul(w_dst[...].T, xdst) + matmul(w_src[...].T, xsrc)
        pre = pre + matmul_nt(w_attr[...].T, attr_ref[...])
        pre_ref[...] = pre
        first = (pre * jax.nn.sigmoid(pre)).astype(BF16)
        first_ref[...] = first
        mixpre = matmul(w_mix[...].T, first)
        mixpre_ref[...] = mixpre
        second_ref[...] = (first.astype(F32) + mixpre * jax.nn.sigmoid(mixpre)).astype(BF16)
        tagged = jnp.concatenate(
            [named * from_dst[channels : channels + 1], named * from_src[channels : channels + 1]],
            axis=0,
        ).astype(BF16)
        at_rank = indicator(lax.broadcasted_iota(jnp.int32, (LANES, edges), 0) == rank)
        tags[...] = matmul_nt(tagged, at_rank)

    slot_onehot(onehot, holder, rank_ref[...], step * GROUP, capacity)
    moved = matmul_nt(onehot[...], second_ref[...]).astype(BF16)
    line = lax.broadcasted_iota(jnp.int32, (TAIL, LANES), 0)
    for p in range(GROUP):
        out_ref[p, :capacity, :] = moved[p * capacity : (p + 1) * capacity]
        tag_dst = tags[pl.ds(step * GROUP + p, 1), :]
        tag_src = tags[pl.ds(devices + step * GROUP + p, 1), :]
        tail = jnp.where(line == 0, tag_dst, jnp.where(line == 1, tag_src, 0.0))
        out_ref[p, capacity:, :] = tail.astype(BF16)


def prepare_kernel(
    cg_ref,
    wleft_ref,
    wright_ref,
    mask_ref,
    pick_a,
    pick_b,
    pick_dst,
    pick_src,
    cg_out,
    cg_t,
    wlr_out,
    pairs_ref,
):
    rows = cg_out.shape[0]
    orb2 = cg_ref.shape[0]

    def pad_rows(array):
        empty = jnp.zeros((rows - orb2, array.shape[1]), F32)
        return jnp.concatenate([array.astype(F32), empty], axis=0)

    tall = pad_rows(cg_ref[...])
    across = jnp.concatenate([tall, jnp.zeros((rows, rows - orb2), F32)], axis=1)
    cg_out[...] = across.astype(BF16)
    cg_t[...] = across.T.astype(BF16)
    both = jnp.concatenate([pad_rows(wleft_ref[...]), pad_rows(wright_ref[...])], axis=0)
    wlr_out[...] = both.astype(BF16)
    carried = mask_ref[...].astype(F32).astype(BF16)
    dst = matmul_tn(carried, pick_dst[...]).astype(BF16)
    src = matmul_tn(carried, pick_src[...]).astype(BF16)
    pairs_ref[...] = (matmul(pick_a[...], dst) * matmul(pick_b[...], src)).astype(BF16)


def holder_kernel(
    recv_ref,
    target_ref,
    wlr_ref,
    cg_ref,
    cg_t,
    pairs_ref,
    place_ref,
    back_ref,
    grad_ref,
    dlr,
):
    step = pl.program_id(0)
    capacity = recv_ref.shape[1] - TAIL
    width = GROUP * capacity
    channels = recv_ref.shape[2]
    rows = cg_ref.shape[0]
    orb2 = target_ref.shape[1]

    @pl.when(step == 0)
    def _():
        grad_ref[...] = jnp.zeros_like(grad_ref)

    second = recv_ref[:, :capacity, :].reshape(width, channels)
    line = lax.broadcasted_iota(jnp.int32, (GROUP * TAIL, width), 0)
    start = place_ref[0:1, :]
    spread = indicator(lax.broadcasted_iota(jnp.int32, (LANES, width), 0) == place_ref[1:2, :])
    tails = recv_ref[:, capacity:, :].reshape(GROUP * TAIL, LANES)
    tags = matmul(tails, spread)
    tag_dst = jnp.sum(jnp.where(line == start, tags, 0.0), axis=0, keepdims=True)
    tag_src = jnp.sum(jnp.where(line == start + 1, tags, 0.0), axis=0, keepdims=True)
    code = jnp.where(tag_dst > 0.5, (tag_dst - 1.0) * KINDS + (tag_src - 1.0), -1.0)
    pair_line = lax.broadcasted_iota(jnp.int32, (pairs_ref.shape[1], width), 0)
    pair = indicator(pair_line == code.astype(jnp.int32))

    both = matmul_nt(wlr_ref[...], second)
    left = both[:rows]
    right = both[rows:]
    predicted = matmul(cg_t[...], (left * right).astype(BF16))
    mask = matmul(pairs_ref[...], pair)
    goal = target_ref[0].astype(F32)
    goal = jnp.concatenate([goal, jnp.zeros((rows - orb2, width), F32)], axis=0)
    resid = mask * (predicted - goal)
    error = jnp.sum(resid * resid, axis=0, keepdims=True) / orb2
    dpred = (resid * (1.0 / orb2)).astype(BF16)
    dcoupled = matmul(cg_ref[...], dpred)
    dlr[:rows] = (dcoupled * right).astype(BF16)
    dlr[rows:] = (dcoupled * left).astype(BF16)
    moved = matmul_tn(dlr[...], wlr_ref[...]).astype(BF16)
    for q in range(GROUP):
        back_ref[q, :capacity, :] = moved[q * capacity : (q + 1) * capacity]
    high = error.astype(BF16).astype(F32)
    middle = (error - high).astype(BF16).astype(F32)
    packed = jnp.where(line == start + 2, error - high - middle, 0.0)
    packed = jnp.where(line == start + 1, middle, packed)
    packed = jnp.where(line == start, high, packed).astype(BF16)
    spelled = matmul_nt(packed, spread).astype(BF16)
    for q in range(GROUP):
        back_ref[q, capacity:, :] = spelled[q * TAIL : (q + 1) * TAIL]
    grad_ref[4 * channels : 4 * channels + 2 * rows] += matmul(dlr[...], second)


def finish_kernel(
    back_ref,
    holder_ref,
    rank_ref,
    xdst_ref,
    xsrc_ref,
    attr_ref,
    first_ref,
    pre_ref,
    mixpre_ref,
    wmix,
    before_ref,
    grad_ref,
    error_ref,
    onehot,
    dsecond,
    found,
):
    step = pl.program_id(0)
    capacity = back_ref.shape[1] - TAIL
    edges = holder_ref.shape[1]
    channels = back_ref.shape[2]
    holder = holder_ref[...]
    rank = rank_ref[...]

    @pl.when(step == 0)
    def _():
        dsecond[...] = jnp.zeros_like(dsecond)
        found[...] = jnp.zeros_like(found)

    slot_onehot(onehot, holder, rank, step * GROUP, capacity)
    rows = back_ref[:, :capacity, :].reshape(GROUP * capacity, channels)
    dsecond[...] += matmul_tn(rows, onehot[...])
    line = lax.broadcasted_iota(jnp.int32, (GROUP * TAIL, edges), 0)
    low = (holder - step * GROUP) * TAIL
    at_holder = indicator(jnp.logical_and(line >= low, line < low + TAIL))
    tails = back_ref[:, capacity:, :].reshape(GROUP * TAIL, LANES)
    found[...] += matmul_tn(tails, at_holder)

    @pl.when(step == pl.num_programs(0) - 1)
    def _():
        place = lax.broadcasted_iota(jnp.int32, found.shape, 0)
        error_ref[...] = jnp.sum(
            jnp.where(place == rank, found[...], 0.0), axis=0, keepdims=True
        )
        dsec = dsecond[...]
        mixpre = mixpre_ref[...]
        dmix = (dsec * slope(mixpre, jax.nn.sigmoid(mixpre))).astype(BF16)
        dfirst = dsec + matmul(wmix[...], dmix)
        pre = pre_ref[...]
        dpre = (dfirst * slope(pre, jax.nn.sigmoid(pre))).astype(BF16)
        grad_ref[0:channels] = matmul_nt(xdst_ref[...], dpre)
        grad_ref[channels : 2 * channels] = matmul_nt(xsrc_ref[...], dpre)
        grad_ref[2 * channels : 3 * channels] = matmul(dpre, attr_ref[...]).T
        grad_ref[3 * channels : 4 * channels] = matmul_nt(first_ref[...], dmix)


def exchange(array, axis, groups=None):
    return lax.all_to_all(
        array, axis, split_axis=0, concat_axis=0, tiled=True, axis_index_groups=groups
    )


WIDE, NARROW, DEEP = 4, 4, 8
PEERS = WIDE * NARROW
SWAP = [(i, i ^ 1) for i in range(WIDE * 2)]
PLANE = [
    [(y * 2 + c) * NARROW * DEEP + z * NARROW + x for y in range(WIDE) for x in range(NARROW)]
    for c in range(2)
    for z in range(DEEP)
]
COLUMN = [[z * NARROW + x for z in range(DEEP)] for x in range(NARROW)]


def sum_everywhere(part):
    half = part.shape[0] // 2
    core = lax.rem(lax.axis_index("rep"), 2)
    keep = lax.dynamic_slice_in_dim(part, core * half, half, 0)
    give = lax.dynamic_slice_in_dim(part, (1 - core) * half, half, 0)
    part = keep + lax.ppermute(give, "rep", SWAP)
    got = exchange(part, ("rep", "edge"), PLANE)
    part = jnp.sum(got.reshape(PEERS, half // PEERS, -1), axis=0)
    got = exchange(jnp.tile(part, (DEEP, 1)), "edge", COLUMN)
    part = jnp.sum(got.reshape(DEEP, *part.shape), axis=0)
    part = exchange(jnp.tile(part, (PEERS, 1)), ("rep", "edge"), PLANE)
    other = lax.ppermute(part, "rep", SWAP)
    low = jnp.where(core == 0, part, other)
    high = jnp.where(core == 0, other, part)
    return jnp.concatenate([low, high], axis=0)


def local(
    node_feats,
    edge_attr,
    edge_src,
    edge_dst,
    species,
    orbital_mask,
    tile_owner,
    target_send,
    w_dst,
    w_src,
    w_attr,
    w_mix,
    w_left,
    w_right,
    cg_basis,
):
    atoms, channels = node_feats.shape[1:]
    edges = edge_attr.shape[1]
    orb2, columns = target_send.shape[1:]
    devices = lax.axis_size("edge")
    capacity = columns // devices
    steps = devices // GROUP
    width = GROUP * capacity
    block = capacity + TAIL
    position = lax.axis_index("edge").astype(jnp.int32)[None]
    nodes = node_feats[0]
    node_lo = lax.ppermute(nodes, "edge", ring(devices, 1))
    node_hi = lax.ppermute(nodes, "edge", ring(devices, -1))
    attr = edge_attr[0]
    rows = -(-orb2 // 32) * 32
    holder = tile_owner.reshape(1, edges)
    params = pltpu.CompilerParams(vmem_limit_bytes=VMEM)

    def whole(shape):
        return pl.BlockSpec(shape, lambda *_: (0,) * len(shape))

    def array(shape, dtype=BF16):
        return jax.ShapeDtypeStruct(shape, dtype)

    square = whole((channels, channels))
    line = whole((1, edges))
    packets = pl.BlockSpec((GROUP, block, channels), lambda i, *_: (i, 0, 0))

    wide = whole((channels, edges))
    onehot = pltpu.VMEM((width, edges), BF16)

    def kinds_of(shift):
        return pl.BlockSpec(
            (1, atoms), lambda i, pos: (0, jnp.clip(pos[0] + shift, 0, devices - 1))
        )

    sent, rank, xdst, xsrc, first, pre, mixpre = pl.pallas_call(
        edge_kernel,
        out_shape=(
            array((devices, block, channels)),
            array((1, edges), jnp.int32),
            array((channels, edges)),
            array((channels, edges)),
            array((channels, edges)),
            array((channels, edges), F32),
            array((channels, edges), F32),
        ),
        grid_spec=pltpu.PrefetchScalarGridSpec(
            num_scalar_prefetch=1,
            grid=(steps,),
            in_specs=[line, line, line, kinds_of(-1), kinds_of(0), kinds_of(1)]
            + [whole((atoms, channels))] * 3
            + [whole((edges, channels))]
            + [square] * 4,
            out_specs=[packets, line] + [wide] * 5,
            scratch_shapes=[
                pltpu.VMEM((channels, edges), BF16),
                onehot,
                pltpu.VMEM((2 * devices, LANES), F32),
            ],
        ),
        compiler_params=params,
    )(
        position,
        edge_dst,
        edge_src,
        holder,
        species,
        species,
        species,
        node_lo,
        nodes,
        node_hi,
        attr,
        w_dst,
        w_src,
        w_attr,
        w_mix,
    )
    received = exchange(sent, "edge")

    species_count, orbs = orbital_mask.shape
    entry = np.arange(rows)[:, None]
    orbit = np.arange(orbs)[None, :]
    valid = entry < orb2
    pick_a = (valid & (entry // orbs == orbit)).astype(BF16)
    pick_b = (valid & (entry % orbs == orbit)).astype(BF16)
    code = np.arange(TAIL)[None, :]
    kind = np.arange(species_count)[:, None]
    known = code < species_count**2
    pick_dst = (known & (code // species_count == kind)).astype(BF16)
    pick_src = (known & (code % species_count == kind)).astype(BF16)
    prepared = [
        array((rows, rows)),
        array((rows, rows)),
        array((2 * rows, channels)),
        array((rows, TAIL)),
    ]
    ready = pl.pallas_call(prepare_kernel, out_shape=prepared, compiler_params=params)(
        cg_basis, w_left, w_right, orbital_mask, pick_a, pick_b, pick_dst, pick_src
    )
    cg, cg_t, wlr, pairs = ready

    slots = np.arange(width)
    places = np.stack([slots // capacity * TAIL, slots % capacity]).astype(np.int32)
    unit = 2 * PEERS * 8
    total = -(-(4 * channels + 2 * rows) // unit) * unit
    shared = (wlr, cg, cg_t, pairs, places)
    back, grads = pl.pallas_call(
        holder_kernel,
        out_shape=(array((devices, block, channels)), array((total, channels), F32)),
        grid=(steps,),
        in_specs=[
            packets,
            pl.BlockSpec((1, orb2, width), lambda i: (0, 0, i)),
            *[whole(a.shape) for a in shared],
        ],
        out_specs=[packets, whole((total, channels))],
        scratch_shapes=[pltpu.VMEM((2 * rows, width), BF16)],
        compiler_params=params,
    )(received, target_send, *shared)
    returned = exchange(back, "edge")

    grads, errors = pl.pallas_call(
        finish_kernel,
        out_shape=(array((total, channels), F32), array((1, edges), F32)),
        grid=(steps,),
        in_specs=[packets, line, line, wide, wide, whole((edges, channels))]
        + [wide, wide, wide, square, pl.BlockSpec(memory_space=pl.ANY)],
        out_specs=[whole((4 * channels, channels)), line],
        scratch_shapes=[
            onehot,
            pltpu.VMEM((channels, edges), F32),
            pltpu.VMEM((LANES, edges), F32),
        ],
        input_output_aliases={10: 0},
        compiler_params=params,
    )(returned, holder, rank, xdst, xsrc, attr, first, pre, mixpre, w_mix, grads)

    grads = sum_everywhere(grads)
    outs = [grads[i * channels : (i + 1) * channels] for i in range(4)]
    outs += [grads[4 * channels + i * rows :][:orb2] for i in range(2)]
    return (*outs, errors)


def solution(mesh):
    return jax.shard_map(
        local,
        mesh=mesh,
        in_specs=(
            P("rep", "edge", None),
            P("rep", "edge", None),
            P("rep", "edge"),
            P("rep", "edge"),
            P("rep", None),
            P(),
            P("rep", "edge", None),
            P("rep", "edge", None),
            P(),
            P(),
            P(),
            P(),
            P(),
            P(),
            P(),
        ),
        out_specs=(P(), P(), P(), P(), P(), P(), P("rep", "edge")),
        check_vma=False,
    )
```

time: 177 us -> 170 us (0.960)
  starting transfers between devices: 70.7 us -> 32.8 us
  waiting for transfers between devices: 15.5 us -> 45.4 us
  blocking collectives: 24.7 us -> 41.6 us
  Pallas kernels: 57.1 us -> 43.5 us
  other arithmetic: 3.44 us -> 1.09 us
    all_to_all x6 -> x2, starting transfers between devices: 47.9 us -> 14.8 us  [exchange(): lax.all_to_all(array, axis, split_axis=0, concat_axis=0, tiled=True, axis...]
    all_to_all x6 -> x2, waiting for transfers between devices: 9.85 us -> 40.6 us  [exchange(): lax.all_to_all(array, axis, split_axis=0, concat_axis=0, tiled=True, axis...]
    all_to_all x2 -> x3, blocking collectives: 24.7 us -> 41.6 us  [exchange(): lax.all_to_all(array, axis, split_axis=0, concat_axis=0, tiled=True, axis...]
    pallas_call x7 -> x4, Pallas kernels: 57.1 us -> 43.5 us  [the longest x1 23.3 us: local(): pl.pallas_call(holder_kernel, out_shape=(array((devices, block, channels)...]
    ppermute x3 -> x2, starting transfers between devices: 14.1 us -> 9.18 us  [the longest x1 5.07 us: sum_everywhere(): part = keep + lax.ppermute(give, 'rep', SWAP)]
    add x2 -> x1, other arithmetic: 2.38 us -> 0.06 us  [sum_everywhere(): part = keep + lax.ppermute(give, 'rep', SWAP)]
    unnamed x14 -> x10, local copies, waits for them, and re-layouts: 0.67 us -> 2.54 us
    ppermute x3 -> x2, waiting for transfers between devices: 3.87 us -> 3.07 us  [the longest x1 1.54 us: sum_everywhere(): part = keep + lax.ppermute(give, 'rep', SWAP)]
  transfers between devices with their start and end apart: 11 -> 6, of which waited for: 7 -> 5; matrix products, arithmetic and copies ran while one was open for 2% -> 0% of each run, Pallas kernels for 29% -> 2%
where the time goes in v4:
time: 170 us; the launch traced here: 169 us
  waiting for transfers between devices  45.4 us (27%)
  Pallas kernels  43.5 us (26%)
  blocking collectives  41.6 us (24%)
  starting transfers between devices  32.8 us (19%)
  local copies, waits for them, and re-layouts  4.47 us (3%)
    all_to_all x3, blocking collectives, exchange(): lax.all_to_all(array, axis, split_axis=0, concat_axis=0, tiled=True, axis...  41.6 us
    all_to_all x2, waiting for transfers between devices, exchange(): lax.all_to_all(array, axis, split_axis=0, concat_axis=0, tiled=True, axis...  40.6 us
    pallas_call x1, Pallas kernels, local(): pl.pallas_call(holder_kernel, out_shape=(array((devices, block, channels)...  23.3 us
    all_to_all x2, starting transfers between devices, exchange(): lax.all_to_all(array, axis, split_axis=0, concat_axis=0, tiled=True, axis...  14.8 us
    pallas_call x1, Pallas kernels, local(): pl.pallas_call(finish_kernel, out_shape=(array((total, channels), F32), a...  8.51 us
    pallas_call x1, Pallas kernels, local(): pl.pallas_call(edge_kernel, out_shape=(array((devices, block, channels)),...  8.25 us
    ppermute x1, starting transfers between devices, local(): node_hi = lax.ppermute(nodes, 'edge', ring(devices, -1))  6.65 us
    ppermute x1, starting transfers between devices, sum_everywhere(): part = keep + lax.ppermute(give, 'rep', SWAP)  5.07 us
  transfers between devices with their start and end apart: 6, of which 5 were waited for; matrix products, arithmetic and copies ran while one was open for 0% of the time, Pallas kernels for 2%

profile of v4, /device:TPU:1, one launch (start us, length us, event | category | flops | bytes accessed | tf_op | source)
XLA Modules:
  0.0 169.5 jit_solution(9072669715692260002)
XLA Ops:
  0.6 2.1 %collective-permute-start = (bf16[256,128]{1,0:T(8,128)(2,1)}, bf16[256,128]{1,0:T(8,128)(2,1)S(1)}, u32[]{:S(2)}, u32[]{:S(2)}) collective-permute-start(bf16[256,128]{1,0:T(8,128)(2,1)} %bitcast.12), channel_id=1, source_target_pairs={{0,1},{1,2},{2,3},{3,4},{4,5},{5,6},{6,7},{7,8},{8,9},{9,10},{10,1... | collective-permute-start | bytes 196616 | tf_op jit(solution)/shard_map/ppermute | solution.py:363
  2.8 6.6 %collective-permute-start.1 = (bf16[256,128]{1,0:T(8,128)(2,1)}, bf16[256,128]{1,0:T(8,128)(2,1)S(1)}, u32[]{:S(2)}, u32[]{:S(2)}) collective-permute-start(bf16[256,128]{1,0:T(8,128)(2,1)} %bitcast.13), channel_id=1, source_target_pairs={{0,31},{1,0},{2,1},{3,2},{4,3},{5,4},{6,5},{7,6},{8,7},{9,8},{10,9... | collective-permute-start | bytes 196616 | tf_op jit(solution)/shard_map/ppermute | solution.py:364
  9.4 1.8 %collective-permute-done.node_lo = bf16[256,128]{1,0:T(8,128)(2,1)S(1)} collective-permute-done((bf16[256,128]{1,0:T(8,128)(2,1)}, bf16[256,128]{1,0:T(8,128)(2,1)S(1)}, u32[]{:S(2)}, u32[]{:S(2)}) %collective-permute-start) | collective-permute-done | bytes 65568 | tf_op jit(solution)/shard_map/ppermute | solution.py:363
  11.2 0.0 copy-start.3
  11.2 0.0 collective-permute-done.1.node_hi
  11.2 0.0 copy-start.4
  11.2 0.6 copy-done.3
  11.8 0.0 copy-done.4
  11.8 8.3 %shard_map.243 = (bf16[32,112,128]{2,1,0:T(8,128)(2,1)}, s32[1,2048]{1,0:T(1,128)}, bf16[128,2048]{1,0:T(8,128)(2,1)}, bf16[128,2048]{1,0:T(8,128)(2,1)}, bf16[1...) custom-call(s32[1]{0:T(128)} %bitcast.pos_ref, s32[1,2048]{1,0:T(1,128)} %dst_ref.1, ...), custom_call_target="tpu_custom_call" | custom-call | tf_op jit(solution)/shard_map/pallas_call | solution.py:388
  20.1 7.9 %all-to-all-start = ((bf16[32,112,128]{2,1,0:T(8,128)(2,1)}), bf16[32,112,128]{2,1,0:T(8,128)(2,1)S(1)}, u32[]{:S(2)}, u32[]{:S(2)}) async-start(bf16[32,112,128]{2,1,0:T(8,128)(2,1)} %get-tuple-element.22), calls=%async_computation | async-start | bytes 1835008 | tf_op jit(solution)/shard_map/all_to_all | solution.py:303
  28.0 3.4 %shard_map.244 = (bf16[736,736]{1,0:T(8,128)(2,1)}, bf16[736,736]{1,0:T(8,128)(2,1)}, bf16[1472,128]{1,0:T(8,128)(2,1)}, bf16[736,16]{1,0:T(8,128)(2,1)}) custom-call(bf16[729,729]{1,0:T(8,128)(2,1)} %cg_ref.1, bf16[729,128]{1,0:T(8,128)(2,1)} %wleft_ref.1, bf16[729,128]{1,0:T(8,128)(2,1)} %wright_ref.1, s32[3,27]{1,0:T(4,128)} %mask_ref.1, ...), custom_call_target="tpu_custom_call" | custom-call | tf_op jit(solution)/shard_map/pallas_call | solution.py:450
  31.4 18.7 %all-to-all-done.recv_ref = bf16[32,112,128]{2,1,0:T(8,128)(2,1)S(1)} async-done(((bf16[32,112,128]{2,1,0:T(8,128)(2,1)}), bf16[32,112,128]{2,1,0:T(8,128)(2,1)S(1)}, u32[]{:S(2)}, u32[]{:S(2)}) %all-to-all-start) | async-done | bytes 917536 | tf_op jit(solution)/shard_map/all_to_all | solution.py:303
  50.2 0.0 copy-start.1
  50.2 1.0 copy-done.1
  51.1 23.3 %shard_map.245 = (bf16[32,112,128]{2,1,0:T(8,128)(2,1)}, f32[2048,128]{1,0:T(8,128)}) custom-call(bf16[32,112,128]{2,1,0:T(8,128)(2,1)} %copy-done.1, bf16[1,729,3072]{2,1,0:T(8,128)(2,1)} %target_ref.1, bf16[1472,128]{1,0:T(8,128)(2,1)} %get-tuple-element.23.wlr_ref, bf16[736,736]{1,0:T(8,128)(2,1)} %get-tuple-element.24.cg_ref, ...), custom_call_target="tpu_custom_call" | custom-call | tf_op jit(solution)/shard_map/pallas_call | solution.py:460
  74.4 6.9 %all-to-all-start.1 = ((bf16[32,112,128]{2,1,0:T(8,128)(2,1)}), bf16[32,112,128]{2,1,0:T(8,128)(2,1)S(1)}, u32[]{:S(2)}, u32[]{:S(2)}) async-start(bf16[32,112,128]{2,1,0:T(8,128)(2,1)} %get-tuple-element.27), calls=%async_computation.1 | async-start | bytes 1835008 | tf_op jit(solution)/shard_map/all_to_all | solution.py:303
  81.3 21.8 %all-to-all-done.1.back_ref = bf16[32,112,128]{2,1,0:T(8,128)(2,1)S(1)} async-done(((bf16[32,112,128]{2,1,0:T(8,128)(2,1)}), bf16[32,112,128]{2,1,0:T(8,128)(2,1)S(1)}, u32[]{:S(2)}, u32[]{:S(2)}) %all-to-all-start.1) | async-done | bytes 917536 | tf_op jit(solution)/shard_map/all_to_all | solution.py:303
  103.1 0.0 copy-start.2
  103.1 0.9 copy-done.2
  104.1 8.5 %shard_map.246 = (f32[2048,128]{1,0:T(8,128)}, f32[1,2048]{1,0:T(1,128)}) custom-call(bf16[32,112,128]{2,1,0:T(8,128)(2,1)} %copy-done.2, s32[1,2048]{1,0:T(1,128)} %bitcast.16, s32[1,2048]{1,0:T(1,128)} %get-tuple-element.28.rank_ref, bf16[128,2048]{1,0:T(8,128)(2,1)} %get-tuple-element.29.xdst_ref, ...), custom_call_target="tpu_custom_call", output_to_operand_aliasing={{0}: (10, {})} | custom-call | tf_op jit(solution)/shard_map/pallas_call | solution.py:475
  112.6 0.0 copy-start
  112.6 1.2 constant_dynamic-slice_fusion
  113.8 5.1 %collective-permute-start.2 = (f32[1024,128]{1,0:T(8,128)S(1)}, f32[1024,128]{1,0:T(8,128)S(1)}, u32[]{:S(2)}, u32[]{:S(2)}) collective-permute-start(f32[1024,128]{1,0:T(8,128)S(1)} %constant_dynamic-slice_fusion), channel_id=1, source_target_pairs={{0,32},{32,0},{64,96},{96,64},{128,160},{160,128},{192,224},{224,1... | collective-permute-start | bytes 1572872 | tf_op jit(solution)/shard_map/ppermute | solution.py:324
  118.8 1.5 collective-permute-done.2
  120.4 0.0 copy-done
  120.4 0.1 dynamic-slice_add_fusion
  120.4 16.8 %all_to_all.34 = f32[16,64,128]{2,1,0:T(8,128)S(1)} all-to-all(f32[16,64,128]{2,1,0:T(8,128)S(1)} %bitcast.11), channel_id=1, replica_groups={{0,1,2,3,64,65,66,67,128,129,130,131,192,193,194,195},{4,5,6,7,68,69,70..., dimensions={0} | all-to-all | bytes 1048576 | tf_op jit(solution)/shard_map/all_to_all | solution.py:303
  137.3 11.9 %all_to_all.35 = f32[8,64,128]{2,1,0:T(8,128)S(1)} all-to-all(f32[8,64,128]{2,1,0:T(8,128)S(1)} %tile.4), channel_id=1, replica_groups={{0,4,8,12,16,20,24,28},{1,5,9,13,17,21,25,29},{2,6,10,14,18,22,26,30},{..., dimensions={0} | all-to-all | bytes 524288 | tf_op jit(solution)/shard_map/all_to_all | solution.py:303
  149.3 12.9 %all_to_all.36 = f32[16,64,128]{2,1,0:T(8,128)S(1)} all-to-all(f32[16,64,128]{2,1,0:T(8,128)S(1)} %tile.5), channel_id=1, replica_groups={{0,1,2,3,64,65,66,67,128,129,130,131,192,193,194,195},{4,5,6,7,68,69,70..., dimensions={0} | all-to-all | bytes 1048576 | tf_op jit(solution)/shard_map/all_to_all | solution.py:303
  162.2 4.1 %collective-permute-start.3 = (f32[1024,128]{1,0:T(8,128)S(1)}, f32[1024,128]{1,0:T(8,128)S(1)}, u32[]{:S(2)}, u32[]{:S(2)}) collective-permute-start(f32[1024,128]{1,0:T(8,128)S(1)} %bitcast.10), channel_id=1, source_target_pairs={{0,32},{32,0},{64,96},{96,64},{128,160},{160,128},{192,224},{224,1... | collective-permute-start | bytes 1572872 | tf_op jit(solution)/shard_map/ppermute | solution.py:330
  166.3 1.5 collective-permute-done.3
  167.8 0.1 broadcast_select_fusion
  167.9 0.7 fusion.1
  168.6 0.9 fusion
  (4 shorter events, 0.1 us)
Async XLA Ops:
  0.6 10.5 %collective-permute-start = (bf16[256,128]{1,0:T(8,128)(2,1)}, bf16[256,128]{1,0:T(8,128)(2,1)S(1)}, u32[]{:S(2)}, u32[]{:S(2)}) collective-permute-start(bf16[256,128]{1,0:T(8,128)(2,1)} %bitcast.12), channel_id=1, source_target_pairs={{0,1},{1,2},{2,3},{3,4},{4,5},{5,6},{6,7},{7,8},{8,9},{9,10},{10,1... | collective-permute-start | bytes 196616 | tf_op jit(solution)/shard_map/ppermute | solution.py:363
  2.8 8.4 %collective-permute-start.1 = (bf16[256,128]{1,0:T(8,128)(2,1)}, bf16[256,128]{1,0:T(8,128)(2,1)S(1)}, u32[]{:S(2)}, u32[]{:S(2)}) collective-permute-start(bf16[256,128]{1,0:T(8,128)(2,1)} %bitcast.13), channel_id=1, source_target_pairs={{0,31},{1,0},{2,1},{3,2},{4,3},{5,4},{6,5},{7,6},{8,7},{9,8},{10,9... | collective-permute-start | bytes 196616 | tf_op jit(solution)/shard_map/ppermute | solution.py:364
  11.2 0.6 copy-start.3
  11.2 0.6 copy-start.4
  20.1 30.1 %all-to-all-start = ((bf16[32,112,128]{2,1,0:T(8,128)(2,1)}), bf16[32,112,128]{2,1,0:T(8,128)(2,1)S(1)}, u32[]{:S(2)}, u32[]{:S(2)}) async-start(bf16[32,112,128]{2,1,0:T(8,128)(2,1)} %get-tuple-element.22), calls=%async_computation | async-start | bytes 1835008 | tf_op jit(solution)/shard_map/all_to_all | solution.py:303
  50.2 1.0 copy-start.1
  74.4 28.7 %all-to-all-start.1 = ((bf16[32,112,128]{2,1,0:T(8,128)(2,1)}), bf16[32,112,128]{2,1,0:T(8,128)(2,1)S(1)}, u32[]{:S(2)}, u32[]{:S(2)}) async-start(bf16[32,112,128]{2,1,0:T(8,128)(2,1)} %get-tuple-element.27), calls=%async_computation.1 | async-start | bytes 1835008 | tf_op jit(solution)/shard_map/all_to_all | solution.py:303
  103.1 0.9 copy-start.2
  112.6 7.8 %copy-start = (f32[2048,128]{1,0:T(8,128)S(1)}, f32[2048,128]{1,0:T(8,128)}, u32[]{:S(2)}) copy-start(f32[2048,128]{1,0:T(8,128)} %get-tuple-element.35) | copy-start | bytes 3145732
  113.8 6.6 %collective-permute-start.2 = (f32[1024,128]{1,0:T(8,128)S(1)}, f32[1024,128]{1,0:T(8,128)S(1)}, u32[]{:S(2)}, u32[]{:S(2)}) collective-permute-start(f32[1024,128]{1,0:T(8,128)S(1)} %constant_dynamic-slice_fusion), channel_id=1, source_target_pairs={{0,32},{32,0},{64,96},{96,64},{128,160},{160,128},{192,224},{224,1... | collective-permute-start | bytes 1572872 | tf_op jit(solution)/shard_map/ppermute | solution.py:324
  162.2 5.6 %collective-permute-start.3 = (f32[1024,128]{1,0:T(8,128)S(1)}, f32[1024,128]{1,0:T(8,128)S(1)}, u32[]{:S(2)}, u32[]{:S(2)}) collective-permute-start(f32[1024,128]{1,0:T(8,128)S(1)} %bitcast.10), channel_id=1, source_target_pairs={{0,32},{32,0},{64,96},{96,64},{128,160},{160,128},{192,224},{224,1... | collective-permute-start | bytes 1572872 | tf_op jit(solution)/shard_map/ppermute | solution.py:330

commit v5 on v4

--- a/solution.py
+++ b/solution.py
@@ -11,6 +11,7 @@
 F32 = jnp.float32
 BF16 = jnp.bfloat16
 GROUP = 8
+EDGE_GROUP = 16
 TAIL = 16
 LANES = 128
 CHUNK = 256
@@ -42,11 +43,18 @@
     return sigma * (1.0 + value * (1.0 - sigma))
 
 
+def layers(xdst, xsrc, attr_ref, w_dst, w_src, w_attr, w_mix):
+    pre = matmul(w_dst[...].T, xdst) + matmul(w_src[...].T, xsrc)
+    pre = pre + matmul_nt(w_attr[...].T, attr_ref[...])
+    first = (pre * jax.nn.sigmoid(pre)).astype(BF16)
+    return pre, first, matmul(w_mix[...].T, first)
+
+
 def slot_onehot(out, holder, rank, base, capacity):
     edges = holder.shape[1]
     place = lax.broadcasted_iota(jnp.int32, (capacity, edges), 0).astype(BF16)
     one = jnp.ones((capacity, edges), BF16)
-    for p in range(GROUP):
+    for p in range(EDGE_GROUP):
         mine = jnp.where(holder == base + p, rank, -1).astype(BF16)
         out[p * capacity : (p + 1) * capacity, :] = jnp.where(place == mine, one, 0.0)
 
@@ -71,9 +79,6 @@
     rank_ref,
     xdst_ref,
     xsrc_ref,
-    first_ref,
-    pre_ref,
-    mixpre_ref,
     second_ref,
     onehot,
     tags,
@@ -121,13 +126,7 @@
         xsrc = from_src[:channels].astype(BF16)
         xdst_ref[...] = xdst
         xsrc_ref[...] = xsrc
-        pre = matmul(w_dst[...].T, xdst) + matmul(w_src[...].T, xsrc)
-        pre = pre + matmul_nt(w_attr[...].T, attr_ref[...])
-        pre_ref[...] = pre
-        first = (pre * jax.nn.sigmoid(pre)).astype(BF16)
-        first_ref[...] = first
-        mixpre = matmul(w_mix[...].T, first)
-        mixpre_ref[...] = mixpre
+        _, first, mixpre = layers(xdst, xsrc, attr_ref, w_dst, w_src, w_attr, w_mix)
         second_ref[...] = (first.astype(F32) + mixpre * jax.nn.sigmoid(mixpre)).astype(BF16)
         tagged = jnp.concatenate(
             [named * from_dst[channels : channels + 1], named * from_src[channels : channels + 1]],
@@ -136,13 +135,13 @@
         at_rank = indicator(lax.broadcasted_iota(jnp.int32, (LANES, edges), 0) == rank)
         tags[...] = matmul_nt(tagged, at_rank)
 
-    slot_onehot(onehot, holder, rank_ref[...], step * GROUP, capacity)
+    slot_onehot(onehot, holder, rank_ref[...], step * EDGE_GROUP, capacity)
     moved = matmul_nt(onehot[...], second_ref[...]).astype(BF16)
     line = lax.broadcasted_iota(jnp.int32, (TAIL, LANES), 0)
-    for p in range(GROUP):
+    for p in range(EDGE_GROUP):
         out_ref[p, :capacity, :] = moved[p * capacity : (p + 1) * capacity]
-        tag_dst = tags[pl.ds(step * GROUP + p, 1), :]
-        tag_src = tags[pl.ds(devices + step * GROUP + p, 1), :]
+        tag_dst = tags[pl.ds(step * EDGE_GROUP + p, 1), :]
+        tag_src = tags[pl.ds(devices + step * EDGE_GROUP + p, 1), :]
         tail = jnp.where(line == 0, tag_dst, jnp.where(line == 1, tag_src, 0.0))
         out_ref[p, capacity:, :] = tail.astype(BF16)
 
@@ -159,6 +158,7 @@
     cg_out,
     cg_t,
     wlr_out,
+    wlr_t,
     pairs_ref,
 ):
     rows = cg_out.shape[0]
@@ -174,6 +174,7 @@
     cg_t[...] = across.T.astype(BF16)
     both = jnp.concatenate([pad_rows(wleft_ref[...]), pad_rows(wright_ref[...])], axis=0)
     wlr_out[...] = both.astype(BF16)
+    wlr_t[...] = both.T.astype(BF16)
     carried = mask_ref[...].astype(F32).astype(BF16)
     dst = matmul_tn(carried, pick_dst[...]).astype(BF16)
     src = matmul_tn(carried, pick_src[...]).astype(BF16)
@@ -184,6 +185,7 @@
     recv_ref,
     target_ref,
     wlr_ref,
+    wlr_t,
     cg_ref,
     cg_t,
     pairs_ref,
@@ -228,7 +230,8 @@
     dcoupled = matmul(cg_ref[...], dpred)
     dlr[:rows] = (dcoupled * right).astype(BF16)
     dlr[rows:] = (dcoupled * left).astype(BF16)
-    moved = matmul_tn(dlr[...], wlr_ref[...]).astype(BF16)
+    grad_ref[4 * channels : 4 * channels + 2 * rows] += matmul(dlr[...], second)
+    moved = matmul(wlr_t[...], dlr[...]).T.astype(BF16)
     for q in range(GROUP):
         back_ref[q, :capacity, :] = moved[q * capacity : (q + 1) * capacity]
     high = error.astype(BF16).astype(F32)
@@ -239,26 +242,29 @@
     spelled = matmul_nt(packed, spread).astype(BF16)
     for q in range(GROUP):
         back_ref[q, capacity:, :] = spelled[q * TAIL : (q + 1) * TAIL]
-    grad_ref[4 * channels : 4 * channels + 2 * rows] += matmul(dlr[...], second)
 
 
 def finish_kernel(
     back_ref,
     holder_ref,
     rank_ref,
-    xdst_ref,
-    xsrc_ref,
-    attr_ref,
-    first_ref,
-    pre_ref,
-    mixpre_ref,
-    wmix,
+    xdst_hbm,
+    xsrc_hbm,
+    attr_hbm,
+    w_dst,
+    w_src,
+    w_attr,
+    w_mix,
     before_ref,
     grad_ref,
     error_ref,
     onehot,
     dsecond,
     found,
+    xdst_ref,
+    xsrc_ref,
+    attr_ref,
+    sems,
 ):
     step = pl.program_id(0)
     capacity = back_ref.shape[1] - TAIL
@@ -267,36 +273,47 @@
     holder = holder_ref[...]
     rank = rank_ref[...]
 
+    wanted = ((xdst_hbm, xdst_ref), (xsrc_hbm, xsrc_ref), (attr_hbm, attr_ref))
+    loads = [
+        pltpu.make_async_copy(source, kept, sems.at[i])
+        for i, (source, kept) in enumerate(wanted)
+    ]
+
     @pl.when(step == 0)
     def _():
+        for load in loads:
+            load.start()
         dsecond[...] = jnp.zeros_like(dsecond)
         found[...] = jnp.zeros_like(found)
 
-    slot_onehot(onehot, holder, rank, step * GROUP, capacity)
-    rows = back_ref[:, :capacity, :].reshape(GROUP * capacity, channels)
+    slot_onehot(onehot, holder, rank, step * EDGE_GROUP, capacity)
+    rows = back_ref[:, :capacity, :].reshape(EDGE_GROUP * capacity, channels)
     dsecond[...] += matmul_tn(rows, onehot[...])
-    line = lax.broadcasted_iota(jnp.int32, (GROUP * TAIL, edges), 0)
-    low = (holder - step * GROUP) * TAIL
+    line = lax.broadcasted_iota(jnp.int32, (EDGE_GROUP * TAIL, edges), 0)
+    low = (holder - step * EDGE_GROUP) * TAIL
     at_holder = indicator(jnp.logical_and(line >= low, line < low + TAIL))
-    tails = back_ref[:, capacity:, :].reshape(GROUP * TAIL, LANES)
+    tails = back_ref[:, capacity:, :].reshape(EDGE_GROUP * TAIL, LANES)
     found[...] += matmul_tn(tails, at_holder)
 
     @pl.when(step == pl.num_programs(0) - 1)
     def _():
+        for load in loads:
+            load.wait()
         place = lax.broadcasted_iota(jnp.int32, found.shape, 0)
         error_ref[...] = jnp.sum(
             jnp.where(place == rank, found[...], 0.0), axis=0, keepdims=True
         )
         dsec = dsecond[...]
-        mixpre = mixpre_ref[...]
+        pre, first, mixpre = layers(
+            xdst_ref[...], xsrc_ref[...], attr_ref, w_dst, w_src, w_attr, w_mix
+        )
         dmix = (dsec * slope(mixpre, jax.nn.sigmoid(mixpre))).astype(BF16)
-        dfirst = dsec + matmul(wmix[...], dmix)
-        pre = pre_ref[...]
+        dfirst = dsec + matmul(w_mix[...], dmix)
         dpre = (dfirst * slope(pre, jax.nn.sigmoid(pre))).astype(BF16)
         grad_ref[0:channels] = matmul_nt(xdst_ref[...], dpre)
         grad_ref[channels : 2 * channels] = matmul_nt(xsrc_ref[...], dpre)
         grad_ref[2 * channels : 3 * channels] = matmul(dpre, attr_ref[...]).T
-        grad_ref[3 * channels : 4 * channels] = matmul_nt(first_ref[...], dmix)
+        grad_ref[3 * channels : 4 * channels] = matmul_nt(first, dmix)
 
 
 def exchange(array, axis, groups=None):
@@ -376,34 +393,33 @@
     square = whole((channels, channels))
     line = whole((1, edges))
     packets = pl.BlockSpec((GROUP, block, channels), lambda i, *_: (i, 0, 0))
+    edge_packets = pl.BlockSpec((EDGE_GROUP, block, channels), lambda i, *_: (i, 0, 0))
 
     wide = whole((channels, edges))
-    onehot = pltpu.VMEM((width, edges), BF16)
+    edge_steps = devices // EDGE_GROUP
+    onehot = pltpu.VMEM((EDGE_GROUP * capacity, edges), BF16)
 
     def kinds_of(shift):
         return pl.BlockSpec(
             (1, atoms), lambda i, pos: (0, jnp.clip(pos[0] + shift, 0, devices - 1))
         )
 
-    sent, rank, xdst, xsrc, first, pre, mixpre = pl.pallas_call(
+    sent, rank, xdst, xsrc = pl.pallas_call(
         edge_kernel,
         out_shape=(
             array((devices, block, channels)),
             array((1, edges), jnp.int32),
             array((channels, edges)),
             array((channels, edges)),
-            array((channels, edges)),
-            array((channels, edges), F32),
-            array((channels, edges), F32),
         ),
         grid_spec=pltpu.PrefetchScalarGridSpec(
             num_scalar_prefetch=1,
-            grid=(steps,),
+            grid=(edge_steps,),
             in_specs=[line, line, line, kinds_of(-1), kinds_of(0), kinds_of(1)]
             + [whole((atoms, channels))] * 3
             + [whole((edges, channels))]
             + [square] * 4,
-            out_specs=[packets, line] + [wide] * 5,
+            out_specs=[edge_packets, line] + [wide] * 2,
             scratch_shapes=[
                 pltpu.VMEM((channels, edges), BF16),
                 onehot,
@@ -445,18 +461,19 @@
         array((rows, rows)),
         array((rows, rows)),
         array((2 * rows, channels)),
+        array((channels, 2 * rows)),
         array((rows, TAIL)),
     ]
-    ready = pl.pallas_call(prepare_kernel, out_shape=prepared, compiler_params=params)(
+    ready = pl.pallas_call(prepare_kernel, out_shape=prepared, compiler_params=pltpu.CompilerParams(vmem_limit_bytes=24 << 20))(
         cg_basis, w_left, w_right, orbital_mask, pick_a, pick_b, pick_dst, pick_src
     )
-    cg, cg_t, wlr, pairs = ready
+    cg, cg_t, wlr, wlr_t, pairs = ready
 
     slots = np.arange(width)
     places = np.stack([slots // capacity * TAIL, slots % capacity]).astype(np.int32)
     unit = 2 * PEERS * 8
     total = -(-(4 * channels + 2 * rows) // unit) * unit
-    shared = (wlr, cg, cg_t, pairs, places)
+    shared = (wlr, wlr_t, cg, cg_t, pairs, places)
     back, grads = pl.pallas_call(
         holder_kernel,
         out_shape=(array((devices, block, channels)), array((total, channels), F32)),
@@ -468,25 +485,31 @@
         ],
         out_specs=[packets, whole((total, channels))],
         scratch_shapes=[pltpu.VMEM((2 * rows, width), BF16)],
-        compiler_params=params,
+        compiler_params=pltpu.CompilerParams(vmem_limit_bytes=52 << 20),
     )(received, target_send, *shared)
     returned = exchange(back, "edge")
 
     grads, errors = pl.pallas_call(
         finish_kernel,
         out_shape=(array((total, channels), F32), array((1, edges), F32)),
-        grid=(steps,),
-        in_specs=[packets, line, line, wide, wide, whole((edges, channels))]
-        + [wide, wide, wide, square, pl.BlockSpec(memory_space=pl.ANY)],
+        grid=(edge_steps,),
+        in_specs=[edge_packets, line, line]
+        + [pl.BlockSpec(memory_space=pl.ANY)] * 3
+        + [square] * 4
+        + [pl.BlockSpec(memory_space=pl.ANY)],
         out_specs=[whole((4 * channels, channels)), line],
         scratch_shapes=[
             onehot,
             pltpu.VMEM((channels, edges), F32),
             pltpu.VMEM((LANES, edges), F32),
+            pltpu.VMEM((channels, edges), BF16),
+            pltpu.VMEM((channels, edges), BF16),
+            pltpu.VMEM((edges, channels), BF16),
+            pltpu.SemaphoreType.DMA((3,)),
         ],
         input_output_aliases={10: 0},
         compiler_params=params,
-    )(returned, holder, rank, xdst, xsrc, attr, first, pre, mixpre, w_mix, grads)
+    )(returned, holder, rank, xdst, xsrc, attr, w_dst, w_src, w_attr, w_mix, grads)
 
     grads = sum_everywhere(grads)
     outs = [grads[i * channels : (i + 1) * channels] for i in range(4)]

time: 170 us -> 164 us (0.965)
  Pallas kernels: 43.5 us -> 35 us
    pallas_call x1, Pallas kernels: 23.3 us -> 19.4 us  [local(): pl.pallas_call(holder_kernel, out_shape=(array((devices, block, channels)...]
    pallas_call x1, Pallas kernels: 3.43 us -> 0.69 us  [local(): pl.pallas_call(prepare_kernel, out_shape=prepared, compiler_params=pltpu....]
    unnamed x10 -> x30, local copies, waits for them, and re-layouts: 2.54 us -> 3.65 us
  transfers between devices with their start and end apart: 6 -> 6, of which waited for: 5 -> 5; matrix products, arithmetic and copies ran while one was open for 0% -> 0% of each run, Pallas kernels for 2% -> 0%
where the time goes in v5:
time: 164 us; the launch traced here: 163 us
  waiting for transfers between devices  46 us (28%)
  blocking collectives  41.6 us (25%)
  Pallas kernels  35 us (21%)
  starting transfers between devices  33.1 us (20%)
  local copies, waits for them, and re-layouts  5.58 us (3%)
    all_to_all x3, blocking collectives, exchange(): lax.all_to_all(array, axis, split_axis=0, concat_axis=0, tiled=True, axis...  41.6 us
    all_to_all x2, waiting for transfers between devices, exchange(): lax.all_to_all(array, axis, split_axis=0, concat_axis=0, tiled=True, axis...  41.2 us
    pallas_call x1, Pallas kernels, local(): pl.pallas_call(holder_kernel, out_shape=(array((devices, block, channels)...  19.4 us
    all_to_all x2, starting transfers between devices, exchange(): lax.all_to_all(array, axis, split_axis=0, concat_axis=0, tiled=True, axis...  15.1 us
    pallas_call x1, Pallas kernels, local(): pl.pallas_call(edge_kernel, out_shape=(array((devices, block, channels)),...  7.77 us
    pallas_call x1, Pallas kernels, local(): pl.pallas_call(finish_kernel, out_shape=(array((total, channels), F32), a...  7.08 us
    ppermute x1, starting transfers between devices, local(): node_hi = lax.ppermute(nodes, 'edge', ring(devices, -1))  6.65 us
    ppermute x1, starting transfers between devices, sum_everywhere(): part = keep + lax.ppermute(give, 'rep', SWAP)  5.08 us
  transfers between devices with their start and end apart: 6, of which 5 were waited for; matrix products, arithmetic and copies ran while one was open for 0% of the time, Pallas kernels for 0%

profile of v5, /device:TPU:1, one launch (start us, length us, event | category | flops | bytes accessed | tf_op | source)
XLA Modules:
  0.0 163.2 jit_solution(6168531939443433289)
XLA Ops:
  0.6 2.1 %collective-permute-start = (bf16[256,128]{1,0:T(8,128)(2,1)}, bf16[256,128]{1,0:T(8,128)(2,1)S(1)}, u32[]{:S(2)}, u32[]{:S(2)}) collective-permute-start(bf16[256,128]{1,0:T(8,128)(2,1)} %bitcast.12), channel_id=1, source_target_pairs={{0,1},{1,2},{2,3},{3,4},{4,5},{5,6},{6,7},{7,8},{8,9},{9,10},{10,1... | collective-permute-start | bytes 196616 | tf_op jit(solution)/shard_map/ppermute | solution.py:380
  2.8 6.6 %collective-permute-start.1 = (bf16[256,128]{1,0:T(8,128)(2,1)}, bf16[256,128]{1,0:T(8,128)(2,1)S(1)}, u32[]{:S(2)}, u32[]{:S(2)}) collective-permute-start(bf16[256,128]{1,0:T(8,128)(2,1)} %bitcast.13), channel_id=1, source_target_pairs={{0,31},{1,0},{2,1},{3,2},{4,3},{5,4},{6,5},{7,6},{8,7},{9,8},{10,9... | collective-permute-start | bytes 196616 | tf_op jit(solution)/shard_map/ppermute | solution.py:381
  9.4 1.8 %collective-permute-done.node_lo = bf16[256,128]{1,0:T(8,128)(2,1)S(1)} collective-permute-done((bf16[256,128]{1,0:T(8,128)(2,1)}, bf16[256,128]{1,0:T(8,128)(2,1)S(1)}, u32[]{:S(2)}, u32[]{:S(2)}) %collective-permute-start) | collective-permute-done | bytes 65568 | tf_op jit(solution)/shard_map/ppermute | solution.py:380
  11.2 0.0 copy-start.13
  11.2 0.0 collective-permute-done.1.node_hi
  11.2 0.0 copy-start.14
  11.2 0.6 copy-done.13
  11.8 0.0 copy-done.14
  11.8 0.0 copy-start.6
  11.8 7.8 %shard_map.243 = (bf16[32,112,128]{2,1,0:T(8,128)(2,1)}, s32[1,2048]{1,0:T(1,128)}, bf16[128,2048]{1,0:T(8,128)(2,1)}, bf16[128,2048]{1,0:T(8,128)(2,1)}) custom-call(s32[1]{0:T(128)} %bitcast.pos_ref, s32[1,2048]{1,0:T(1,128)} %dst_ref.1, s32[1,2048]{1,0:T(1,128)} %src_ref.1, s32[1,2048]{1,0:T(1,128)} %bitcast.15, s32[1,8192]{1,0:T(1,128)} %spec_hi.1, ...), custom_call_target="tpu_custom_call" | custom-call | tf_op jit(solution)/shard_map/pallas_call | solution.py:407
  19.6 0.0 copy-start.2
  19.6 0.0 copy-start.3
  19.6 0.0 copy-start.4
  19.6 0.0 copy-start.5
  19.6 0.0 copy-start.8
  19.6 0.0 copy-start.9
  19.7 0.0 copy-start.10
  19.7 8.2 %all-to-all-start = ((bf16[32,112,128]{2,1,0:T(8,128)(2,1)}), bf16[32,112,128]{2,1,0:T(8,128)(2,1)}, u32[]{:S(2)}, u32[]{:S(2)}) async-start(bf16[32,112,128]{2,1,0:T(8,128)(2,1)} %get-tuple-element.20), calls=%async_computation | async-start | bytes 1835008 | tf_op jit(solution)/shard_map/all_to_all | solution.py:320
  27.9 0.0 copy-done.6
  27.9 0.0 copy-done.2
  27.9 0.0 copy-done.3
  27.9 0.0 copy-done.4
  27.9 0.0 copy-done.5
  27.9 0.0 copy-done.8
  28.0 0.0 copy-done.9
  28.0 0.0 copy-done.10
  28.0 0.0 copy-start.7
  28.0 0.7 shard_map.244
  28.7 0.0 copy-start
  28.7 1.0 copy-done
  29.7 0.0 copy-start.1
  29.7 1.0 copy-done.1
  30.7 19.4 %all-to-all-done.recv_ref = bf16[32,112,128]{2,1,0:T(8,128)(2,1)} async-done(((bf16[32,112,128]{2,1,0:T(8,128)(2,1)}), bf16[32,112,128]{2,1,0:T(8,128)(2,1)}, u32[]{:S(2)}, u32[]{:S(2)}) %all-to-all-start) | async-done | bytes 917536 | tf_op jit(solution)/shard_map/all_to_all | solution.py:320
  50.1 0.0 copy-done.7
  50.1 19.4 %shard_map.245 = (bf16[32,112,128]{2,1,0:T(8,128)(2,1)}, f32[2048,128]{1,0:T(8,128)}) custom-call(bf16[32,112,128]{2,1,0:T(8,128)(2,1)} %all-to-all-done.recv_ref, bf16[1,729,3072]{2,1,0:T(8,128)(2,1)} %target_ref.1, bf16[1472,128]{1,0:T(8,128)(2,1)S(1)} %get-tuple-element.21.wlr_ref, bf16[128,1472]{1,0:T(8,128)(2,1)S(1)} %get-tuple-element.22.wlr_t, ...), custom_call_target="tpu_custom_call" | custom-call | tf_op jit(solution)/shard_map/pallas_call | solution.py:477
  69.5 6.9 %all-to-all-start.1 = ((bf16[32,112,128]{2,1,0:T(8,128)(2,1)}), bf16[32,112,128]{2,1,0:T(8,128)(2,1)S(1)}, u32[]{:S(2)}, u32[]{:S(2)}) async-start(bf16[32,112,128]{2,1,0:T(8,128)(2,1)} %get-tuple-element.26), calls=%async_computation.1 | async-start | bytes 1835008 | tf_op jit(solution)/shard_map/all_to_all | solution.py:320
  76.4 21.8 %all-to-all-done.1.back_ref = bf16[32,112,128]{2,1,0:T(8,128)(2,1)S(1)} async-done(((bf16[32,112,128]{2,1,0:T(8,128)(2,1)}), bf16[32,112,128]{2,1,0:T(8,128)(2,1)S(1)}, u32[]{:S(2)}, u32[]{:S(2)}) %all-to-all-start.1) | async-done | bytes 917536 | tf_op jit(solution)/shard_map/all_to_all | solution.py:320
  98.2 0.0 copy-start.12
  98.2 0.9 copy-done.12
  99.2 7.1 %shard_map.246 = (f32[2048,128]{1,0:T(8,128)}, f32[1,2048]{1,0:T(1,128)}) custom-call(bf16[32,112,128]{2,1,0:T(8,128)(2,1)} %copy-done.12, s32[1,2048]{1,0:T(1,128)} %bitcast.16, s32[1,2048]{1,0:T(1,128)} %get-tuple-element.27.rank_ref, bf16[128,2048]{1,0:T(8,128)(2,1)} %get-tuple-element.28.xdst_hbm, ...), custom_call_target="tpu_custom_call", output_to_operand_aliasing={{0}: (10, {})} | custom-call | tf_op jit(solution)/shard_map/pallas_call | solution.py:492
  106.2 0.0 copy-start.11
  106.3 1.2 constant_dynamic-slice_fusion
  107.4 5.1 %collective-permute-start.2 = (f32[1024,128]{1,0:T(8,128)S(1)}, f32[1024,128]{1,0:T(8,128)S(1)}, u32[]{:S(2)}, u32[]{:S(2)}) collective-permute-start(f32[1024,128]{1,0:T(8,128)S(1)} %constant_dynamic-slice_fusion), channel_id=1, source_target_pairs={{0,32},{32,0},{64,96},{96,64},{128,160},{160,128},{192,224},{224,1... | collective-permute-start | bytes 1572872 | tf_op jit(solution)/shard_map/ppermute | solution.py:341
  112.5 1.5 collective-permute-done.2
  114.0 0.0 copy-done.11
  114.0 0.1 dynamic-slice_add_fusion
  114.1 16.8 %all_to_all.34 = f32[16,64,128]{2,1,0:T(8,128)S(1)} all-to-all(f32[16,64,128]{2,1,0:T(8,128)S(1)} %bitcast.11), channel_id=1, replica_groups={{0,1,2,3,64,65,66,67,128,129,130,131,192,193,194,195},{4,5,6,7,68,69,70..., dimensions={0} | all-to-all | bytes 1048576 | tf_op jit(solution)/shard_map/all_to_all | solution.py:320
  130.9 11.9 %all_to_all.35 = f32[8,64,128]{2,1,0:T(8,128)S(1)} all-to-all(f32[8,64,128]{2,1,0:T(8,128)S(1)} %tile.4), channel_id=1, replica_groups={{0,4,8,12,16,20,24,28},{1,5,9,13,17,21,25,29},{2,6,10,14,18,22,26,30},{..., dimensions={0} | all-to-all | bytes 524288 | tf_op jit(solution)/shard_map/all_to_all | solution.py:320
  143.0 12.9 %all_to_all.36 = f32[16,64,128]{2,1,0:T(8,128)S(1)} all-to-all(f32[16,64,128]{2,1,0:T(8,128)S(1)} %tile.5), channel_id=1, replica_groups={{0,1,2,3,64,65,66,67,128,129,130,131,192,193,194,195},{4,5,6,7,68,69,70..., dimensions={0} | all-to-all | bytes 1048576 | tf_op jit(solution)/shard_map/all_to_all | solution.py:320
  155.8 4.1 %collective-permute-start.3 = (f32[1024,128]{1,0:T(8,128)S(1)}, f32[1024,128]{1,0:T(8,128)S(1)}, u32[]{:S(2)}, u32[]{:S(2)}) collective-permute-start(f32[1024,128]{1,0:T(8,128)S(1)} %bitcast.10), channel_id=1, source_target_pairs={{0,32},{32,0},{64,96},{96,64},{128,160},{160,128},{192,224},{224,1... | collective-permute-start | bytes 1572872 | tf_op jit(solution)/shard_map/ppermute | solution.py:347
  159.9 1.5 collective-permute-done.3
  161.5 0.1 broadcast_select_fusion
  161.5 0.7 fusion.1
  162.2 0.9 fusion
  (4 shorter events, 0.1 us)
Async XLA Ops:
  0.6 10.5 %collective-permute-start = (bf16[256,128]{1,0:T(8,128)(2,1)}, bf16[256,128]{1,0:T(8,128)(2,1)S(1)}, u32[]{:S(2)}, u32[]{:S(2)}) collective-permute-start(bf16[256,128]{1,0:T(8,128)(2,1)} %bitcast.12), channel_id=1, source_target_pairs={{0,1},{1,2},{2,3},{3,4},{4,5},{5,6},{6,7},{7,8},{8,9},{9,10},{10,1... | collective-permute-start | bytes 196616 | tf_op jit(solution)/shard_map/ppermute | solution.py:380
  2.8 8.4 %collective-permute-start.1 = (bf16[256,128]{1,0:T(8,128)(2,1)}, bf16[256,128]{1,0:T(8,128)(2,1)S(1)}, u32[]{:S(2)}, u32[]{:S(2)}) collective-permute-start(bf16[256,128]{1,0:T(8,128)(2,1)} %bitcast.13), channel_id=1, source_target_pairs={{0,31},{1,0},{2,1},{3,2},{4,3},{5,4},{6,5},{7,6},{8,7},{9,8},{10,9... | collective-permute-start | bytes 196616 | tf_op jit(solution)/shard_map/ppermute | solution.py:381
  11.2 0.6 copy-start.13
  11.2 0.6 copy-start.14
  11.8 16.1 %copy-start.6 = (bf16[736,27]{1,0:T(8,128)(2,1)S(1)}, bf16[736,27]{1,0:T(8,128)(2,1)}, u32[]{:S(2)}) copy-start(bf16[736,27]{1,0:T(8,128)(2,1)} %constant.33.clone.pick_b) | copy-start | bytes 119236
  19.6 8.3 %copy-start.2 = (bf16[729,729]{1,0:T(8,128)(2,1)S(1)}, bf16[729,729]{1,0:T(8,128)(2,1)}, u32[]{:S(2)}) copy-start(bf16[729,729]{1,0:T(8,128)(2,1)} %cg_ref.1) | copy-start | bytes 3188650
  19.6 8.3 %copy-start.3 = (bf16[729,128]{1,0:T(8,128)(2,1)S(1)}, bf16[729,128]{1,0:T(8,128)(2,1)}, u32[]{:S(2)}) copy-start(bf16[729,128]{1,0:T(8,128)(2,1)} %wleft_ref.1) | copy-start | bytes 559876
  19.6 8.3 %copy-start.4 = (bf16[729,128]{1,0:T(8,128)(2,1)S(1)}, bf16[729,128]{1,0:T(8,128)(2,1)}, u32[]{:S(2)}) copy-start(bf16[729,128]{1,0:T(8,128)(2,1)} %wright_ref.1) | copy-start | bytes 559876
  19.6 8.3 %copy-start.5 = (bf16[736,27]{1,0:T(8,128)(2,1)S(1)}, bf16[736,27]{1,0:T(8,128)(2,1)}, u32[]{:S(2)}) copy-start(bf16[736,27]{1,0:T(8,128)(2,1)} %constant.32.clone.pick_a) | copy-start | bytes 119236
  19.6 8.3 %copy-start.8 = (s32[3,27]{1,0:T(4,128)S(1)}, s32[3,27]{1,0:T(4,128)}, u32[]{:S(2)}) copy-start(s32[3,27]{1,0:T(4,128)} %mask_ref.1) | copy-start | bytes 976
  19.6 8.3 %copy-start.9 = (bf16[3,16]{1,0:T(4,128)(2,1)S(1)}, bf16[3,16]{1,0:T(4,128)(2,1)}, u32[]{:S(2)}) copy-start(bf16[3,16]{1,0:T(4,128)(2,1)} %constant.34.clone.pick_dst) | copy-start | bytes 292
  19.7 8.3 %copy-start.10 = (bf16[3,16]{1,0:T(4,128)(2,1)S(1)}, bf16[3,16]{1,0:T(4,128)(2,1)}, u32[]{:S(2)}) copy-start(bf16[3,16]{1,0:T(4,128)(2,1)} %constant.35.clone.pick_src) | copy-start | bytes 292
  19.7 30.4 %all-to-all-start = ((bf16[32,112,128]{2,1,0:T(8,128)(2,1)}), bf16[32,112,128]{2,1,0:T(8,128)(2,1)}, u32[]{:S(2)}, u32[]{:S(2)}) async-start(bf16[32,112,128]{2,1,0:T(8,128)(2,1)} %get-tuple-element.20), calls=%async_computation | async-start | bytes 1835008 | tf_op jit(solution)/shard_map/all_to_all | solution.py:320
  28.0 22.1 %copy-start.7 = (s32[2,768]{1,0:T(2,128)S(1)}, s32[2,768]{1,0:T(2,128)}, u32[]{:S(2)}) copy-start(s32[2,768]{1,0:T(2,128)} %constant.36.clone.place_ref) | copy-start | bytes 18436
  28.7 1.0 copy-start
  29.7 1.0 copy-start.1
  69.5 28.7 %all-to-all-start.1 = ((bf16[32,112,128]{2,1,0:T(8,128)(2,1)}), bf16[32,112,128]{2,1,0:T(8,128)(2,1)S(1)}, u32[]{:S(2)}, u32[]{:S(2)}) async-start(bf16[32,112,128]{2,1,0:T(8,128)(2,1)} %get-tuple-element.26), calls=%async_computation.1 | async-start | bytes 1835008 | tf_op jit(solution)/shard_map/all_to_all | solution.py:320
  98.2 0.9 copy-start.12
  106.2 7.8 %copy-start.11 = (f32[2048,128]{1,0:T(8,128)S(1)}, f32[2048,128]{1,0:T(8,128)}, u32[]{:S(2)}) copy-start(f32[2048,128]{1,0:T(8,128)} %get-tuple-element.31) | copy-start | bytes 3145732
  107.4 6.6 %collective-permute-start.2 = (f32[1024,128]{1,0:T(8,128)S(1)}, f32[1024,128]{1,0:T(8,128)S(1)}, u32[]{:S(2)}, u32[]{:S(2)}) collective-permute-start(f32[1024,128]{1,0:T(8,128)S(1)} %constant_dynamic-slice_fusion), channel_id=1, source_target_pairs={{0,32},{32,0},{64,96},{96,64},{128,160},{160,128},{192,224},{224,1... | collective-permute-start | bytes 1572872 | tf_op jit(solution)/shard_map/ppermute | solution.py:341
  155.8 5.6 %collective-permute-start.3 = (f32[1024,128]{1,0:T(8,128)S(1)}, f32[1024,128]{1,0:T(8,128)S(1)}, u32[]{:S(2)}, u32[]{:S(2)}) collective-permute-start(f32[1024,128]{1,0:T(8,128)S(1)} %bitcast.10), channel_id=1, source_target_pairs={{0,32},{32,0},{64,96},{96,64},{128,160},{160,128},{192,224},{224,1... | collective-permute-start | bytes 1572872 | tf_op jit(solution)/shard_map/ppermute | solution.py:347

commit v6 on v5

--- a/solution.py
+++ b/solution.py
@@ -11,7 +11,7 @@
 F32 = jnp.float32
 BF16 = jnp.bfloat16
 GROUP = 8
-EDGE_GROUP = 16
+EDGE_GROUP = 32
 TAIL = 16
 LANES = 128
 CHUNK = 256

time: 164 us -> 163 us (level)
  no operation moved by 1% of the time
where the time goes in v6:
time: 163 us
  waiting for transfers between devices  46.2 us (28%)
  blocking collectives  41.5 us (25%)
  Pallas kernels  34.4 us (21%)
  starting transfers between devices  32.9 us (20%)
  local copies, waits for them, and re-layouts  5.58 us (3%)
    all_to_all x3, blocking collectives, exchange(): lax.all_to_all(array, axis, split_axis=0, concat_axis=0, tiled=True, axis...  41.5 us
    all_to_all x2, waiting for transfers between devices, exchange(): lax.all_to_all(array, axis, split_axis=0, concat_axis=0, tiled=True, axis...  41.4 us
    pallas_call x1, Pallas kernels, local(): pl.pallas_call(holder_kernel, out_shape=(array((devices, block, channels)...  19.4 us
    all_to_all x2, starting transfers between devices, exchange(): lax.all_to_all(array, axis, split_axis=0, concat_axis=0, tiled=True, axis...  14.9 us
    pallas_call x1, Pallas kernels, local(): pl.pallas_call(edge_kernel, out_shape=(array((devices, block, channels)),...  7.47 us
    pallas_call x1, Pallas kernels, local(): pl.pallas_call(finish_kernel, out_shape=(array((total, channels), F32), a...  6.76 us
    ppermute x1, starting transfers between devices, local(): node_hi = lax.ppermute(nodes, 'edge', ring(devices, -1))  6.65 us
    ppermute x1, starting transfers between devices, sum_everywhere(): part = keep + lax.ppermute(give, 'rep', SWAP)  5.1 us
  transfers between devices with their start and end apart: 6, of which 5 were waited for; matrix products, arithmetic and copies ran while one was open for 0% of the time, Pallas kernels for 0%

profile of v6, /device:TPU:1, one launch (start us, length us, event | category | flops | bytes accessed | tf_op | source)
XLA Modules:
  0.0 162.6 jit_solution(14546638784588677379)
XLA Ops:
  0.6 2.1 %collective-permute-start = (bf16[256,128]{1,0:T(8,128)(2,1)}, bf16[256,128]{1,0:T(8,128)(2,1)S(1)}, u32[]{:S(2)}, u32[]{:S(2)}) collective-permute-start(bf16[256,128]{1,0:T(8,128)(2,1)} %bitcast.12), channel_id=1, source_target_pairs={{0,1},{1,2},{2,3},{3,4},{4,5},{5,6},{6,7},{7,8},{8,9},{9,10},{10,1... | collective-permute-start | bytes 196616 | tf_op jit(solution)/shard_map/ppermute | solution.py:380
  2.8 6.6 %collective-permute-start.1 = (bf16[256,128]{1,0:T(8,128)(2,1)}, bf16[256,128]{1,0:T(8,128)(2,1)S(1)}, u32[]{:S(2)}, u32[]{:S(2)}) collective-permute-start(bf16[256,128]{1,0:T(8,128)(2,1)} %bitcast.13), channel_id=1, source_target_pairs={{0,31},{1,0},{2,1},{3,2},{4,3},{5,4},{6,5},{7,6},{8,7},{9,8},{10,9... | collective-permute-start | bytes 196616 | tf_op jit(solution)/shard_map/ppermute | solution.py:381
  9.4 1.8 %collective-permute-done.node_lo = bf16[256,128]{1,0:T(8,128)(2,1)S(1)} collective-permute-done((bf16[256,128]{1,0:T(8,128)(2,1)}, bf16[256,128]{1,0:T(8,128)(2,1)S(1)}, u32[]{:S(2)}, u32[]{:S(2)}) %collective-permute-start) | collective-permute-done | bytes 65568 | tf_op jit(solution)/shard_map/ppermute | solution.py:380
  11.2 0.0 copy-start.13
  11.2 0.0 collective-permute-done.1.node_hi
  11.2 0.0 copy-start.14
  11.2 0.6 copy-done.13
  11.8 0.0 copy-done.14
  11.8 0.0 copy-start.6
  11.8 7.5 %shard_map.243 = (bf16[32,112,128]{2,1,0:T(8,128)(2,1)}, s32[1,2048]{1,0:T(1,128)}, bf16[128,2048]{1,0:T(8,128)(2,1)}, bf16[128,2048]{1,0:T(8,128)(2,1)}) custom-call(s32[1]{0:T(128)} %bitcast.pos_ref, s32[1,2048]{1,0:T(1,128)} %dst_ref.1, s32[1,2048]{1,0:T(1,128)} %src_ref.1, s32[1,2048]{1,0:T(1,128)} %bitcast.15, s32[1,8192]{1,0:T(1,128)} %spec_hi.1, ...), custom_call_target="tpu_custom_call" | custom-call | tf_op jit(solution)/shard_map/pallas_call | solution.py:407
  19.3 0.0 copy-start.2
  19.3 0.0 copy-start.3
  19.3 0.0 copy-start.4
  19.3 0.0 copy-start.5
  19.3 0.0 copy-start.8
  19.4 0.0 copy-start.9
  19.4 0.0 copy-start.10
  19.4 8.4 %all-to-all-start = ((bf16[32,112,128]{2,1,0:T(8,128)(2,1)}), bf16[32,112,128]{2,1,0:T(8,128)(2,1)}, u32[]{:S(2)}, u32[]{:S(2)}) async-start(bf16[32,112,128]{2,1,0:T(8,128)(2,1)} %get-tuple-element.20), calls=%async_computation | async-start | bytes 1835008 | tf_op jit(solution)/shard_map/all_to_all | solution.py:320
  27.8 0.0 copy-done.6
  27.8 0.0 copy-done.2
  27.8 0.0 copy-done.3
  27.8 0.0 copy-done.4
  27.8 0.0 copy-done.5
  27.8 0.0 copy-done.8
  27.8 0.0 copy-done.9
  27.9 0.0 copy-done.10
  27.9 0.0 copy-start.7
  27.9 0.7 shard_map.244
  28.6 0.0 copy-start
  28.6 1.0 copy-done
  29.6 0.0 copy-start.1
  29.6 1.0 copy-done.1
  30.6 19.4 %all-to-all-done.recv_ref = bf16[32,112,128]{2,1,0:T(8,128)(2,1)} async-done(((bf16[32,112,128]{2,1,0:T(8,128)(2,1)}), bf16[32,112,128]{2,1,0:T(8,128)(2,1)}, u32[]{:S(2)}, u32[]{:S(2)}) %all-to-all-start) | async-done | bytes 917536 | tf_op jit(solution)/shard_map/all_to_all | solution.py:320
  50.0 0.0 copy-done.7
  50.0 19.4 %shard_map.245 = (bf16[32,112,128]{2,1,0:T(8,128)(2,1)}, f32[2048,128]{1,0:T(8,128)}) custom-call(bf16[32,112,128]{2,1,0:T(8,128)(2,1)} %all-to-all-done.recv_ref, bf16[1,729,3072]{2,1,0:T(8,128)(2,1)} %target_ref.1, bf16[1472,128]{1,0:T(8,128)(2,1)S(1)} %get-tuple-element.21.wlr_ref, bf16[128,1472]{1,0:T(8,128)(2,1)S(1)} %get-tuple-element.22.wlr_t, ...), custom_call_target="tpu_custom_call" | custom-call | tf_op jit(solution)/shard_map/pallas_call | solution.py:477
  69.4 6.5 %all-to-all-start.1 = ((bf16[32,112,128]{2,1,0:T(8,128)(2,1)}), bf16[32,112,128]{2,1,0:T(8,128)(2,1)S(1)}, u32[]{:S(2)}, u32[]{:S(2)}) async-start(bf16[32,112,128]{2,1,0:T(8,128)(2,1)} %get-tuple-element.26), calls=%async_computation.1 | async-start | bytes 1835008 | tf_op jit(solution)/shard_map/all_to_all | solution.py:320
  76.0 22.0 %all-to-all-done.1.back_ref = bf16[32,112,128]{2,1,0:T(8,128)(2,1)S(1)} async-done(((bf16[32,112,128]{2,1,0:T(8,128)(2,1)}), bf16[32,112,128]{2,1,0:T(8,128)(2,1)S(1)}, u32[]{:S(2)}, u32[]{:S(2)}) %all-to-all-start.1) | async-done | bytes 917536 | tf_op jit(solution)/shard_map/all_to_all | solution.py:320
  98.0 0.0 copy-start.12
  98.0 0.9 copy-done.12
  98.9 6.8 %shard_map.246 = (f32[2048,128]{1,0:T(8,128)}, f32[1,2048]{1,0:T(1,128)}) custom-call(bf16[32,112,128]{2,1,0:T(8,128)(2,1)} %copy-done.12, s32[1,2048]{1,0:T(1,128)} %bitcast.16, s32[1,2048]{1,0:T(1,128)} %get-tuple-element.27.rank_ref, bf16[128,2048]{1,0:T(8,128)(2,1)} %get-tuple-element.28.xdst_hbm, ...), custom_call_target="tpu_custom_call", output_to_operand_aliasing={{0}: (10, {})} | custom-call | tf_op jit(solution)/shard_map/pallas_call | solution.py:492
  105.7 0.0 copy-start.11
  105.7 1.2 constant_dynamic-slice_fusion
  106.8 5.1 %collective-permute-start.2 = (f32[1024,128]{1,0:T(8,128)S(1)}, f32[1024,128]{1,0:T(8,128)S(1)}, u32[]{:S(2)}, u32[]{:S(2)}) collective-permute-start(f32[1024,128]{1,0:T(8,128)S(1)} %constant_dynamic-slice_fusion), channel_id=1, source_target_pairs={{0,32},{32,0},{64,96},{96,64},{128,160},{160,128},{192,224},{224,1... | collective-permute-start | bytes 1572872 | tf_op jit(solution)/shard_map/ppermute | solution.py:341
  111.9 1.5 collective-permute-done.2
  113.5 0.0 copy-done.11
  113.5 0.1 dynamic-slice_add_fusion
  113.5 16.7 %all_to_all.34 = f32[16,64,128]{2,1,0:T(8,128)S(1)} all-to-all(f32[16,64,128]{2,1,0:T(8,128)S(1)} %bitcast.11), channel_id=1, replica_groups={{0,1,2,3,64,65,66,67,128,129,130,131,192,193,194,195},{4,5,6,7,68,69,70..., dimensions={0} | all-to-all | bytes 1048576 | tf_op jit(solution)/shard_map/all_to_all | solution.py:320
  130.3 11.9 %all_to_all.35 = f32[8,64,128]{2,1,0:T(8,128)S(1)} all-to-all(f32[8,64,128]{2,1,0:T(8,128)S(1)} %tile.4), channel_id=1, replica_groups={{0,4,8,12,16,20,24,28},{1,5,9,13,17,21,25,29},{2,6,10,14,18,22,26,30},{..., dimensions={0} | all-to-all | bytes 524288 | tf_op jit(solution)/shard_map/all_to_all | solution.py:320
  142.4 12.9 %all_to_all.36 = f32[16,64,128]{2,1,0:T(8,128)S(1)} all-to-all(f32[16,64,128]{2,1,0:T(8,128)S(1)} %tile.5), channel_id=1, replica_groups={{0,1,2,3,64,65,66,67,128,129,130,131,192,193,194,195},{4,5,6,7,68,69,70..., dimensions={0} | all-to-all | bytes 1048576 | tf_op jit(solution)/shard_map/all_to_all | solution.py:320
  155.2 4.1 %collective-permute-start.3 = (f32[1024,128]{1,0:T(8,128)S(1)}, f32[1024,128]{1,0:T(8,128)S(1)}, u32[]{:S(2)}, u32[]{:S(2)}) collective-permute-start(f32[1024,128]{1,0:T(8,128)S(1)} %bitcast.10), channel_id=1, source_target_pairs={{0,32},{32,0},{64,96},{96,64},{128,160},{160,128},{192,224},{224,1... | collective-permute-start | bytes 1572872 | tf_op jit(solution)/shard_map/ppermute | solution.py:347
  159.3 1.5 collective-permute-done.3
  160.9 0.1 broadcast_select_fusion
  160.9 0.7 fusion.1
  161.6 0.9 fusion
  (4 shorter events, 0.1 us)
Async XLA Ops:
  0.6 10.5 %collective-permute-start = (bf16[256,128]{1,0:T(8,128)(2,1)}, bf16[256,128]{1,0:T(8,128)(2,1)S(1)}, u32[]{:S(2)}, u32[]{:S(2)}) collective-permute-start(bf16[256,128]{1,0:T(8,128)(2,1)} %bitcast.12), channel_id=1, source_target_pairs={{0,1},{1,2},{2,3},{3,4},{4,5},{5,6},{6,7},{7,8},{8,9},{9,10},{10,1... | collective-permute-start | bytes 196616 | tf_op jit(solution)/shard_map/ppermute | solution.py:380
  2.8 8.4 %collective-permute-start.1 = (bf16[256,128]{1,0:T(8,128)(2,1)}, bf16[256,128]{1,0:T(8,128)(2,1)S(1)}, u32[]{:S(2)}, u32[]{:S(2)}) collective-permute-start(bf16[256,128]{1,0:T(8,128)(2,1)} %bitcast.13), channel_id=1, source_target_pairs={{0,31},{1,0},{2,1},{3,2},{4,3},{5,4},{6,5},{7,6},{8,7},{9,8},{10,9... | collective-permute-start | bytes 196616 | tf_op jit(solution)/shard_map/ppermute | solution.py:381
  11.2 0.6 copy-start.13
  11.2 0.6 copy-start.14
  11.8 16.0 %copy-start.6 = (bf16[736,27]{1,0:T(8,128)(2,1)S(1)}, bf16[736,27]{1,0:T(8,128)(2,1)}, u32[]{:S(2)}) copy-start(bf16[736,27]{1,0:T(8,128)(2,1)} %constant.33.clone.pick_b) | copy-start | bytes 119236
  19.3 8.5 %copy-start.2 = (bf16[729,729]{1,0:T(8,128)(2,1)S(1)}, bf16[729,729]{1,0:T(8,128)(2,1)}, u32[]{:S(2)}) copy-start(bf16[729,729]{1,0:T(8,128)(2,1)} %cg_ref.1) | copy-start | bytes 3188650
  19.3 8.5 %copy-start.3 = (bf16[729,128]{1,0:T(8,128)(2,1)S(1)}, bf16[729,128]{1,0:T(8,128)(2,1)}, u32[]{:S(2)}) copy-start(bf16[729,128]{1,0:T(8,128)(2,1)} %wleft_ref.1) | copy-start | bytes 559876
  19.3 8.5 %copy-start.4 = (bf16[729,128]{1,0:T(8,128)(2,1)S(1)}, bf16[729,128]{1,0:T(8,128)(2,1)}, u32[]{:S(2)}) copy-start(bf16[729,128]{1,0:T(8,128)(2,1)} %wright_ref.1) | copy-start | bytes 559876
  19.3 8.5 %copy-start.5 = (bf16[736,27]{1,0:T(8,128)(2,1)S(1)}, bf16[736,27]{1,0:T(8,128)(2,1)}, u32[]{:S(2)}) copy-start(bf16[736,27]{1,0:T(8,128)(2,1)} %constant.32.clone.pick_a) | copy-start | bytes 119236
  19.3 8.5 %copy-start.8 = (s32[3,27]{1,0:T(4,128)S(1)}, s32[3,27]{1,0:T(4,128)}, u32[]{:S(2)}) copy-start(s32[3,27]{1,0:T(4,128)} %mask_ref.1) | copy-start | bytes 976
  19.4 8.5 %copy-start.9 = (bf16[3,16]{1,0:T(4,128)(2,1)S(1)}, bf16[3,16]{1,0:T(4,128)(2,1)}, u32[]{:S(2)}) copy-start(bf16[3,16]{1,0:T(4,128)(2,1)} %constant.34.clone.pick_dst) | copy-start | bytes 292
  19.4 8.5 %copy-start.10 = (bf16[3,16]{1,0:T(4,128)(2,1)S(1)}, bf16[3,16]{1,0:T(4,128)(2,1)}, u32[]{:S(2)}) copy-start(bf16[3,16]{1,0:T(4,128)(2,1)} %constant.35.clone.pick_src) | copy-start | bytes 292
  19.4 30.6 %all-to-all-start = ((bf16[32,112,128]{2,1,0:T(8,128)(2,1)}), bf16[32,112,128]{2,1,0:T(8,128)(2,1)}, u32[]{:S(2)}, u32[]{:S(2)}) async-start(bf16[32,112,128]{2,1,0:T(8,128)(2,1)} %get-tuple-element.20), calls=%async_computation | async-start | bytes 1835008 | tf_op jit(solution)/shard_map/all_to_all | solution.py:320
  27.9 22.1 %copy-start.7 = (s32[2,768]{1,0:T(2,128)S(1)}, s32[2,768]{1,0:T(2,128)}, u32[]{:S(2)}) copy-start(s32[2,768]{1,0:T(2,128)} %constant.36.clone.place_ref) | copy-start | bytes 18436
  28.6 1.0 copy-start
  29.6 1.0 copy-start.1
  69.4 28.5 %all-to-all-start.1 = ((bf16[32,112,128]{2,1,0:T(8,128)(2,1)}), bf16[32,112,128]{2,1,0:T(8,128)(2,1)S(1)}, u32[]{:S(2)}, u32[]{:S(2)}) async-start(bf16[32,112,128]{2,1,0:T(8,128)(2,1)} %get-tuple-element.26), calls=%async_computation.1 | async-start | bytes 1835008 | tf_op jit(solution)/shard_map/all_to_all | solution.py:320
  98.0 0.9 copy-start.12
  105.7 7.8 %copy-start.11 = (f32[2048,128]{1,0:T(8,128)S(1)}, f32[2048,128]{1,0:T(8,128)}, u32[]{:S(2)}) copy-start(f32[2048,128]{1,0:T(8,128)} %get-tuple-element.31) | copy-start | bytes 3145732
  106.8 6.6 %collective-permute-start.2 = (f32[1024,128]{1,0:T(8,128)S(1)}, f32[1024,128]{1,0:T(8,128)S(1)}, u32[]{:S(2)}, u32[]{:S(2)}) collective-permute-start(f32[1024,128]{1,0:T(8,128)S(1)} %constant_dynamic-slice_fusion), channel_id=1, source_target_pairs={{0,32},{32,0},{64,96},{96,64},{128,160},{160,128},{192,224},{224,1... | collective-permute-start | bytes 1572872 | tf_op jit(solution)/shard_map/ppermute | solution.py:341
  155.2 5.6 %collective-permute-start.3 = (f32[1024,128]{1,0:T(8,128)S(1)}, f32[1024,128]{1,0:T(8,128)S(1)}, u32[]{:S(2)}, u32[]{:S(2)}) collective-permute-start(f32[1024,128]{1,0:T(8,128)S(1)} %bitcast.10), channel_id=1, source_target_pairs={{0,32},{32,0},{64,96},{96,64},{128,160},{160,128},{192,224},{224,1... | collective-permute-start | bytes 1572872 | tf_op jit(solution)/shard_map/ppermute | solution.py:347
